TPU v7x, 32 devices: a whole 2x2x4 slice. The times are simulated.
32 devices in a mesh: batch: 2 (over x), blk: 16 (over z, y, core).
Axes of the slice: x: 2, y: 2, z: 4, core: 2. Of those that a mesh axis runs over, the one named last changes fastest.
Arguments:
- triplane: bfloat16 [4, 768, 1024], P('batch', 'blk'), may hold values from -6 to 6
- patches: bfloat16 [4, 256, 1024], P('batch', 'blk'), may hold values from -6 to 6
- cotangent: bfloat16 [4, 768, 1024], P('batch', 'blk'), may hold values from -6 to 6
- camera_index: int32 [4, 4], P('batch'), may hold values from 0 to 255
- triplane_count: int32 [4], P('batch'), may hold values from 744 to 768, as said below
- patch_count: int32 [4], P('batch'), may hold values from 128 to 256, as said below
- camera_table: bfloat16 [256, 1024], replicated, may hold values from -6 to 6
- mod_weight: bfloat16 [1024, 2048], replicated, may hold values from -0.1875 to 0.1875
- qkv_weight: bfloat16 [1024, 3072], replicated, may hold values from -0.1875 to 0.1875
- self_out: bfloat16 [1024, 1024], replicated, may hold values from -3 to 3
- gain_mid: float32 [1024], replicated, may hold values from 0.25 to 1.75
- bias_mid: float32 [1024], replicated, may hold values from -3 to 3
- cross_query: bfloat16 [1024, 1024], replicated, may hold values from -0.1875 to 0.1875
- cross_memory: bfloat16 [1024, 2048], replicated, may hold values from -0.1875 to 0.1875
- cross_out: bfloat16 [1024, 1024], replicated, may hold values from -3 to 3
- gain_last: float32 [1024], replicated, may hold values from 0.25 to 1.75
- bias_last: float32 [1024], replicated, may hold values from -3 to 3
- up_weight: bfloat16 [1024, 4096], replicated, may hold values from -0.1875 to 0.1875
- down_weight: bfloat16 [4096, 1024], replicated, may hold values from -0.09375 to 0.09375
Outputs:
- layer_out: float32 [4, 768, 1024], P('batch', 'blk')
- grad_triplane: float32 [4, 768, 1024], P('batch', 'blk')
- grad_patches: float32 [4, 256, 1024], P('batch', 'blk')
- grad_camera_table: float32 [256, 1024], P(('batch', 'blk'))
- grad_mod_weight: float32 [1024, 2048], P(('batch', 'blk'))
- grad_qkv_weight: float32 [1024, 3072], P(('batch', 'blk'))
- grad_self_out: float32 [1024, 1024], P(('batch', 'blk'))
- grad_gain_mid: float32 [1024], P(('batch', 'blk'))
- grad_bias_mid: float32 [1024], P(('batch', 'blk'))
- grad_cross_query: float32 [1024, 1024], P(('batch', 'blk'))
- grad_cross_memory: float32 [1024, 2048], P(('batch', 'blk'))
- grad_cross_out: float32 [1024, 1024], P(('batch', 'blk'))
- grad_gain_last: float32 [1024], P(('batch', 'blk'))
- grad_bias_last: float32 [1024], P(('batch', 'blk'))
- grad_up_weight: float32 [1024, 4096], P(('batch', 'blk'))
- grad_down_weight: float32 [4096, 1024], P(('batch', 'blk'))
Inputs may be any that keep to these rules, and one draw needn't show every extreme that they name: Only the first triplane_count triplane tokens of an item are keys of its self-attention; in every draw one item of each 2 in a row has all 768, the others lose at most 48. Only the first patch_count patch tokens of an item are keys of its cross-attention; in every draw one item of each 2 in a row has all 256, the others lose at most 128.
All inputs are finite; a program needn't handle non-finite values.
Results may differ from a plain program's by a relative error of at most 0.035.
Values may be sent and summed in bfloat16 or wider, within the bound.
No kernel may reach another device: no remote copies, remote signals or barrier semaphores. Data moves between devices by JAX's collectives and lax.ppermute only.
A program may use at most 384 MiB of HBM per device.

v0:
```python
import functools

import jax
import jax.numpy as jnp
from jax import lax
from jax.experimental import pallas as pl
from jax.experimental.pallas import tpu as pltpu
from jax.sharding import PartitionSpec as P

HEADS = 16
HEAD_DIM = 64
LANES = 128
PAIRS = HEADS * HEAD_DIM // LANES
BF = jnp.bfloat16
F32 = jnp.float32
BOTH = ("batch", "blk")
TINY = -1e30
GROUP = 4
WIDE = GROUP * HEAD_DIM
ANYWHERE = pl.BlockSpec(memory_space=pl.ANY)
ROOM = 60 << 20
IN_SMEM = pl.BlockSpec(memory_space=pltpu.SMEM)


def whole(shape):
    return pl.BlockSpec(shape, lambda *at: (0,) * len(shape))


def mm(a, b):
    return jnp.dot(a, b, preferred_element_type=F32)


def mm_nt(a, b):
    return lax.dot_general(a, b, (((1,), (1,)), ((), ())), preferred_element_type=F32)


def mm_tn(a, b):
    return lax.dot_general(a, b, (((0,), (0,)), ((), ())), preferred_element_type=F32)


def center_scale(values):
    center = values - jnp.mean(values, axis=-1, keepdims=True)
    rstd = lax.rsqrt(jnp.mean(center * center, axis=-1, keepdims=True) + 1e-05)
    return center * rstd, rstd


def norm_back(unit, rstd, grad):
    return rstd * (
        grad
        - jnp.mean(grad, axis=-1, keepdims=True)
        - unit * jnp.mean(grad * unit, axis=-1, keepdims=True)
    )


def self_forward_kernel(count_ref, q_ref, k_ref, v_ref, out_ref, lse_ref):
    queries = q_ref[...].reshape(-1, LANES) * BF(HEAD_DIM**-0.5)
    keys = k_ref[...].reshape(-1, LANES)
    values_t = v_ref[...].reshape(-1, LANES).T
    lane = lax.broadcasted_iota(jnp.int32, queries.shape, 1) // HEAD_DIM
    row = lax.broadcasted_iota(jnp.int32, (keys.shape[0], queries.shape[0]), 0)
    parts = []
    for item in range(2):
        mine = jnp.where(lane == item, queries, BF(0))
        scores = jnp.where(row < count_ref[item], mm_nt(keys, mine), TINY)
        top = jnp.max(scores, axis=0, keepdims=True)
        weights = jnp.exp(scores - top)
        total = jnp.sum(weights, axis=0, keepdims=True)
        span = slice(item * HEAD_DIM, (item + 1) * HEAD_DIM)
        parts.append(mm(values_t[span], weights.astype(BF)) / total)
        lse_ref[item : item + 1, :] = top + jnp.log(total)
    out = jnp.concatenate(parts, axis=0).T
    out_ref[...] = out.astype(BF).reshape(out_ref.shape)


def self_backward_kernel(
    steps, count_ref, q_ref, k_ref, v_ref, do_ref, lse_ref, *rest
):
    dq_ref, dkv_ref, dk_acc, dv_acc = rest[-4:]
    step = pl.program_id(0)
    queries = q_ref[...].reshape(-1, LANES) * BF(HEAD_DIM**-0.5)
    keys = k_ref[...].reshape(-1, LANES)
    values = v_ref[...].reshape(-1, LANES)
    keys_t = keys.T
    grads = do_ref[...].reshape(-1, LANES)
    lane = lax.broadcasted_iota(jnp.int32, queries.shape, 1) // HEAD_DIM
    row = lax.broadcasted_iota(jnp.int32, (keys.shape[0], queries.shape[0]), 0)
    parts = []
    d_keys = None
    for item in range(2):
        mine = jnp.where(lane == item, queries, BF(0))
        d_mine = jnp.where(lane == item, grads, BF(0))
        scores = mm_nt(keys, mine)
        probs = jnp.where(
            row < count_ref[item], jnp.exp(scores - lse_ref[item : item + 1, :]), 0.0
        )
        d_probs = mm_nt(values, d_mine)
        delta = jnp.sum(probs * d_probs, axis=0, keepdims=True)
        d_scores = (probs * (d_probs - delta)).astype(BF)
        new_v = mm(probs.astype(BF), d_mine)
        new_k = mm(d_scores, mine)
        d_values = new_v if d_keys is None else d_values + new_v
        d_keys = new_k if d_keys is None else d_keys + new_k
        span = slice(item * HEAD_DIM, (item + 1) * HEAD_DIM)
        parts.append(mm(keys_t[span], d_scores) * HEAD_DIM**-0.5)
    d_q = jnp.concatenate(parts, axis=0).T
    dq_ref[...] = d_q.astype(BF).reshape(dq_ref.shape)

    @pl.when(step == 0)
    def _():
        dk_acc[...] = d_keys
        dv_acc[...] = d_values

    @pl.when(step > 0)
    def _():
        dk_acc[...] += d_keys
        dv_acc[...] += d_values

    @pl.when(step == steps - 1)
    def _():
        shape = (dkv_ref.shape[0], 1) + dkv_ref.shape[2:]
        dkv_ref[:, 0:1] = dk_acc[...].astype(dkv_ref.dtype).reshape(shape)
        dkv_ref[:, 1:2] = dv_acc[...].astype(dkv_ref.dtype).reshape(shape)


def q_steps(blocks):
    return 2 if blocks % 2 == 0 else 1


def self_specs(q_arr, kv_arr, first):
    blocks, _, rows, _ = q_arr.shape
    steps = q_steps(blocks)
    part = blocks // steps
    many = kv_arr.shape[0]
    return steps, part, rows, many, [
        pl.BlockSpec(memory_space=pltpu.SMEM),
        pl.BlockSpec((part, 1, rows, LANES), lambda i: (i, 0, 0, 0)),
        pl.BlockSpec((many, 1, rows, LANES), lambda i: (0, first, 0, 0)),
        pl.BlockSpec((many, 1, rows, LANES), lambda i: (0, first + 1, 0, 0)),
    ]


def self_forward(counts, q_arr, kv_arr, first):
    steps, part, rows, many, specs = self_specs(q_arr, kv_arr, first)
    blocks = q_arr.shape[0]
    pairs = blocks * rows * many * rows * 2
    return pl.pallas_call(
        self_forward_kernel,
        grid=(steps,),
        in_specs=specs,
        out_specs=[
            pl.BlockSpec((part, rows, LANES), lambda i: (i, 0, 0)),
            pl.BlockSpec((2, part * rows), lambda i: (0, i)),
        ],
        out_shape=[
            jax.ShapeDtypeStruct((blocks, rows, LANES), BF),
            jax.ShapeDtypeStruct((2, blocks * rows), F32),
        ],
        compiler_params=pltpu.CompilerParams(vmem_limit_bytes=ROOM),
        cost_estimate=pl.CostEstimate(
            flops=pairs * 4 * LANES, bytes_accessed=1 << 20, transcendentals=pairs
        ),
        name="self_forward",
    )(counts, q_arr, kv_arr, kv_arr)


def self_backward(counts, q_arr, kv_arr, first, d_out, lse, low):
    steps, part, rows, many, specs = self_specs(q_arr, kv_arr, first)
    blocks = q_arr.shape[0]
    pairs = blocks * rows * many * rows * 2
    return pl.pallas_call(
        functools.partial(self_backward_kernel, steps),
        grid=(steps,),
        in_specs=specs
        + [
            pl.BlockSpec((part, 1, rows, LANES), lambda i: (i, 0, 0, 0)),
            pl.BlockSpec((2, part * rows), lambda i: (0, i)),
        ],
        out_specs=[
            pl.BlockSpec((part, 1, rows, LANES), lambda i: (i, 0, 0, 0)),
            pl.BlockSpec((many, 2, rows, LANES), lambda i: (0, 0, 0, 0)),
        ],
        out_shape=[
            jax.ShapeDtypeStruct((blocks, 1, rows, LANES), BF),
            jax.ShapeDtypeStruct((many, 2, rows, LANES), BF if low else F32),
        ],
        scratch_shapes=[
            pltpu.VMEM((many * rows, LANES), F32),
            pltpu.VMEM((many * rows, LANES), F32),
        ],
        compiler_params=pltpu.CompilerParams(vmem_limit_bytes=ROOM),
        cost_estimate=pl.CostEstimate(
            flops=pairs * 10 * LANES, bytes_accessed=2 << 20, transcendentals=pairs
        ),
        name="self_backward",
    )(counts, q_arr, kv_arr, kv_arr, d_out, lse)


def stack_heads(block, lane):
    zero = jnp.zeros((), block.dtype)
    return jnp.concatenate(
        [jnp.where(lane == head, block, zero) for head in range(GROUP)], axis=0
    )


def merge_heads(block, lane):
    rows = block.shape[0] // GROUP
    out = block[:rows]
    for head in range(1, GROUP):
        out = jnp.where(lane == head, block[head * rows : (head + 1) * rows], out)
    return out


def cross_forward_kernel(
    count_ref,
    q_ref,
    mem_ref,
    mid_ref,
    gain,
    bias,
    out_hbm,
    out_ref,
    lse_ref,
    later_ref,
    normed_ref,
    out_w,
    sem,
):
    fetch = pltpu.make_async_copy(out_hbm, out_w, sem)
    fetch.start()
    items, rows, width = q_ref.shape
    many = mem_ref.shape[1]
    lane = lax.broadcasted_iota(jnp.int32, (rows, WIDE), 1) // HEAD_DIM
    row = lax.broadcasted_iota(jnp.int32, (many, GROUP * rows), 0)

    def body(group, carry):
        span = pl.ds(pl.multiple_of(group * WIDE, WIDE), WIDE)
        over = pl.ds(pl.multiple_of(width + group * WIDE, WIDE), WIDE)
        for item in range(items):
            queries = stack_heads(q_ref[item, :, span] * BF(HEAD_DIM**-0.5), lane)
            scores = mm_nt(mem_ref[item, :, span], queries)
            scores = jnp.where(row < count_ref[item], scores, TINY)
            top = jnp.max(scores, axis=0, keepdims=True)
            weights = jnp.exp(scores - top)
            total = jnp.sum(weights, axis=0, keepdims=True)
            out = mm(mem_ref[item, :, over].T, weights.astype(BF)) / total
            out_ref[item, :, span] = merge_heads(out.T, lane).astype(BF)
            lse_ref[item, pl.ds(group, 1), : GROUP * rows] = top + jnp.log(total)
        return carry

    lax.fori_loop(0, width // WIDE, body, 0, unroll=2)
    fetch.wait()
    later = mid_ref[...] + mm(out_ref[...].reshape(items * rows, width), out_w[...])
    later_ref[...] = later
    unit, unused = center_scale(later)
    normed_ref[...] = (unit * gain[...] + bias[...]).astype(BF)


def cross_backward_kernel(count_ref, q_ref, mem_ref, do_ref, lse_ref, dq_ref):
    items, rows, width = q_ref.shape
    many = mem_ref.shape[1]
    lane = lax.broadcasted_iota(jnp.int32, (rows, WIDE), 1) // HEAD_DIM
    row = lax.broadcasted_iota(jnp.int32, (many, GROUP * rows), 0)

    def body(group, carry):
        span = pl.ds(pl.multiple_of(group * WIDE, WIDE), WIDE)
        over = pl.ds(pl.multiple_of(width + group * WIDE, WIDE), WIDE)
        for item in range(items):
            queries = stack_heads(q_ref[item, :, span] * BF(HEAD_DIM**-0.5), lane)
            grads = stack_heads(do_ref[item, :, span], lane)
            keys = mem_ref[item, :, span]
            scores = mm_nt(keys, queries)
            lse = lse_ref[item, pl.ds(group, 1), : GROUP * rows]
            probs = jnp.where(row < count_ref[item], jnp.exp(scores - lse), 0.0)
            d_probs = mm_nt(mem_ref[item, :, over], grads)
            delta = jnp.sum(probs * d_probs, axis=0, keepdims=True)
            d_scores = (probs * (d_probs - delta)).astype(BF)
            d_q = mm(keys.T, d_scores) * HEAD_DIM**-0.5
            dq_ref[item, :, span] = merge_heads(d_q.T, lane).astype(BF)
        return carry

    lax.fori_loop(0, width // WIDE, body, 0, unroll=2)


def cross_forward(counts, cross_q, memory, middle, cross_out, gain, bias):
    items, rows, width = cross_q.shape
    many = memory.shape[1]
    pairs = items * rows * HEADS * many
    return pl.pallas_call(
        cross_forward_kernel,
        grid=(1,),
        in_specs=[IN_SMEM]
        + [whole(x.shape) for x in (cross_q, memory, middle)]
        + [whole((1, width))] * 2
        + [ANYWHERE],
        out_specs=[
            whole((items, rows, width)),
            whole((items, width // WIDE, WIDE)),
            whole((items * rows, width)),
            whole((items * rows, width)),
        ],
        out_shape=[
            jax.ShapeDtypeStruct((items, rows, width), BF),
            jax.ShapeDtypeStruct((items, width // WIDE, WIDE), F32),
            jax.ShapeDtypeStruct((items * rows, width), F32),
            jax.ShapeDtypeStruct((items * rows, width), BF),
        ],
        scratch_shapes=[pltpu.VMEM(cross_out.shape, BF), pltpu.SemaphoreType.DMA],
        compiler_params=pltpu.CompilerParams(vmem_limit_bytes=ROOM),
        cost_estimate=pl.CostEstimate(
            flops=pairs * 4 * WIDE, bytes_accessed=3 << 20, transcendentals=pairs
        ),
        name="cross_forward",
    )(counts, cross_q, memory, middle, gain[None], bias[None], cross_out)


def cross_backward(counts, cross_q, memory, d_out, lse):
    items, rows, width = cross_q.shape
    many = memory.shape[1]
    pairs = items * rows * HEADS * many
    return pl.pallas_call(
        cross_backward_kernel,
        grid=(1,),
        in_specs=[IN_SMEM] + [whole(x.shape) for x in (cross_q, memory, d_out, lse)],
        out_specs=whole((items, rows, width)),
        out_shape=jax.ShapeDtypeStruct((items, rows, width), BF),
        compiler_params=pltpu.CompilerParams(vmem_limit_bytes=ROOM),
        cost_estimate=pl.CostEstimate(
            flops=pairs * 10 * WIDE, bytes_accessed=6 << 20, transcendentals=pairs
        ),
        name="cross_backward",
    )(counts, cross_q, memory, d_out, lse)


def memory_back_kernel(head_ref, count_ref, q_ref, do_ref, k_ref, v_ref, out_ref):
    items, many, _ = k_ref.shape
    odd = lax.rem(head_ref[0], 2)
    queries = q_ref[...].reshape(-1, LANES) * BF(HEAD_DIM**-0.5)
    grads = do_ref[...].reshape(-1, LANES)
    lane = lax.broadcasted_iota(jnp.int32, (many, LANES), 1) // HEAD_DIM
    row = lax.broadcasted_iota(jnp.int32, (many, queries.shape[0]), 0)

    def turn(ref, item):
        block = ref[item].astype(F32)
        block = jnp.where(odd == item, block, swap_half(block))
        return jnp.where(lane == item, block, 0.0).astype(BF)

    d_keys = None
    for item in range(items):
        scores = mm_nt(turn(k_ref, item), queries)
        scores = jnp.where(row < count_ref[item], scores, TINY)
        weights = jnp.exp(scores - jnp.max(scores, axis=0, keepdims=True))
        probs = weights * (1.0 / jnp.sum(weights, axis=0, keepdims=True))
        d_probs = mm_nt(turn(v_ref, item), grads)
        delta = jnp.sum(probs * d_probs, axis=0, keepdims=True)
        d_scores = (probs * (d_probs - delta)).astype(BF)
        new_k = mm(d_scores, queries)
        new_v = mm(probs.astype(BF), grads)
        d_values = new_v if d_keys is None else jnp.where(lane == item, new_v, d_values)
        d_keys = new_k if d_keys is None else jnp.where(lane == item, new_k, d_keys)
    shape = (out_ref.shape[0], 1) + out_ref.shape[2:]
    out_ref[:, 0:1] = d_keys.astype(out_ref.dtype).reshape(shape)
    out_ref[:, 1:2] = d_values.astype(out_ref.dtype).reshape(shape)


def memory_back(head, counts, got, memory, part, low):
    blocks, _, own, _ = got.shape
    items, many, double = memory.shape
    pairs = double // 2 // LANES
    work = items * many * blocks * own
    return pl.pallas_call(
        memory_back_kernel,
        grid_spec=pltpu.PrefetchScalarGridSpec(
            num_scalar_prefetch=2,
            grid=(1,),
            in_specs=[
                pl.BlockSpec((blocks, 1, own, LANES), lambda i, h, c: (0, 1, 0, 0)),
                pl.BlockSpec((blocks, 1, own, LANES), lambda i, h, c: (0, 2, 0, 0)),
                pl.BlockSpec((items, many, LANES), lambda i, h, c: (0, 0, lax.div(h[0], 2))),
                pl.BlockSpec(
                    (items, many, LANES), lambda i, h, c: (0, 0, pairs + lax.div(h[0], 2))
                ),
            ],
            out_specs=whole((many // part, 2, part, LANES)),
        ),
        out_shape=jax.ShapeDtypeStruct((many // part, 2, part, LANES), BF if low else F32),
        compiler_params=pltpu.CompilerParams(vmem_limit_bytes=ROOM),
        cost_estimate=pl.CostEstimate(
            flops=work * 8 * LANES, bytes_accessed=2 << 20, transcendentals=work
        ),
        name="memory_back",
    )(head, counts, got, got, memory, memory)


def swap_half(block):
    return pltpu.roll(block, HEAD_DIM, 1)


def first_half(shape):
    return lax.broadcasted_iota(jnp.int32, shape, 1) < HEAD_DIM


def pair_to_heads(block):
    own = block.shape[0] // 2
    left, right = block[:own], block[own:]
    low = first_half(left.shape)
    return (
        jnp.where(low, left, swap_half(right)),
        jnp.where(low, swap_half(left), right),
    )


def project_kernel(tri_ref, mod_ref, q_ref, k_ref, v_ref, out_ref, normed):
    items, own, width = tri_ref.shape

    @pl.when(pl.program_id(0) == 0)
    def _():
        for item in range(items):
            unit, unused = center_scale(tri_ref[item].astype(F32))
            scale = mod_ref[item : item + 1, width:]
            shift = mod_ref[item : item + 1, :width]
            normed[item * own : (item + 1) * own] = (unit * (1.0 + scale) + shift).astype(BF)

    for kind, ref in enumerate((q_ref, k_ref, v_ref)):
        block = mm(normed[...], ref[...])
        for pair in range(WIDE // LANES):
            first, second = pair_to_heads(block[:, pair * LANES : (pair + 1) * LANES])
            out_ref[2 * pair, kind] = first.astype(BF)
            out_ref[2 * pair + 1, kind] = second.astype(BF)


def project(triplane, modulation, qkv_weight):
    items, own, width = triplane.shape
    steps = width // WIDE
    return pl.pallas_call(
        project_kernel,
        grid=(steps,),
        in_specs=[
            pl.BlockSpec((items, own, width), lambda i: (0, 0, 0)),
            pl.BlockSpec((items, 2 * width), lambda i: (0, 0)),
            pl.BlockSpec((width, WIDE), lambda i: (0, i)),
            pl.BlockSpec((width, WIDE), lambda i: (0, steps + i)),
            pl.BlockSpec((width, WIDE), lambda i: (0, 2 * steps + i)),
        ],
        out_specs=pl.BlockSpec((GROUP, 3, own, LANES), lambda i: (i, 0, 0, 0)),
        out_shape=jax.ShapeDtypeStruct((HEADS, 3, own, LANES), BF),
        scratch_shapes=[pltpu.VMEM((items * own, width), BF)],
        compiler_params=pltpu.CompilerParams(vmem_limit_bytes=ROOM),
        cost_estimate=pl.CostEstimate(
            flops=6 * items * own * width * width, bytes_accessed=8 << 20, transcendentals=0
        ),
        name="project",
    )(triplane, modulation, qkv_weight, qkv_weight, qkv_weight)


def middle_kernel(
    got_ref,
    tri_ref,
    gain,
    bias,
    out_hbm,
    query_hbm,
    att_ref,
    mid_ref,
    normed_ref,
    query_ref,
    out_w,
    query_w,
    sems,
):
    fetch_out = pltpu.make_async_copy(out_hbm, out_w, sems.at[0])
    fetch_out.start()
    fetch_query = pltpu.make_async_copy(query_hbm, query_w, sems.at[1])
    fetch_query.start()
    heads, own, _ = got_ref.shape
    for pair in range(heads // 2):
        left = got_ref[2 * pair].astype(F32)
        right = got_ref[2 * pair + 1].astype(F32)
        low = first_half(left.shape)
        span = slice(pair * LANES, (pair + 1) * LANES)
        att_ref[:own, span] = jnp.where(low, left, swap_half(right)).astype(BF)
        att_ref[own:, span] = jnp.where(low, swap_half(left), right).astype(BF)
    fetch_out.wait()
    middle = tri_ref[...].astype(F32) + mm(att_ref[...], out_w[...])
    mid_ref[...] = middle
    unit, unused = center_scale(middle)
    normed = (unit * gain[...] + bias[...]).astype(BF)
    normed_ref[...] = normed
    fetch_query.wait()
    query_ref[...] = mm(normed, query_w[...]).astype(BF)


def middle_part(got, tri_rows, self_out, gain, bias, cross_query):
    rows, width = tri_rows.shape
    low = jax.ShapeDtypeStruct((rows, width), BF)
    return pl.pallas_call(
        middle_kernel,
        grid=(1,),
        in_specs=[whole(got.shape), whole((rows, width)), whole((1, width)), whole((1, width))]
        + [ANYWHERE] * 2,
        out_specs=[whole((rows, width))] * 4,
        out_shape=[low, jax.ShapeDtypeStruct((rows, width), F32), low, low],
        scratch_shapes=[
            pltpu.VMEM(self_out.shape, BF),
            pltpu.VMEM(cross_query.shape, BF),
            pltpu.SemaphoreType.DMA((2,)),
        ],
        compiler_params=pltpu.CompilerParams(vmem_limit_bytes=ROOM),
        cost_estimate=pl.CostEstimate(
            flops=4 * rows * width * width, bytes_accessed=5 << 20, transcendentals=0
        ),
        name="middle_part",
    )(got, tri_rows, gain[None], bias[None], self_out, cross_query)


def middle_back_kernel(
    dq_ref,
    mid_ref,
    gain,
    later_ref,
    query_ref,
    crossed_ref,
    query_hbm,
    out_hbm,
    d_mid_ref,
    low_ref,
    heads_ref,
    sums_ref,
    query_w,
    out_w,
    sems,
):
    fetch_query = pltpu.make_async_copy(query_hbm, query_w, sems.at[0])
    fetch_query.start()
    fetch_out = pltpu.make_async_copy(out_hbm, out_w, sems.at[1])
    fetch_out.start()

    def by_head(values, kind):
        for pair in range(values.shape[1] // LANES):
            block = values[:, pair * LANES : (pair + 1) * LANES].astype(F32)
            first, second = pair_to_heads(block)
            heads_ref[2 * pair, kind] = first.astype(BF)
            heads_ref[2 * pair + 1, kind] = second.astype(BF)

    by_head(query_ref[...], 1)
    by_head(crossed_ref[...], 2)
    fetch_query.wait()
    d_normed = mm_nt(dq_ref[...], query_w[...])
    unit, rstd = center_scale(mid_ref[...])
    sums_ref[0:1] = jnp.sum(d_normed * unit, axis=0, keepdims=True)
    sums_ref[1:2] = jnp.sum(d_normed, axis=0, keepdims=True)
    d_middle = later_ref[...] + norm_back(unit, rstd, d_normed * gain[...])
    d_mid_ref[...] = d_middle
    low = d_middle.astype(BF)
    low_ref[...] = low
    fetch_out.wait()
    by_head(mm_nt(low, out_w[...]), 0)


def middle_back(own, d_query, cross_query, middle, gain, d_later, self_out, cross_q, d_crossed):
    rows, width = middle.shape
    return pl.pallas_call(
        middle_back_kernel,
        grid=(1,),
        in_specs=[whole((rows, width)), whole((rows, width)), whole((1, width))]
        + [whole((rows, width))] * 3
        + [ANYWHERE] * 2,
        out_specs=[
            whole((rows, width)),
            whole((rows, width)),
            whole((HEADS, 3, own, LANES)),
            whole((2, width)),
        ],
        scratch_shapes=[
            pltpu.VMEM(cross_query.shape, BF),
            pltpu.VMEM(self_out.shape, BF),
            pltpu.SemaphoreType.DMA((2,)),
        ],
        out_shape=[
            jax.ShapeDtypeStruct((rows, width), F32),
            jax.ShapeDtypeStruct((rows, width), BF),
            jax.ShapeDtypeStruct((HEADS, 3, own, LANES), BF),
            jax.ShapeDtypeStruct((2, width), F32),
        ],
        compiler_params=pltpu.CompilerParams(vmem_limit_bytes=ROOM),
        cost_estimate=pl.CostEstimate(
            flops=4 * rows * width * width, bytes_accessed=6 << 20, transcendentals=0
        ),
        name="middle_back",
    )(d_query, middle, gain[None], d_later, cross_q, d_crossed, cross_query, self_out)


def first_back_kernel(
    steps, got_ref, q_ref, k_ref, v_ref, tri_ref, mod_ref, mid_ref, out_ref, total
):
    items, own, width = tri_ref.shape
    step = pl.program_id(0)
    added = None
    for kind, ref in enumerate((q_ref, k_ref, v_ref)):
        columns = []
        for pair in range(WIDE // LANES):
            at = slice(kind * own, (kind + 1) * own)
            left = got_ref[2 * pair, at].astype(F32)
            right = got_ref[2 * pair + 1, at].astype(F32)
            low = first_half(left.shape)
            columns.append(
                jnp.concatenate(
                    [
                        jnp.where(low, left, swap_half(right)),
                        jnp.where(low, swap_half(left), right),
                    ],
                    axis=0,
                )
            )
        term = mm_nt(jnp.concatenate(columns, axis=1).astype(BF), ref[...])
        added = term if added is None else added + term

    @pl.when(step == 0)
    def _():
        total[...] = added

    @pl.when(step > 0)
    def _():
        total[...] += added

    @pl.when(step == steps - 1)
    def _():
        for item in range(items):
            unit, rstd = center_scale(tri_ref[item].astype(F32))
            grad = total[item * own : (item + 1) * own] * (1.0 + mod_ref[item : item + 1, width:])
            out_ref[item] = mid_ref[item] + norm_back(unit, rstd, grad)


def first_back(got, qkv_weight, triplane, modulation, d_middle):
    items, own, width = triplane.shape
    steps = width // WIDE
    return pl.pallas_call(
        functools.partial(first_back_kernel, steps),
        grid=(steps,),
        in_specs=[
            pl.BlockSpec((GROUP,) + got.shape[1:], lambda i: (i, 0, 0)),
            pl.BlockSpec((width, WIDE), lambda i: (0, i)),
            pl.BlockSpec((width, WIDE), lambda i: (0, steps + i)),
            pl.BlockSpec((width, WIDE), lambda i: (0, 2 * steps + i)),
            pl.BlockSpec((items, own, width), lambda i: (0, 0, 0)),
            pl.BlockSpec((items, 2 * width), lambda i: (0, 0)),
            pl.BlockSpec((items, own, width), lambda i: (0, 0, 0)),
        ],
        out_specs=pl.BlockSpec((items, own, width), lambda i: (0, 0, 0)),
        out_shape=jax.ShapeDtypeStruct((items, own, width), F32),
        scratch_shapes=[pltpu.VMEM((items * own, width), F32)],
        compiler_params=pltpu.CompilerParams(vmem_limit_bytes=ROOM),
        cost_estimate=pl.CostEstimate(
            flops=6 * items * own * width * width, bytes_accessed=8 << 20, transcendentals=0
        ),
        name="first_back",
    )(got, qkv_weight, qkv_weight, qkv_weight, triplane, modulation, d_middle)


def head_back_kernel(
    packed,
    head_ref,
    dq_ref,
    dkv_ref,
    dmem_ref,
    tri_ref,
    patch_ref,
    q_ref,
    k_ref,
    v_ref,
    mod_ref,
    *rest,
):
    units = rest[-1]
    items, many, width = tri_ref.shape
    odd = lax.rem(head_ref[0], 2) == 1
    grads = [
        dq_ref[:, 0].reshape(many, LANES).astype(F32).T,
        dkv_ref[:, 0].reshape(many, LANES).astype(F32).T,
        dkv_ref[:, 1].reshape(many, LANES).astype(F32).T,
    ]
    weight = []
    for ref in (q_ref, k_ref, v_ref):
        turned = ref[...].astype(F32).T
        weight.append(jnp.where(odd, turned[HEAD_DIM:], turned[:HEAD_DIM]))
    weight = jnp.concatenate(weight, axis=0)
    product = None
    terms = []
    for item in range(items):
        unit, unused = center_scale(tri_ref[item].astype(F32))
        units[...] = unit.astype(BF)
        span = slice(item * HEAD_DIM, (item + 1) * HEAD_DIM)
        mine = jnp.concatenate([part[span] for part in grads], axis=0)
        outer = mm(mine.astype(BF), units[...])
        column = jnp.sum(mine, axis=1, keepdims=True)
        shift = mod_ref[item : item + 1, :width]
        scale = mod_ref[item : item + 1, width:]
        terms.append(jnp.sum(column * weight, axis=0, keepdims=True))
        terms.append(jnp.sum(outer * weight, axis=0, keepdims=True))
        term = outer * (1.0 + scale) + column * shift
        product = term if product is None else product + term
    product = product.T
    patch_rows = patch_ref.shape[1]
    grads = [dmem_ref[:, kind].reshape(patch_rows, LANES).astype(F32).T for kind in range(2)]
    memory = None
    for item in range(items):
        span = slice(item * HEAD_DIM, (item + 1) * HEAD_DIM)
        mine = jnp.concatenate([part[span] for part in grads], axis=0).astype(BF)
        term = mm(mine, patch_ref[item])
        memory = term if memory is None else memory + term
    memory = memory.T
    if not packed:
        out_ref, memory_ref, terms_ref = rest[:3]
        out_ref[...] = product.astype(BF)
        memory_ref[...] = memory.astype(BF)
        for item in range(items):
            terms_ref[item : item + 1, :width] = terms[2 * item]
            terms_ref[item : item + 1, width:] = terms[2 * item + 1]
        return
    ends_ref, out_ref, terms_ref, unused = rest
    devices = out_ref.shape[0]
    span = width // devices
    product = product.reshape(devices, span, 3 * HEAD_DIM).astype(BF)
    out_ref[:, :span] = memory.reshape(devices, span, LANES).astype(BF)
    out_ref[:, span : 2 * span] = product[:, :, :LANES]
    last = product[:, :, LANES:]
    at = 2 * span + span // 2
    out_ref[:, 2 * span : at] = jnp.concatenate(
        [last[:, : span // 2], last[:, span // 2 :]], axis=2
    )
    out_ref[:, at:] = ends_ref[...]
    lines = [
        term[:, k * LANES : (k + 1) * LANES] for term in terms for k in range(width // LANES)
    ]
    terms_ref[...] = jnp.concatenate(lines, axis=0).astype(BF)


def head_back(head, d_q, d_kv, d_mem, rows_all, patch_part, qkv_weight, modulation, ends):
    items, many, width = rows_all.shape
    blocks, _, own, _ = d_q.shape
    pairs = width // LANES
    product = jax.ShapeDtypeStruct((width, 3 * HEAD_DIM), BF)
    if ends is None:
        more = []
        shapes = [
            product,
            jax.ShapeDtypeStruct((width, LANES), BF),
            jax.ShapeDtypeStruct((items, 2 * width), F32),
        ]
    else:
        devices, tail, _ = ends.shape
        more = [ends]
        many_rows = 5 * width // devices // 2 + tail
        shapes = [
            jax.ShapeDtypeStruct((devices, many_rows, LANES), BF),
            jax.ShapeDtypeStruct((2 * items * pairs, LANES), BF),
        ]

    def whole_block(shape):
        return pl.BlockSpec(shape, lambda i, h: (0,) * len(shape))

    return pl.pallas_call(
        functools.partial(head_back_kernel, ends is not None),
        grid_spec=pltpu.PrefetchScalarGridSpec(
            num_scalar_prefetch=1,
            grid=(1,),
            in_specs=[
                pl.BlockSpec((blocks, 1, own, LANES), lambda i, h: (0, 0, 0, 0)),
                pl.BlockSpec((blocks, 2, own, LANES), lambda i, h: (0, 0, 0, 0)),
                whole_block(d_mem.shape),
                pl.BlockSpec((items, many, width), lambda i, h: (0, 0, 0)),
                whole_block(patch_part.shape),
                pl.BlockSpec((width, LANES), lambda i, h: (0, lax.div(h[0], 2))),
                pl.BlockSpec((width, LANES), lambda i, h: (0, pairs + lax.div(h[0], 2))),
                pl.BlockSpec((width, LANES), lambda i, h: (0, 2 * pairs + lax.div(h[0], 2))),
                whole_block((items, 2 * width)),
            ]
            + [whole_block(array.shape) for array in more],
            out_specs=[whole_block(shape.shape) for shape in shapes],
            scratch_shapes=[pltpu.VMEM((many, width), BF)],
        ),
        out_shape=shapes,
        compiler_params=pltpu.CompilerParams(vmem_limit_bytes=ROOM),
        cost_estimate=pl.CostEstimate(
            flops=6 * items * many * width * HEAD_DIM, bytes_accessed=5 << 20, transcendentals=0
        ),
        name="head_back",
    )(
        head,
        d_q,
        d_kv,
        d_mem,
        rows_all,
        patch_part,
        qkv_weight,
        qkv_weight,
        qkv_weight,
        modulation,
        *more,
    )


def by_heads_kernel(got_ref, out_ref):
    parts, heads, rows, _ = got_ref.shape
    width = heads * HEAD_DIM
    for pair in range(heads // 2):
        left = got_ref[0, 2 * pair].astype(F32)
        right = got_ref[0, 2 * pair + 1].astype(F32)
        for part in range(1, parts):
            left = left + got_ref[part, 2 * pair].astype(F32)
            right = right + got_ref[part, 2 * pair + 1].astype(F32)
        for kind in range(3):
            span = slice(kind * HEAD_DIM, (kind + 1) * HEAD_DIM)
            at = kind * width + pair * LANES
            out_ref[:, at : at + LANES] = jnp.concatenate([left[:, span], right[:, span]], axis=1)


def by_heads(got):
    parts, heads, rows, features = got.shape
    return pl.pallas_call(
        by_heads_kernel,
        grid=(1,),
        in_specs=[whole(got.shape)],
        out_specs=whole((rows, heads * features)),
        out_shape=jax.ShapeDtypeStruct((rows, heads * features), F32),
        compiler_params=pltpu.CompilerParams(vmem_limit_bytes=ROOM),
        name="by_heads",
    )(got)


def unpack_kernel(tail, got_ref, mem_ref, qkv_ref, mod_ref, ends_ref):
    span = qkv_ref.shape[0]
    width = HEADS * HEAD_DIM
    at = 2 * span + span // 2

    def columns(head):
        full = got_ref[head, :at].astype(F32)
        last = full[2 * span :]
        last = jnp.concatenate([last[:, :HEAD_DIM], last[:, HEAD_DIM:]], axis=0)
        first, second = full[:span], full[span : 2 * span]
        return (
            first[:, :HEAD_DIM],
            first[:, HEAD_DIM:],
            second[:, :HEAD_DIM],
            second[:, HEAD_DIM:],
            last,
        )

    for pair in range(HEADS // 2):
        both = [
            jnp.concatenate(sides, axis=1)
            for sides in zip(columns(2 * pair), columns(2 * pair + 1))
        ]
        for kind in range(2):
            start = kind * width + pair * LANES
            mem_ref[:, start : start + LANES] = both[kind]
        for kind in range(3):
            start = kind * width + pair * LANES
            qkv_ref[:, start : start + LANES] = both[2 + kind]
    total = got_ref[0, at:].astype(F32)
    for head in range(1, HEADS):
        total = total + got_ref[head, at:].astype(F32)
    ends_ref[...] = total[:tail]
    mod_ref[...] = total[tail:]


def unpack(got, span, tail):
    _, many, _ = got.shape
    shapes = [
        (span, 2 * HEADS * HEAD_DIM),
        (span, 3 * HEADS * HEAD_DIM),
        (many - tail - 2 * span - span // 2, LANES),
        (tail, LANES),
    ]
    return pl.pallas_call(
        functools.partial(unpack_kernel, tail),
        grid=(1,),
        in_specs=[whole(got.shape)],
        out_specs=[whole(shape) for shape in shapes],
        out_shape=[jax.ShapeDtypeStruct(shape, F32) for shape in shapes],
        compiler_params=pltpu.CompilerParams(vmem_limit_bytes=ROOM),
        name="unpack",
    )(got)


def gather_lanes(block, starts, span):
    out = []
    lane = lax.broadcasted_iota(jnp.int32, (block.shape[0], LANES), 1)
    for at in range(0, len(starts) * span, LANES):
        merged = None
        for to in range(0, LANES, min(span, LANES)):
            start = starts[(at + to) // span] + (at + to) % span
            base = start // LANES * LANES
            part = block[:, base : base + LANES]
            shift = (to - (start - base)) % LANES
            if shift:
                part = pltpu.roll(part, shift, 1)
            if merged is None:
                merged = part
            else:
                merged = jnp.where((lane >= to) & (lane < to + span), part, merged)
        out.append(merged)
    return jnp.concatenate(out, axis=1)


def starts_y(features, devices, quarter):
    span = features // devices
    return [(group * 4 + quarter) * span for group in range(devices // 4)]


def starts_x(features, devices, half, low):
    span = features // devices
    many = devices // 2
    return [
        (half * many + rest * 4 + y * 2 + low) * span
        for y in range(2)
        for rest in range(many // 4)
    ]


def mlp_kernel(
    steps,
    devices,
    normed_ref,
    dh_ref,
    up_ref,
    later_ref,
    c_ref,
    gain,
    out_w,
    hidden_ref,
    pre_ref,
    up_piece_ref,
    down_piece_ref,
    d_later_ref,
    low_ref,
    d_crossed_ref,
    sums_ref,
    total,
):
    step = pl.program_id(0)

    @pl.when(step == 0)
    def _():
        values = normed_ref[...].astype(F32)
        for quarter in range(4):
            starts = starts_y(values.shape[1], devices, quarter)
            span = values.shape[1] // devices
            up_piece_ref[quarter] = gather_lanes(values, starts, span).astype(BF)

    pre = mm(normed_ref[...], up_ref[...])
    square = pre * pre
    slope = (2.0 / 3.141592653589793) ** 0.5
    turn = jnp.tanh(slope * (pre + 0.044715 * (pre * square)))
    hidden = 0.5 * pre * (1.0 + turn)
    hidden_ref[...] = hidden.astype(BF)
    part = hidden.shape[1]
    span = part * steps // devices
    half = lax.div(step, steps // 2)
    for low in range(2):
        for y in range(2):
            starts = [(rest * 4 + y * 2 + low) * span for rest in range(part // (4 * span))]
            at = y * (part * steps // 8) + lax.rem(step, steps // 2) * (part // 4)
            at = pl.ds(pl.multiple_of(at, LANES), part // 4)
            down_piece_ref[2 * half + low, :, at] = gather_lanes(hidden, starts, span).astype(BF)
    change = 0.5 * (1.0 + turn) + 0.5 * pre * (1.0 - turn * turn) * (
        slope * (1.0 + 3.0 * 0.044715 * square)
    )
    d_pre = (dh_ref[...] * change).astype(BF)
    pre_ref[...] = d_pre
    added = mm_nt(d_pre, up_ref[...])

    @pl.when(step == 0)
    def _():
        total[...] = added

    @pl.when(step > 0)
    def _():
        total[...] += added

    @pl.when(step == steps - 1)
    def _():
        d_normed = total[...]
        unit, rstd = center_scale(later_ref[...])
        sums_ref[0:1] = jnp.sum(d_normed * unit, axis=0, keepdims=True)
        sums_ref[1:2] = jnp.sum(d_normed, axis=0, keepdims=True)
        d_later = c_ref[...].astype(F32) + norm_back(unit, rstd, d_normed * gain[...])
        d_later_ref[...] = d_later
        low = d_later.astype(BF)
        low_ref[...] = low
        d_crossed_ref[...] = mm_nt(low, out_w[...]).astype(BF)


def mlp(devices, normed, d_hidden, up_weight, later, grad_out, gain, cross_out):
    rows, width = normed.shape
    hidden_width = up_weight.shape[1]
    part = min(1024, hidden_width)
    steps = hidden_width // part
    low = jax.ShapeDtypeStruct((rows, width), BF)
    return pl.pallas_call(
        functools.partial(mlp_kernel, steps, devices),
        grid=(steps,),
        in_specs=[
            whole((rows, width)),
            pl.BlockSpec((rows, part), lambda i: (0, i)),
            pl.BlockSpec((width, part), lambda i: (0, i)),
            whole((rows, width)),
            whole((rows, width)),
            whole((1, width)),
            whole((width, width)),
        ],
        out_specs=[
            pl.BlockSpec((rows, part), lambda i: (0, i)),
            pl.BlockSpec((rows, part), lambda i: (0, i)),
            whole((4, rows, width // 4)),
            whole((4, rows, hidden_width // 4)),
            whole((rows, width)),
            whole((rows, width)),
            whole((rows, width)),
            whole((2, width)),
        ],
        out_shape=[
            jax.ShapeDtypeStruct((rows, hidden_width), BF),
            jax.ShapeDtypeStruct((rows, hidden_width), BF),
            jax.ShapeDtypeStruct((4, rows, width // 4), BF),
            jax.ShapeDtypeStruct((4, rows, hidden_width // 4), BF),
            jax.ShapeDtypeStruct((rows, width), F32),
            low,
            low,
            jax.ShapeDtypeStruct((2, width), F32),
        ],
        scratch_shapes=[pltpu.VMEM((rows, width), F32)],
        compiler_params=pltpu.CompilerParams(vmem_limit_bytes=ROOM),
        cost_estimate=pl.CostEstimate(
            flops=4 * rows * width * hidden_width,
            bytes_accessed=12 << 20,
            transcendentals=rows * hidden_width,
        ),
        name="mlp",
    )(normed, d_hidden, up_weight, later, grad_out, gain[None], cross_out)


def pieces_kernel(devices, *refs):
    out_ref = refs[-1]
    for k, ref in enumerate(refs[:-1]):
        values = ref[...].astype(F32)
        span = values.shape[1] // devices
        for half in range(2):
            for low in range(2):
                starts = starts_x(values.shape[1], devices, half, low)
                out_ref[2 * half + low, k] = gather_lanes(values, starts, span).astype(BF)


def pieces(devices, *arrays):
    rows, width = arrays[0].shape
    return pl.pallas_call(
        functools.partial(pieces_kernel, devices),
        grid=(1,),
        in_specs=[whole((rows, width))] * len(arrays),
        out_specs=whole((4, len(arrays), rows, width // 4)),
        out_shape=jax.ShapeDtypeStruct((4, len(arrays), rows, width // 4), BF),
        compiler_params=pltpu.CompilerParams(vmem_limit_bytes=ROOM),
        name="pieces",
    )(*arrays)


def product_kernel(half_ref, *refs):
    x_refs, y_refs, (keep_ref, send_ref, left) = refs[:4], refs[4:8], refs[8:]

    @pl.when(pl.program_id(1) == 0)
    def _():
        left[...] = jnp.concatenate([ref[0] for ref in x_refs], axis=0).T

    right = jnp.concatenate([ref[0] for ref in y_refs], axis=0)
    quads, _, span, many = keep_ref.shape
    both = mm(left[...], right).reshape(2, quads, 1, span, many)

    @pl.when(half_ref[0] == 0)
    def _():
        keep_ref[...] = both[0].astype(BF)
        send_ref[...] = both[1].astype(BF)

    @pl.when(half_ref[0] == 1)
    def _():
        keep_ref[...] = both[1].astype(BF)
        send_ref[...] = both[0].astype(BF)


def product(half, quads, left, right):
    entries, rows, wide = left[0].shape
    columns = right[0].shape[2]
    span = wide // (2 * quads)
    part = min(columns, 512)
    shape = jax.ShapeDtypeStruct((quads, entries, span, columns), BF)
    spec = pl.BlockSpec((quads, 1, span, part), lambda e, i: (0, e, 0, i))
    return pl.pallas_call(
        product_kernel,
        grid=(entries, columns // part),
        in_specs=[IN_SMEM]
        + [pl.BlockSpec((1, rows, wide), lambda e, i: (e, 0, 0))] * 4
        + [pl.BlockSpec((1, rows, part), lambda e, i: (e, 0, i))] * 4,
        out_specs=[spec, spec],
        out_shape=[shape, shape],
        scratch_shapes=[pltpu.VMEM((wide, 4 * rows), BF)],
        compiler_params=pltpu.CompilerParams(vmem_limit_bytes=ROOM),
        cost_estimate=pl.CostEstimate(
            flops=8 * entries * rows * wide * columns, bytes_accessed=8 << 20, transcendentals=0
        ),
        name="product",
    )(half.reshape(1).astype(jnp.int32), *left, *right)


def xor_blk(values, bit, count):
    return lax.ppermute(values, "blk", [(i, i ^ bit) for i in range(count)])


def swap_batch(values):
    return lax.ppermute(values, "batch", [(0, 1), (1, 0)])


def after(values, *first):
    return lax.optimization_barrier((values, first))[0]


def take(values, index, axis):
    return lax.dynamic_index_in_dim(values, index, axis, keepdims=False)


def local(
    count_blk,
    triplane,
    patches,
    cotangent,
    camera_index,
    triplane_count,
    patch_count,
    camera_table,
    mod_weight,
    qkv_weight,
    self_out,
    gain_mid,
    bias_mid,
    cross_query,
    cross_memory,
    cross_out,
    gain_last,
    bias_last,
    up_weight,
    down_weight,
):
    items, own, width = triplane.shape
    own_patches = patches.shape[1]
    rows = items * own
    spare = count_blk // HEADS
    quads = count_blk // 4
    devices = 2 * count_blk
    row_groups = (
        None
        if spare == 1
        else [[part * HEADS + head for head in range(HEADS)] for part in range(spare)]
    )
    head_groups = [[part * HEADS + head for part in range(spare)] for head in range(HEADS)]
    batch_at = lax.axis_index("batch")
    blk_at = lax.axis_index("blk")
    head_at = lax.rem(blk_at, HEADS)
    place = batch_at * count_blk + blk_at

    def to_heads(values):
        return lax.all_to_all(values, "blk", 0, 0, axis_index_groups=row_groups, tiled=True)

    def swap_corner(values):
        return lax.ppermute(
            values,
            BOTH,
            [
                (b * count_blk + j, (1 - b) * count_blk + (j ^ 1))
                for b in range(2)
                for j in range(count_blk)
            ],
        )

    def quad_y(values):
        far = xor_blk(values, 2, count_blk)
        return [values, xor_blk(values, 1, count_blk), far, xor_blk(far, 1, count_blk)]

    def quad_x(values):
        far = swap_batch(values)
        return [values, xor_blk(values, 1, count_blk), far, xor_blk(far, 1, count_blk)]

    def exchange_y(cut):
        low = jnp.bitwise_and(blk_at, 3)
        got = [take(cut, low, 0)]
        for bit in (1, 2, 3):
            got.append(xor_blk(take(cut, jnp.bitwise_xor(low, bit), 0), bit, count_blk))
        return got

    def exchange_x(cut):
        low = jnp.bitwise_and(blk_at, 1)
        return [
            take(cut, 2 * batch_at + low, 0),
            xor_blk(take(cut, 2 * batch_at + 1 - low, 0), 1, count_blk),
            swap_batch(take(cut, 2 * (1 - batch_at) + low, 0)),
            swap_corner(take(cut, 2 * (1 - batch_at) + 1 - low, 0)),
        ]

    def half_x(values):
        given = swap_batch(take(values, 1 - batch_at, 0))
        return (take(values, batch_at, 0).astype(F32) + given.astype(F32)).astype(BF)

    def rest_sum(keep, given):
        many = quads
        bit = 4
        while many > 1:
            low = jnp.bitwise_and(lax.div(blk_at, bit), 1)
            shape = (many // 2, 2) + keep.shape[1:]
            keep, given = keep.reshape(shape), given.reshape(shape)

            def part(index):
                total = take(keep, index, 1).astype(F32) + take(given, index, 1).astype(F32)
                return total.astype(BF)

            keep, given = part(low), xor_blk(part(1 - low), bit, count_blk)
            many //= 2
            bit *= 2
        return (keep.astype(F32) + given.astype(F32))[0]

    views = camera_index.shape[1]
    table_rows = jnp.arange(camera_table.shape[0], dtype=jnp.int32)

    def pick_of(cams):
        return jnp.sum((cams[:, :, None] == table_rows[None, None, :]).astype(F32), axis=1)

    def code_of(pick):
        return (mm(pick.astype(BF), camera_table) / views).astype(BF)

    modulation = mm(code_of(pick_of(camera_index)), mod_weight)
    sent = project(triplane, modulation, qkv_weight)
    qkv = to_heads(sent)

    patches_all = lax.all_gather(patches, "blk", axis=1, tiled=True)
    bit_y = jnp.bitwise_and(lax.div(blk_at, 2), 1)
    many_patches = patches_all.shape[1]
    memory = (
        mm(patches_all.reshape(items * many_patches, width), cross_memory)
        .astype(BF)
        .reshape(items, many_patches, 2 * width)
    )
    grad_out = cotangent.reshape(rows, width)
    d_hidden = mm_nt(grad_out, down_weight)
    grad_quad = quad_x(lax.optimization_barrier((grad_out, sent))[0])

    qkv, d_hidden = lax.optimization_barrier((qkv, d_hidden))
    if spare == 1:
        kv, kv_first = qkv, 1
    else:
        kv = lax.all_gather(qkv[:, 1:], "blk", axis=0, axis_index_groups=head_groups, tiled=True)
        kv_first = 0
    attended_heads, self_lse = self_forward(triplane_count, qkv, kv, kv_first)
    attended_got = to_heads(attended_heads)
    kept = lax.optimization_barrier((triplane, attended_heads))[0]
    rows_all = lax.all_gather(kept, "blk", axis=1, axis_index_groups=row_groups, tiled=True)

    attended_got, memory, grad_quad = lax.optimization_barrier(
        (attended_got, memory, grad_quad)
    )
    attended_low, middle, normed_mid, cross_q = middle_part(
        attended_got, triplane.reshape(rows, width), self_out, gain_mid, bias_mid, cross_query
    )
    cross_q = cross_q.reshape(items, own, width)
    crossed, cross_lse, later, normed_last = cross_forward(
        patch_count, cross_q, memory, middle, cross_out, gain_last, bias_last
    )
    hidden, d_pre, last_pieces, hidden_pieces, d_later, d_later_low, d_crossed, sums_last = mlp(
        devices, normed_last, d_hidden, up_weight, later, grad_out, gain_last, cross_out
    )
    pre_far = xor_blk(d_pre, 2, count_blk)
    pre_near = xor_blk(d_pre, 1, count_blk)
    last_pieces = exchange_y(last_pieces)
    hidden_pieces = exchange_x(hidden_pieces)

    d_cross_q = cross_backward(
        patch_count, cross_q, memory, d_crossed.reshape(items, own, width), cross_lse
    )
    d_cross_low = d_cross_q.reshape(rows, width)
    d_middle, d_middle_low, back_heads, sums_mid = middle_back(
        own,
        d_cross_low,
        cross_query,
        middle,
        gain_mid,
        d_later,
        self_out,
        cross_q.reshape(rows, width),
        d_crossed,
    )
    pre_quad = [d_pre, pre_near, pre_far, xor_blk(pre_far, 1, count_blk)]
    back_heads = to_heads(back_heads)

    up_keep, up_send = product(
        batch_at, quads, [p[None] for p in last_pieces], [p[None] for p in pre_quad]
    )
    down_keep, down_send = product(
        bit_y, quads, [p[None] for p in hidden_pieces], [p[None] for p in grad_quad]
    )
    up_given = swap_batch(up_send)
    down_given = xor_blk(down_send, 2, count_blk)
    lefts, rights = after(
        (
            (crossed.reshape(rows, width), normed_mid, attended_low),
            (d_later_low, d_cross_low, d_middle_low),
        ),
        up_keep,
        down_keep,
    )
    squares = exchange_x(pieces(devices, *lefts))
    rights = jnp.stack(rights)
    rights_far = swap_batch(rights)
    rights_near = xor_blk(rights, 1, count_blk)

    back_heads = after(back_heads, up_keep, down_keep)
    d_q, d_kv = self_backward(
        triplane_count, qkv, kv, kv_first, back_heads, self_lse, spare == 1
    )
    head = head_at.reshape(1).astype(jnp.int32)
    d_mem = memory_back(head, patch_count, back_heads, memory, own_patches, spare == 1)
    if spare > 1:
        d_kv, d_mem = [
            lax.psum_scatter(
                values, "blk", scatter_dimension=0, axis_index_groups=head_groups, tiled=True
            ).astype(BF)
            for values in (d_kv, d_mem)
        ]
    d_got = to_heads(
        jnp.concatenate(
            [values.reshape(HEADS, -1, LANES) for values in (d_q, d_kv, d_mem)], axis=1
        )
    )

    mod_rows = width // devices
    ends = jnp.concatenate([sums_mid, sums_last], axis=0)
    ends = jnp.transpose(ends.reshape(4, devices, -1), (1, 0, 2)).reshape(devices, 1, -1)
    packed = mod_rows % 32 == 0 and ends.shape[2] == LANES and spare == 1
    if packed:
        high = ends.astype(BF)
        low = (ends - high.astype(F32)).astype(BF)
        ends = jnp.concatenate([high, low, jnp.zeros((devices, 14, LANES), BF)], axis=1)
    part_patches = HEADS * own_patches
    first_patch = lax.div(blk_at, HEADS) * part_patches
    payload = head_back(
        head,
        d_q,
        d_kv,
        d_mem,
        rows_all,
        lax.dynamic_slice_in_dim(patches_all, first_patch, part_patches, 1)
        if spare > 1
        else patches_all,
        qkv_weight,
        modulation,
        ends if packed else None,
    )
    later = after(later, payload)

    squares_quad = [rights, rights_near, rights_far, xor_blk(rights_far, 1, count_blk)]
    squares_keep, squares_send = product(bit_y, quads, squares, squares_quad)
    squares_given = xor_blk(squares_send, 2, count_blk)

    d_memory_rows = d_got[:, 3 * own :].reshape(HEADS, 2, own_patches, items, HEAD_DIM)
    d_memory_rows = jnp.transpose(d_memory_rows, (3, 2, 1, 0, 4)).reshape(-1, 2 * width)
    d_patches = mm_nt(d_memory_rows, cross_memory)

    def spread(values):
        span = values.shape[0] // devices
        return lax.all_to_all(
            values.reshape(devices, span, values.shape[1]), BOTH, 0, 0, tiled=True
        )

    if packed:
        own_part, terms = payload
        own_part = own_part.reshape((2, HEADS) + own_part.shape[1:])
        own_part = half_x(own_part)
        terms = jnp.broadcast_to(terms, (HEADS,) + terms.shape)
        got = to_heads(jnp.concatenate([own_part, terms], axis=1))
        g_cross_mem, g_qkv, d_modulation, ends = unpack(got, mod_rows, 16)
        ends = (ends[0] + ends[1]).reshape(4, -1)
        others = swap_batch(d_modulation)
        d_modulation = jnp.where(
            batch_at == 0,
            jnp.concatenate([d_modulation, others], axis=0),
            jnp.concatenate([others, d_modulation], axis=0),
        )
    else:
        qkv_product, memory_product, terms = payload
        g_qkv = by_heads(spread(qkv_product).reshape(2 * spare, HEADS, mod_rows, 3 * HEAD_DIM))
        terms = terms.reshape(1, -1, ends.shape[2])
        terms = jnp.broadcast_to(terms, (devices,) + terms.shape[1:])
        small = lax.all_to_all(jnp.concatenate([terms, ends], axis=1), BOTH, 0, 0, tiled=True)
        ends = jnp.sum(small[:, -1], axis=0).reshape(4, -1)
        d_modulation = jnp.sum(small[:, :-1].reshape(2, count_blk, -1), axis=1)
        memory_got = spread(memory_product).astype(F32)
        memory_got = memory_got.reshape(2 * spare, HEADS, mod_rows, 2, HEAD_DIM)
        memory_got = jnp.transpose(jnp.sum(memory_got, axis=0), (1, 2, 0, 3))
        g_cross_mem = memory_got.reshape(mod_rows, 2 * width)
    d_modulation = d_modulation.reshape(2 * items, 2 * width)
    own_cams = lax.optimization_barrier((camera_index, modulation))[0]
    others = swap_batch(own_cams)
    cams = jnp.where(
        batch_at == 0,
        jnp.concatenate([own_cams, others], axis=0),
        jnp.concatenate([others, own_cams], axis=0),
    )
    pick = pick_of(cams)
    code_low = code_of(pick)
    code_rows = lax.dynamic_slice_in_dim(code_low, place * mod_rows, mod_rows, 1).astype(F32)
    g_mod = jnp.sum(code_rows[:, :, None] * d_modulation[:, None, :], axis=0)
    d_code = mm_nt(d_modulation.astype(BF), mod_weight)
    cam_rows = camera_table.shape[0] // devices
    pick_rows = lax.dynamic_slice_in_dim(pick, place * cam_rows, cam_rows, 1)
    g_table = jnp.sum(pick_rows[:, :, None] * d_code[:, None, :], axis=0) / views

    d_triplane = first_back(
        d_got, qkv_weight, triplane, modulation, d_middle.reshape(items, own, width)
    )
    g_up = rest_sum(up_keep, up_given)[0]
    g_down = rest_sum(down_keep, down_given)[0]
    g_squares = rest_sum(squares_keep, squares_given)
    result = later + mm(hidden, down_weight)
    return (
        result.reshape(items, own, width),
        d_triplane,
        d_patches.reshape(items, own_patches, width),
        g_table,
        g_mod,
        g_qkv,
        g_squares[2],
        ends[0],
        ends[1],
        g_squares[1],
        g_cross_mem,
        g_squares[0],
        ends[2],
        ends[3],
        g_up,
        g_down,
    )


def solution(mesh):
    rows = P("batch", "blk", None)
    split = P(BOTH, None)
    line = P(BOTH)
    whole = P()
    return jax.shard_map(
        functools.partial(local, mesh.shape["blk"]),
        mesh=mesh,
        in_specs=(rows, rows, rows, P("batch", None), P("batch"), P("batch")) + (whole,) * 13,
        out_specs=(
            rows,
            rows,
            rows,
            split,
            split,
            split,
            split,
            line,
            line,
            split,
            split,
            split,
            line,
            line,
            split,
            split,
        ),
        check_vma=False,
    )
```

profile of v0, /device:TPU:0, one launch (start us, length us, event | category | flops | bytes accessed | tf_op | source)
XLA Modules:
  0.0 292.0 jit_solution(14306193310701742295)
XLA Ops:
  8.7 3.6 %fusion.3.mod_ref = f32[2,2048]{1,0:T(2,128)} fusion(bf16[1024,2048]{1,0:T(8,128)(2,1)} %param.26, bf16[256,1024]{1,0:T(8,128)(2,1)S(1)} %copy-done, bf16[2,256]{1,0:T(2,128)(2,1)S(1)} %convert_reduce_fusion.1), kind=kOutput, calls=%fused_computation.6 | convolution fusion | flops 9441280 | bytes 4736000 | tf_op jit(solution)/shard_map/dot_general | solution.py:30
  12.3 5.6 %project.1 = bf16[16,3,48,128]{3,2,1,0:T(8,128)(2,1)} custom-call(bf16[2,48,1024]{2,1,0:T(8,128)(2,1)} %tri_ref.3, f32[2,2048]{1,0:T(2,128)} %fusion.3.mod_ref, bf16[1024,3072]{1,0:T(8,128)(2,1)} %v_ref.5, bf16[1024,3072]{1,0:T(8,128)(2,1)} %v_ref.5, bf16[1024,3072]{1,0:T(8,128)(2,1)} %v_ref.5), custom_call_target="tpu_custom_call" | custom-call | flops 603979776 | bytes 8388608 | tf_op jit(solution)/shard_map/project/pallas_call | solution.py:434
  17.9 7.4 %all-to-all-start = ((bf16[16,3,48,128]{3,2,1,0:T(8,128)(2,1)}), bf16[16,3,48,128]{3,2,1,0:T(8,128)(2,1)S(1)}, u32[]{:S(2)}, u32[]{:S(2)}) async-start(bf16[16,3,48,128]{3,2,1,0:T(8,128)(2,1)} %project.1), calls=%async_computation | async-start | bytes 1179648 | tf_op jit(solution)/shard_map/all_to_all | solution.py:1168
  25.4 1.6 collective-permute-start.1
  26.9 7.2 %fusion.26.dh_ref = f32[96,4096]{1,0:T(8,128)} fusion(bf16[96,1024]{1,0:T(8,128)(2,1)S(1)} %bitcast.176, bf16[4096,1024]{1,0:T(8,128)(2,1)} %param.37), kind=kOutput, calls=%fused_computation.83 | convolution fusion | flops 805306368 | bytes 10158080 | tf_op jit(solution)/shard_map/dot_general | solution.py:34
  34.2 7.3 %all-to-all-done.q_ref.k_ref.v_ref = bf16[16,3,48,128]{3,2,1,0:T(8,128)(2,1)S(1)} async-done(((bf16[16,3,48,128]{3,2,1,0:T(8,128)(2,1)}), bf16[16,3,48,128]{3,2,1,0:T(8,128)(2,1)S(1)}, u32[]{:S(2)}, u32[]{:S(2)}) %all-to-all-start) | async-done | bytes 589856 | tf_op jit(solution)/shard_map/all_to_all | solution.py:1168
  42.3 4.3 %self_forward.1 = (bf16[16,48,128]{2,1,0:T(8,128)(2,1)}, f32[2,768]{1,0:T(2,128)}) custom-call(s32[2]{0:T(128)} %count_ref.8, bf16[16,3,48,128]{3,2,1,0:T(8,128)(2,1)} %copy-done.15, bf16[16,3,48,128]{3,2,1,0:T(8,128)(2,1)} %copy-done.15, bf16[16,3,48,128]{3,2,1,0:T(8,128)(2,1)} %copy-done.15), custom_call_target="tpu_custom_call" | custom-call | flops 603979776 | bytes 1048576 | tf_op jit(solution)/shard_map/self_forward/pallas_call | solution.py:146
  46.6 1.6 collective-permute-start.12
  48.9 6.3 %all-to-all-start.1 = ((bf16[16,48,128]{2,1,0:T(8,128)(2,1)}), bf16[16,48,128]{2,1,0:T(8,128)(2,1)S(1)}, u32[]{:S(2)}, u32[]{:S(2)}) async-start(bf16[16,48,128]{2,1,0:T(8,128)(2,1)} %get-tuple-element.72), calls=%async_computation.1 | async-start | bytes 393216 | tf_op jit(solution)/shard_map/all_to_all | solution.py:1168
  55.3 6.2 %convolution_convert_fusion = bf16[512,2048]{1,0:T(8,128)(2,1)} fusion(bf16[512,1024]{1,0:T(8,128)(2,1)} %bitcast.155, bf16[1024,2048]{1,0:T(8,128)(2,1)} %param.32), kind=kOutput, calls=%fused_computation.2 | convolution fusion | flops 2148532224 | bytes 7340032 | tf_op jit(solution)/shard_map/dot_general | solution.py:30
  61.5 2.7 all-to-all-done.1.got_ref
  64.9 4.5 %middle_part.1 = (bf16[96,1024]{1,0:T(8,128)(2,1)}, f32[96,1024]{1,0:T(8,128)}, bf16[96,1024]{1,0:T(8,128)(2,1)}, bf16[96,1024]{1,0:T(8,128)(2,1)}) custom-call(bf16[16,48,128]{2,1,0:T(8,128)(2,1)} %copy-done.12, bf16[96,1024]{1,0:T(8,128)(2,1)} %bitcast.152, f32[1,1024]{1,0:T(1,128)} %bitcast.190, f32[1,1024]{1,0:T(1,128)} %bitcast.192, ...), custom_call_target="tpu_custom_call" | custom-call | flops 402653184 | bytes 5242880 | tf_op jit(solution)/shard_map/middle_part/pallas_call | solution.py:495
  69.4 5.2 %cross_forward.1 = (bf16[2,48,1024]{2,1,0:T(8,128)(2,1)}, f32[2,4,256]{2,1,0:T(4,128)}, f32[96,1024]{1,0:T(8,128)}, bf16[96,1024]{1,0:T(8,128)(2,1)}) custom-call(s32[2]{0:T(128)} %count_ref.9, bf16[2,48,1024]{2,1,0:T(8,128)(2,1)} %bitcast.164, bf16[2,256,2048]{2,1,0:T(8,128)(2,1)} %bitcast.148, f32[96,1024]{1,0:T(8,128)} %get-tuple-element.77.mid_ref, ...), custom_call_target="tpu_custom_call" | custom-call | flops 402653184 | bytes 3145728 | tf_op jit(solution)/shard_map/cross_forward/pallas_call | solution.py:288
  74.6 11.5 %mlp.1 = (bf16[96,4096]{1,0:T(8,128)(2,1)}, bf16[96,4096]{1,0:T(8,128)(2,1)}, bf16[4,96,256]{2,1,0:T(8,128)(2,1)}, bf16[4,96,1024]{2,1,0:T(8,128)(2,1)}, f32[96,...) custom-call(bf16[96,1024]{1,0:T(8,128)(2,1)} %get-tuple-element.79.normed_ref, ...), custom_call_target="tpu_custom_call" | custom-call | flops 1610612736 | bytes 12582912 | tf_op jit(solution)/shard_map/mlp/pallas_call | solution.py:999
  86.2 2.0 dynamic-slice_bitcast_fusion.1
  88.6 1.5 collective-permute-start.11
  90.2 5.7 %collective-permute-done.10 = bf16[96,1024]{1,0:T(8,128)(2,1)S(1)} collective-permute-done((bf16[96,1024]{1,0:T(8,128)(2,1)S(1)}, bf16[96,1024]{1,0:T(8,128)(2,1)S(1)}, u32[]{:S(2)}, u32[]{:S(2)}) %collective-permute-start.10) | collective-permute-done | bytes 196640 | tf_op jit(solution)/shard_map/ppermute | solution.py:1117
  95.9 3.4 %collective-permute-done.11 = bf16[96,1024]{1,0:T(8,128)(2,1)S(1)} collective-permute-done((bf16[96,1024]{1,0:T(8,128)(2,1)S(1)}, bf16[96,1024]{1,0:T(8,128)(2,1)S(1)}, u32[]{:S(2)}, u32[]{:S(2)}) %collective-permute-start.11) | collective-permute-done | bytes 196640 | tf_op jit(solution)/shard_map/ppermute | solution.py:1171
  100.0 4.3 %product.4 = (bf16[4,1,128,1024]{3,2,1,0:T(8,128)(2,1)}, bf16[4,1,128,1024]{3,2,1,0:T(8,128)(2,1)}) custom-call(s32[1]{0:T(128)} %bitcast.23.half_ref, bf16[1,96,1024]{2,1,0:T(8,128)(2,1)} %get-tuple-element.131.refs_0_, bf16[1,96,1024]{2,1,0:T(8,128)(2,1)} %bitcast.197, bf16[1,96,1024]{2,1,0:T(8,128)(2,1)} %bitcast.198, bf16[1,96,1024]{2,1,0:T(8,128)(2,1)} %bitcast.199, ...), custom_call_target="tpu_custom_call" | custom-call | flops 805306368 | bytes 8388608 | tf_op jit(solution)/shard_map/product/pallas_call | solution.py:1095
  104.3 2.0 collective-permute-start.27
  107.0 5.4 %cross_backward.1 = bf16[2,48,1024]{2,1,0:T(8,128)(2,1)} custom-call(s32[2]{0:T(128)} %count_ref.9, bf16[2,48,1024]{2,1,0:T(8,128)(2,1)} %bitcast.165, bf16[2,256,2048]{2,1,0:T(8,128)(2,1)} %bitcast.149, bf16[2,48,1024]{2,1,0:T(8,128)(2,1)} %bitcast.181, f32[2,4,256]{2,1,0:T(4,128)} %get-tuple-element.82.lse_ref), custom_call_target="tpu_custom_call" | custom-call | flops 1006632960 | bytes 6291456 | tf_op jit(solution)/shard_map/cross_backward/pallas_call | solution.py:320
  112.4 5.6 %middle_back.1 = (f32[96,1024]{1,0:T(8,128)}, bf16[96,1024]{1,0:T(8,128)(2,1)}, bf16[16,3,48,128]{3,2,1,0:T(8,128)(2,1)}, f32[2,1024]{1,0:T(2,128)}) custom-call(bf16[96,1024]{1,0:T(8,128)(2,1)} %bitcast.166, f32[96,1024]{1,0:T(8,128)} %get-tuple-element.77.mid_ref, f32[1,1024]{1,0:T(1,128)} %bitcast.191, f32[96,1024]{1,0:T(8,128)} %get-tuple-element.83.later_ref, ...), custom_call_target="tpu_custom_call" | custom-call | flops 402653184 | bytes 6291456 | tf_op jit(solution)/shard_map/middle_back/pallas_call | solution.py:561
  118.1 3.8 %all-to-all-start.2 = ((bf16[16,3,48,128]{3,2,1,0:T(8,128)(2,1)}), bf16[16,3,48,128]{3,2,1,0:T(8,128)(2,1)S(1)}, u32[]{:S(2)}, u32[]{:S(2)}) async-start(bf16[16,3,48,128]{3,2,1,0:T(8,128)(2,1)} %get-tuple-element.84), calls=%async_computation.2 | async-start | bytes 1179648 | tf_op jit(solution)/shard_map/all_to_all | solution.py:1168
  124.1 1.6 collective-permute-start.4
  126.6 7.5 %collective-permute-done.27 = bf16[4,1,128,1024]{3,2,1,0:T(8,128)(2,1)S(1)} collective-permute-done((bf16[4,1,128,1024]{3,2,1,0:T(8,128)(2,1)}, bf16[4,1,128,1024]{3,2,1,0:T(8,128)(2,1)S(1)}, u32[]{:S(2)}, u32[]{:S(2)}) %collective-permute-start.27) | collective-permute-done | bytes 1048608 | tf_op jit(solution)/shard_map/ppermute | solution.py:1113
  134.1 1.4 collective-permute-start.5
  137.3 1.0 collective-permute-done.4
  139.5 7.4 %product.3 = (bf16[4,1,32,4096]{3,2,1,0:T(8,128)(2,1)}, bf16[4,1,32,4096]{3,2,1,0:T(8,128)(2,1)}) custom-call(s32[1]{0:T(128)} %bitcast.12.half_ref, bf16[1,96,256]{2,1,0:T(8,128)(2,1)} %get-tuple-element.142.refs_0_, bf16[1,96,256]{2,1,0:T(8,128)(2,1)} %bitcast.185, bf16[1,96,256]{2,1,0:T(8,128)(2,1)} %bitcast.186, bf16[1,96,256]{2,1,0:T(8,128)(2,1)} %bitcast.187, ...), custom_call_target="tpu_custom_call" | custom-call | flops 805306368 | bytes 8388608 | tf_op jit(solution)/shard_map/product/pallas_call | solution.py:1095
  146.9 1.4 collective-permute-start.24
  148.3 6.5 %self_backward.1 = (bf16[16,1,48,128]{3,2,1,0:T(8,128)(2,1)}, bf16[16,2,48,128]{3,2,1,0:T(8,128)(2,1)}) custom-call(s32[2]{0:T(128)} %count_ref.8, bf16[16,3,48,128]{3,2,1,0:T(8,128)(2,1)} %copy-done.15, bf16[16,3,48,128]{3,2,1,0:T(8,128)(2,1)} %copy-done.15, bf16[16,3,48,128]{3,2,1,0:T(8,128)(2,1)} %copy-done.15, bf16[16,3,48,128]{3,2,1,0:T(8,128)(2,1)} %copy-done.2, ...), custom_call_target="tpu_custom_call" | custom-call | flops 1509949440 | bytes 2097152 | tf_op jit(solution)/shard_map/self_backward/pallas_call | solution.py:170
  154.9 4.2 %memory_back.1.dmem_ref = bf16[16,2,16,128]{3,2,1,0:T(8,128)(2,1)} custom-call(s32[1]{0:T(128)} %bitcast.9.head_ref, s32[2]{0:T(128)} %count_ref.9, bf16[16,3,48,128]{3,2,1,0:T(8,128)(2,1)} %copy-done.2, bf16[16,3,48,128]{3,2,1,0:T(8,128)(2,1)} %copy-done.2, bf16[2,256,2048]{2,1,0:T(8,128)(2,1)} %bitcast.150, bf16[2,256,2048]{2,1,0:T(8,128)(2,1)} %bitcast.151), custom_call_target="tpu_custom_call" | custom-call | flops 402653184 | bytes 2097152 | tf_op jit(solution)/shard_map/memory_back/pallas_call | solution.py:370
  159.1 1.9 pad_maximum_fusion
  161.0 5.4 %all-to-all-start.3 = ((bf16[16,176,128]{2,1,0:T(8,128)(2,1)}), bf16[16,176,128]{2,1,0:T(8,128)(2,1)S(1)}, u32[]{:S(2)}, u32[]{:S(2)}) async-start(bf16[16,176,128]{2,1,0:T(8,128)(2,1)} %pad_maximum_fusion), calls=%async_computation.3 | async-start | bytes 1441792 | tf_op jit(solution)/shard_map/all_to_all | solution.py:1168
  166.4 1.2 pad_maximum_fusion.1.refs_4_
  168.4 1.0 fusion.7
  169.4 2.9 collective-permute-start.29
  173.1 2.5 pieces.1
  175.6 1.8 dynamic-slice_bitcast_fusion.4
  177.9 19.3 %collective-permute-done.29 = bf16[1,1,128,1024]{3,2,1,0:T(8,128)(2,1)S(1)} collective-permute-done((bf16[1,1,128,1024]{3,2,1,0:T(8,128)(2,1)S(1)}, bf16[1,1,128,1024]{3,2,1,0:T(8,128)(2,1)S(1)}, u32[]{:S(2)}, u32[]{:S(2)}) %collective-permute-start.29) | collective-permute-done | bytes 262176 | tf_op jit(solution)/shard_map/ppermute | solution.py:1113
  197.9 1.9 add_bitcast_fusion
  200.0 1.2 collective-permute-start.20
  201.2 2.0 fusion.5
  203.2 1.2 add_convert_fusion.3
  204.4 1.4 collective-permute-done.17.refs_3_
  206.4 6.1 %product.5 = (bf16[4,3,32,1024]{3,2,1,0:T(8,128)(2,1)}, bf16[4,3,32,1024]{3,2,1,0:T(8,128)(2,1)}) custom-call(s32[1]{0:T(128)} %bitcast.23.half_ref, bf16[3,96,256]{2,1,0:T(8,128)(2,1)} %get-tuple-element.135.refs_0_, bf16[3,96,256]{2,1,0:T(8,128)(2,1)} %copy-done.17, bf16[3,96,256]{2,1,0:T(8,128)(2,1)} %copy-done.18, bf16[3,96,256]{2,1,0:T(8,128)(2,1)} %copy-done.19, ...), custom_call_target="tpu_custom_call" | custom-call | flops 603979776 | bytes 8388608 | tf_op jit(solution)/shard_map/product/pallas_call | solution.py:1095
  212.5 1.5 collective-permute-start.21
  214.9 6.5 %first_back.1 = f32[2,48,1024]{2,1,0:T(8,128)} custom-call(bf16[16,176,128]{2,1,0:T(8,128)(2,1)} %copy-done.3, bf16[1024,3072]{1,0:T(8,128)(2,1)} %v_ref.5, bf16[1024,3072]{1,0:T(8,128)(2,1)} %v_ref.5, bf16[1024,3072]{1,0:T(8,128)(2,1)} %v_ref.5, bf16[2,48,1024]{2,1,0:T(8,128)(2,1)} %tri_ref.3, f32[2,2048]{1,0:T(2,128)} %fusion.3.mod_ref, ...), custom_call_target="tpu_custom_call" | custom-call | flops 603979776 | bytes 8388608 | tf_op jit(solution)/shard_map/first_back/pallas_call | solution.py:636
  221.3 4.3 %fusion = f32[2,16,1024]{2,1,0:T(8,128)} fusion(bf16[2,16,2048]{2,1,0:T(8,128)(2,1)S(1)} %dot_general.31, bf16[1024,2048]{1,0:T(8,128)(2,1)} %param.32), kind=kOutput, calls=%fused_computation | convolution fusion | flops 134217728 | bytes 4456448 | tf_op jit(solution)/shard_map/dot_general | solution.py:34
  225.6 1.7 fusion.9
  228.0 4.2 %collective-permute-done.21 = bf16[4,3,32,1024]{3,2,1,0:T(8,128)(2,1)S(1)} collective-permute-done((bf16[4,3,32,1024]{3,2,1,0:T(8,128)(2,1)}, bf16[4,3,32,1024]{3,2,1,0:T(8,128)(2,1)S(1)}, u32[]{:S(2)}, u32[]{:S(2)}) %collective-permute-start.21) | collective-permute-done | bytes 786464 | tf_op jit(solution)/shard_map/ppermute | solution.py:1113
  232.2 1.1 add_convert_fusion.5
  233.6 6.8 %head_back.1 = (bf16[32,96,128]{2,1,0:T(8,128)(2,1)}, bf16[32,128]{1,0:T(8,128)(2,1)}) custom-call(s32[1]{0:T(128)} %bitcast.9.head_ref, bf16[16,1,48,128]{3,2,1,0:T(8,128)(2,1)} %get-tuple-element.96.dq_ref, bf16[16,2,48,128]{3,2,1,0:T(8,128)(2,1)} %get-tuple-element.97.dkv_ref, bf16[16,2,16,128]{3,2,1,0:T(8,128)(2,1)} %memory_back.1.dmem_ref, ...), custom_call_target="tpu_custom_call" | custom-call | flops 603979776 | bytes 5242880 | tf_op jit(solution)/shard_map/head_back/pallas_call | solution.py:761
  240.5 1.1 dynamic-slice_bitcast_fusion
  242.4 1.9 add_bitcast_fusion.1
  244.3 4.7 %collective-permute-done.22 = bf16[2,3,32,1024]{3,2,1,0:T(8,128)(2,1)S(1)} collective-permute-done((bf16[2,3,32,1024]{3,2,1,0:T(8,128)(2,1)}, bf16[2,3,32,1024]{3,2,1,0:T(8,128)(2,1)S(1)}, u32[]{:S(2)}, u32[]{:S(2)}) %collective-permute-start.22) | collective-permute-done | bytes 393248 | tf_op jit(solution)/shard_map/ppermute | solution.py:1113
  249.2 2.2 collective-permute-done.13
  251.4 1.1 fusion.4
  254.1 4.1 %all-to-all-start.4 = ((bf16[16,128,128]{2,1,0:T(8,128)(2,1)}), bf16[16,128,128]{2,1,0:T(8,128)(2,1)S(1)}, u32[]{:S(2)}, u32[]{:S(2)}) async-start(bf16[16,128,128]{2,1,0:T(8,128)(2,1)} %pad_maximum_fusion.2), calls=%async_computation.4 | async-start | bytes 1048576 | tf_op jit(solution)/shard_map/all_to_all | solution.py:1168
  258.1 1.2 collective-permute-done.23
  260.1 5.6 %convolution_add_fusion = f32[96,1024]{1,0:T(8,128)} fusion(f32[96,1024]{1,0:T(8,128)S(1)} %copy-done.7, bf16[96,4096]{1,0:T(8,128)(2,1)S(1)} %copy-done.4, bf16[4096,1024]{1,0:T(8,128)(2,1)} %param.37), kind=kOutput, calls=%fused_computation.3 | convolution fusion | flops 805404672 | bytes 9961472 | tf_op jit(solution)/shard_map/dot_general | solution.py:30
  265.8 6.8 %all-to-all-done.4.got_ref = bf16[16,128,128]{2,1,0:T(8,128)(2,1)S(1)} async-done(((bf16[16,128,128]{2,1,0:T(8,128)(2,1)}), bf16[16,128,128]{2,1,0:T(8,128)(2,1)S(1)}, u32[]{:S(2)}, u32[]{:S(2)}) %all-to-all-start.4) | async-done | bytes 524320 | tf_op jit(solution)/shard_map/all_to_all | solution.py:1168
  273.4 2.1 unpack.1
  277.3 2.1 collective-permute-done.14
  280.2 3.4 %fusion.14 = f32[4,1024]{1,0:T(4,128)S(1)} fusion(bf16[1024,2048]{1,0:T(8,128)(2,1)} %param.26, f32[4,2048]{1,0:T(4,128)S(1)} %select_n.125), kind=kOutput, calls=%fused_computation.57 | convolution fusion | flops 16785408 | bytes 4243456 | tf_op jit(solution)/shard_map/dot_general | solution.py:34
  (148 shorter events, 25.9 us)
Async XLA Ops:
  7.2 1.5 copy-start
  7.2 48.1 %all-gather.3.cloned.1.call-start = ((), (), s32[]{:S(2)}) async-start(), calls=%async_computation.5 | async-start | bytes 1114112 | tf_op jit(solution)/shard_map/all_gather | solution.py:1239
  12.3 13.1 %copy-start.14 = (bf16[2,48,1024]{2,1,0:T(8,128)(2,1)S(1)}, bf16[2,48,1024]{2,1,0:T(8,128)(2,1)}, u32[]{:S(2)}) copy-start(bf16[2,48,1024]{2,1,0:T(8,128)(2,1)} %param.21) | copy-start | bytes 589828
  17.9 23.5 %all-to-all-start = ((bf16[16,3,48,128]{3,2,1,0:T(8,128)(2,1)}), bf16[16,3,48,128]{3,2,1,0:T(8,128)(2,1)S(1)}, u32[]{:S(2)}, u32[]{:S(2)}) async-start(bf16[16,3,48,128]{3,2,1,0:T(8,128)(2,1)} %project.1), calls=%async_computation | async-start | bytes 1179648 | tf_op jit(solution)/shard_map/all_to_all | solution.py:1168
  25.3 208.3 %all-gather.5.cloned.1.call-start = ((), (), s32[]{:S(2)}) async-start(), calls=%async_computation.6 | async-start | bytes 3342336 | tf_op jit(solution)/shard_map/all_gather | solution.py:1260
  25.4 21.3 %copy-start.26 = (s32[2,4]{1,0:T(2,128)S(1)}, s32[2,4]{1,0:T(2,128)}, u32[]{:S(2)}) copy-start(s32[2,4]{1,0:T(2,128)} %param.22) | copy-start | bytes 100
  25.4 23.4 %collective-permute-start.1 = (bf16[96,1024]{1,0:T(8,128)(2,1)S(1)}, bf16[96,1024]{1,0:T(8,128)(2,1)S(1)}, u32[]{:S(2)}, u32[]{:S(2)}) collective-permute-start(bf16[96,1024]{1,0:T(8,128)(2,1)S(1)} %bitcast.175), channel_id=1, source_target_pairs={{0,16},{16,0},{1,17},{17,1},{2,18},{18,2},{3,19},{19,3},{4,20},{20... | collective-permute-start | bytes 589832 | tf_op jit(solution)/shard_map/ppermute | solution.py:1117
  46.5 15.0 %collective-permute-start = (bf16[96,1024]{1,0:T(8,128)(2,1)S(1)}, bf16[96,1024]{1,0:T(8,128)(2,1)S(1)}, u32[]{:S(2)}, u32[]{:S(2)}) collective-permute-start(bf16[96,1024]{1,0:T(8,128)(2,1)S(1)} %bitcast.177), channel_id=1, source_target_pairs={{0,1},{1,0},{2,3},{3,2},{4,5},{5,4},{6,7},{7,6},{8,9},{9,8},{10,11... | collective-permute-start | bytes 589832 | tf_op jit(solution)/shard_map/ppermute | solution.py:1113
  46.6 43.4 %collective-permute-start.12 = (s32[2,4]{1,0:T(2,128)S(1)}, s32[2,4]{1,0:T(2,128)S(1)}, u32[]{:S(2)}, u32[]{:S(2)}) collective-permute-start(s32[2,4]{1,0:T(2,128)S(1)} %copy-done.26), channel_id=1, source_target_pairs={{0,16},{16,0},{1,17},{17,1},{2,18},{18,2},{3,19},{19,3},{4,20},{20... | collective-permute-start | bytes 104 | tf_op jit(solution)/shard_map/ppermute | solution.py:1117
  48.8 12.7 %copy-start.28 = (bf16[96,1024]{1,0:T(8,128)(2,1)}, bf16[96,1024]{1,0:T(8,128)(2,1)S(1)}, u32[]{:S(2)}) copy-start(bf16[96,1024]{1,0:T(8,128)(2,1)S(1)} %collective-permute-done.1) | copy-start | bytes 589828
  48.8 12.7 %collective-permute-start.2 = (bf16[96,1024]{1,0:T(8,128)(2,1)S(1)}, bf16[96,1024]{1,0:T(8,128)(2,1)S(1)}, u32[]{:S(2)}, u32[]{:S(2)}) collective-permute-start(bf16[96,1024]{1,0:T(8,128)(2,1)S(1)} %collective-permute-done.1), channel_id=1, source_target_pairs={{0,1},{1,0},{2,3},{3,2},{4,5},{5,4},{6,7},{7,6},{8,9},{9,8},{10,11... | collective-permute-start | bytes 589832 | tf_op jit(solution)/shard_map/ppermute | solution.py:1113
  48.9 15.3 %all-to-all-start.1 = ((bf16[16,48,128]{2,1,0:T(8,128)(2,1)}), bf16[16,48,128]{2,1,0:T(8,128)(2,1)S(1)}, u32[]{:S(2)}, u32[]{:S(2)}) async-start(bf16[16,48,128]{2,1,0:T(8,128)(2,1)} %get-tuple-element.72), calls=%async_computation.1 | async-start | bytes 393216 | tf_op jit(solution)/shard_map/all_to_all | solution.py:1168
  61.5 37.8 %copy-start.29 = (bf16[96,1024]{1,0:T(8,128)(2,1)}, bf16[96,1024]{1,0:T(8,128)(2,1)S(1)}, u32[]{:S(2)}) copy-start(bf16[96,1024]{1,0:T(8,128)(2,1)S(1)} %collective-permute-done) | copy-start | bytes 589828
  61.5 37.8 %copy-start.30 = (bf16[96,1024]{1,0:T(8,128)(2,1)}, bf16[96,1024]{1,0:T(8,128)(2,1)S(1)}, u32[]{:S(2)}) copy-start(bf16[96,1024]{1,0:T(8,128)(2,1)S(1)} %collective-permute-done.2) | copy-start | bytes 589828
  86.1 36.1 %collective-permute-start.7 = (bf16[96,4096]{1,0:T(8,128)(2,1)}, bf16[96,4096]{1,0:T(8,128)(2,1)}, u32[]{:S(2)}, u32[]{:S(2)}) collective-permute-start(bf16[96,4096]{1,0:T(8,128)(2,1)} %get-tuple-element.86), channel_id=1, source_target_pairs={{0,2},{1,3},{2,0},{3,1},{4,6},{5,7},{6,4},{7,5},{8,10},{9,11},{10,... | collective-permute-start | bytes 2359304 | tf_op jit(solution)/shard_map/ppermute | solution.py:1113
  88.2 2.0 collective-permute-start.9
  88.2 7.7 %collective-permute-start.10 = (bf16[96,1024]{1,0:T(8,128)(2,1)S(1)}, bf16[96,1024]{1,0:T(8,128)(2,1)S(1)}, u32[]{:S(2)}, u32[]{:S(2)}) collective-permute-start(bf16[96,1024]{1,0:T(8,128)(2,1)S(1)} %get-tuple-element.129), channel_id=1, source_target_pairs={{0,16},{16,0},{1,17},{17,1},{2,18},{18,2},{3,19},{19,3},{4,20},{20... | collective-permute-start | bytes 589832 | tf_op jit(solution)/shard_map/ppermute | solution.py:1117
  88.6 10.7 %collective-permute-start.11 = (bf16[96,1024]{1,0:T(8,128)(2,1)S(1)}, bf16[96,1024]{1,0:T(8,128)(2,1)S(1)}, u32[]{:S(2)}, u32[]{:S(2)}) collective-permute-start(bf16[96,1024]{1,0:T(8,128)(2,1)S(1)} %get-tuple-element.128), channel_id=1, source_target_pairs={{0,17},{1,16},{2,19},{3,18},{4,21},{5,20},{6,23},{7,22},{8,25},{9,... | collective-permute-start | bytes 589832 | tf_op jit(solution)/shard_map/ppermute | solution.py:1171
  90.2 9.2 %copy-start.31 = (bf16[96,1024]{1,0:T(8,128)(2,1)}, bf16[96,1024]{1,0:T(8,128)(2,1)S(1)}, u32[]{:S(2)}) copy-start(bf16[96,1024]{1,0:T(8,128)(2,1)S(1)} %collective-permute-done.9) | copy-start | bytes 589828
  95.9 3.5 %copy-start.32 = (bf16[96,1024]{1,0:T(8,128)(2,1)}, bf16[96,1024]{1,0:T(8,128)(2,1)S(1)}, u32[]{:S(2)}) copy-start(bf16[96,1024]{1,0:T(8,128)(2,1)S(1)} %collective-permute-done.10) | copy-start | bytes 589828
  104.3 29.8 %collective-permute-start.27 = (bf16[4,1,128,1024]{3,2,1,0:T(8,128)(2,1)}, bf16[4,1,128,1024]{3,2,1,0:T(8,128)(2,1)S(1)}, u32[]{:S(2)}, u32[]{:S(2)}) collective-permute-start(bf16[4,1,128,1024]{3,2,1,0:T(8,128)(2,1)} %get-tuple-element.125), channel_id=1, source_target_pairs={{0,2},{1,3},{2,0},{3,1},{4,6},{5,7},{6,4},{7,5},{8,10},{9,11},{10,... | collective-permute-start | bytes 3145736 | tf_op jit(solution)/shard_map/ppermute | solution.py:1113
  112.4 10.8 %copy-start.16 = (bf16[4,96,256]{2,1,0:T(8,128)(2,1)S(1)}, bf16[4,96,256]{2,1,0:T(8,128)(2,1)}, u32[]{:S(2)}) copy-start(bf16[4,96,256]{2,1,0:T(8,128)(2,1)} %get-tuple-element.85) | copy-start | bytes 589828
  112.4 13.2 %copy-start.25 = (f32[2,1024]{1,0:T(2,128)S(1)}, f32[2,1024]{1,0:T(2,128)}, u32[]{:S(2)}) copy-start(f32[2,1024]{1,0:T(2,128)} %get-tuple-element.100) | copy-start | bytes 24580
  112.4 23.1 %copy-start.10 = (bf16[4,1,128,1024]{3,2,1,0:T(8,128)(2,1)S(1)}, bf16[4,1,128,1024]{3,2,1,0:T(8,128)(2,1)}, u32[]{:S(2)}) copy-start(bf16[4,1,128,1024]{3,2,1,0:T(8,128)(2,1)} %get-tuple-element.93) | copy-start | bytes 3145732
  118.1 28.8 %all-to-all-start.2 = ((bf16[16,3,48,128]{3,2,1,0:T(8,128)(2,1)}), bf16[16,3,48,128]{3,2,1,0:T(8,128)(2,1)S(1)}, u32[]{:S(2)}, u32[]{:S(2)}) async-start(bf16[16,3,48,128]{3,2,1,0:T(8,128)(2,1)} %get-tuple-element.84), calls=%async_computation.2 | async-start | bytes 1179648 | tf_op jit(solution)/shard_map/all_to_all | solution.py:1168
  122.1 16.8 %collective-permute-start.6 = (bf16[96,4096]{1,0:T(8,128)(2,1)}, bf16[96,4096]{1,0:T(8,128)(2,1)}, u32[]{:S(2)}, u32[]{:S(2)}) collective-permute-start(bf16[96,4096]{1,0:T(8,128)(2,1)} %get-tuple-element.86), channel_id=1, source_target_pairs={{0,1},{1,0},{2,3},{3,2},{4,5},{5,4},{6,7},{7,6},{8,9},{9,8},{10,11... | collective-permute-start | bytes 2359304 | tf_op jit(solution)/shard_map/ppermute | solution.py:1113
  122.3 16.7 %collective-permute-start.8 = (bf16[96,4096]{1,0:T(8,128)(2,1)}, bf16[96,4096]{1,0:T(8,128)(2,1)}, u32[]{:S(2)}, u32[]{:S(2)}) collective-permute-start(bf16[96,4096]{1,0:T(8,128)(2,1)} %collective-permute-done.7), channel_id=1, source_target_pairs={{0,1},{1,0},{2,3},{3,2},{4,5},{5,4},{6,7},{7,6},{8,9},{9,8},{10,11... | collective-permute-start | bytes 2359304 | tf_op jit(solution)/shard_map/ppermute | solution.py:1113
  123.9 12.6 %collective-permute-start.3 = (bf16[96,256]{1,0:T(8,128)(2,1)S(1)}, bf16[96,256]{1,0:T(8,128)(2,1)S(1)}, u32[]{:S(2)}, u32[]{:S(2)}) collective-permute-start(bf16[96,256]{1,0:T(8,128)(2,1)S(1)} %get-tuple-element.141), channel_id=1, source_target_pairs={{0,1},{1,0},{2,3},{3,2},{4,5},{5,4},{6,7},{7,6},{8,9},{9,8},{10,11... | collective-permute-start | bytes 147464 | tf_op jit(solution)/shard_map/ppermute | solution.py:1113
  124.1 14.3 %collective-permute-start.4 = (bf16[96,256]{1,0:T(8,128)(2,1)S(1)}, bf16[96,256]{1,0:T(8,128)(2,1)S(1)}, u32[]{:S(2)}, u32[]{:S(2)}) collective-permute-start(bf16[96,256]{1,0:T(8,128)(2,1)S(1)} %get-tuple-element.140), channel_id=1, source_target_pairs={{0,2},{1,3},{2,0},{3,1},{4,6},{5,7},{6,4},{7,5},{8,10},{9,11},{10,... | collective-permute-start | bytes 147464 | tf_op jit(solution)/shard_map/ppermute | solution.py:1113
  134.1 4.8 %collective-permute-start.5 = (bf16[96,256]{1,0:T(8,128)(2,1)S(1)}, bf16[96,256]{1,0:T(8,128)(2,1)S(1)}, u32[]{:S(2)}, u32[]{:S(2)}) collective-permute-start(bf16[96,256]{1,0:T(8,128)(2,1)S(1)} %get-tuple-element.139), channel_id=1, source_target_pairs={{0,3},{1,2},{2,1},{3,0},{4,7},{5,6},{6,5},{7,4},{8,11},{9,10},{10,... | collective-permute-start | bytes 147464 | tf_op jit(solution)/shard_map/ppermute | solution.py:1113
  136.5 2.4 copy-start.20
  136.5 31.9 %collective-permute-start.28 = (bf16[2,1,128,1024]{3,2,1,0:T(8,128)(2,1)}, bf16[2,1,128,1024]{3,2,1,0:T(8,128)(2,1)}, u32[]{:S(2)}, u32[]{:S(2)}) collective-permute-start(bf16[2,1,128,1024]{3,2,1,0:T(8,128)(2,1)} %fusion.6), channel_id=1, source_target_pairs={{0,4},{1,5},{2,6},{3,7},{4,0},{5,1},{6,2},{7,3},{8,12},{9,13},{10,... | collective-permute-start | bytes 1572872 | tf_op jit(solution)/shard_map/ppermute | solution.py:1113
  146.9 1.5 copy-start.2
  146.9 53.1 %collective-permute-start.24 = (bf16[4,1,32,4096]{3,2,1,0:T(8,128)(2,1)}, bf16[4,1,32,4096]{3,2,1,0:T(8,128)(2,1)}, u32[]{:S(2)}, u32[]{:S(2)}) collective-permute-start(bf16[4,1,32,4096]{3,2,1,0:T(8,128)(2,1)} %get-tuple-element.124), channel_id=1, source_target_pairs={{0,16},{16,0},{1,17},{17,1},{2,18},{18,2},{3,19},{19,3},{4,20},{20... | collective-permute-start | bytes 3145736 | tf_op jit(solution)/shard_map/ppermute | solution.py:1117
  154.8 4.2 %copy-start.8 = (bf16[16,2,48,128]{3,2,1,0:T(8,128)(2,1)S(1)}, bf16[16,2,48,128]{3,2,1,0:T(8,128)(2,1)}, u32[]{:S(2)}) copy-start(bf16[16,2,48,128]{3,2,1,0:T(8,128)(2,1)} %get-tuple-element.97.dkv_ref) | copy-start | bytes 1179652
  154.8 4.2 %copy-start.11 = (bf16[16,1,48,128]{3,2,1,0:T(8,128)(2,1)S(1)}, bf16[16,1,48,128]{3,2,1,0:T(8,128)(2,1)}, u32[]{:S(2)}) copy-start(bf16[16,1,48,128]{3,2,1,0:T(8,128)(2,1)} %get-tuple-element.96.dq_ref) | copy-start | bytes 589828
  154.9 17.5 %copy-start.27 = (bf16[16]{0:T(256)(128)(2,1)S(1)}, bf16[16]{0:T(256)(128)(2,1)}, u32[]{:S(2)}) copy-start(bf16[16]{0:T(256)(128)(2,1)} %pad.18.clone) | copy-start | bytes 100
  159.1 42.1 %copy-start.9 = (bf16[4,1,32,4096]{3,2,1,0:T(8,128)(2,1)S(1)}, bf16[4,1,32,4096]{3,2,1,0:T(8,128)(2,1)}, u32[]{:S(2)}) copy-start(bf16[4,1,32,4096]{3,2,1,0:T(8,128)(2,1)} %get-tuple-element.87) | copy-start | bytes 3145732
  161.0 53.0 %all-to-all-start.3 = ((bf16[16,176,128]{2,1,0:T(8,128)(2,1)}), bf16[16,176,128]{2,1,0:T(8,128)(2,1)S(1)}, u32[]{:S(2)}, u32[]{:S(2)}) async-start(bf16[16,176,128]{2,1,0:T(8,128)(2,1)} %pad_maximum_fusion), calls=%async_computation.3 | async-start | bytes 1441792 | tf_op jit(solution)/shard_map/all_to_all | solution.py:1168
  167.6 38.2 %copy-start.5 = (bf16[3,96,1024]{2,1,0:T(8,128)(2,1)}, bf16[3,96,1024]{2,1,0:T(8,128)(2,1)S(1)}, u32[]{:S(2)}) copy-start(bf16[3,96,1024]{2,1,0:T(8,128)(2,1)S(1)} %pad_maximum_fusion.1.refs_4_) | copy-start | bytes 1769476
  167.6 32.1 %collective-permute-start.19 = (bf16[3,96,1024]{2,1,0:T(8,128)(2,1)S(1)}, bf16[3,96,1024]{2,1,0:T(8,128)(2,1)}, u32[]{:S(2)}, u32[]{:S(2)}) collective-permute-start(bf16[3,96,1024]{2,1,0:T(8,128)(2,1)S(1)} %pad_maximum_fusion.1.refs_4_), channel_id=1, source_target_pairs={{0,16},{16,0},{1,17},{17,1},{2,18},{18,2},{3,19},{19,3},{4,20},{20... | collective-permute-start | bytes 1769480 | tf_op jit(solution)/shard_map/ppermute | solution.py:1117
  169.4 27.8 %collective-permute-start.29 = (bf16[1,1,128,1024]{3,2,1,0:T(8,128)(2,1)S(1)}, bf16[1,1,128,1024]{3,2,1,0:T(8,128)(2,1)S(1)}, u32[]{:S(2)}, u32[]{:S(2)}) collective-permute-start(bf16[1,1,128,1024]{3,2,1,0:T(8,128)(2,1)S(1)} %fusion.7), channel_id=1, source_target_pairs={{0,8},{1,9},{2,10},{3,11},{4,12},{5,13},{6,14},{7,15},{8,0},{9,1},... | collective-permute-start | bytes 786440 | tf_op jit(solution)/shard_map/ppermute | solution.py:1113
  173.1 32.7 %collective-permute-start.18 = (bf16[3,96,1024]{2,1,0:T(8,128)(2,1)S(1)}, bf16[3,96,1024]{2,1,0:T(8,128)(2,1)}, u32[]{:S(2)}, u32[]{:S(2)}) collective-permute-start(bf16[3,96,1024]{2,1,0:T(8,128)(2,1)S(1)} %pad_maximum_fusion.1.refs_4_), channel_id=1, source_target_pairs={{0,1},{1,0},{2,3},{3,2},{4,5},{5,4},{6,7},{7,6},{8,9},{9,8},{10,11... | collective-permute-start | bytes 1769480 | tf_op jit(solution)/shard_map/ppermute | solution.py:1113
  177.4 25.8 %collective-permute-start.15 = (bf16[3,96,256]{2,1,0:T(8,128)(2,1)S(1)}, bf16[3,96,256]{2,1,0:T(8,128)(2,1)S(1)}, u32[]{:S(2)}, u32[]{:S(2)}) collective-permute-start(bf16[3,96,256]{2,1,0:T(8,128)(2,1)S(1)} %get-tuple-element.134), channel_id=1, source_target_pairs={{0,1},{1,0},{2,3},{3,2},{4,5},{5,4},{6,7},{7,6},{8,9},{9,8},{10,11... | collective-permute-start | bytes 442376 | tf_op jit(solution)/shard_map/ppermute | solution.py:1113
  197.2 7.2 %collective-permute-start.16 = (bf16[3,96,256]{2,1,0:T(8,128)(2,1)S(1)}, bf16[3,96,256]{2,1,0:T(8,128)(2,1)S(1)}, u32[]{:S(2)}, u32[]{:S(2)}) collective-permute-start(bf16[3,96,256]{2,1,0:T(8,128)(2,1)S(1)} %get-tuple-element.133), channel_id=1, source_target_pairs={{0,16},{16,0},{1,17},{17,1},{2,18},{18,2},{3,19},{19,3},{4,20},{20... | collective-permute-start | bytes 442376 | tf_op jit(solution)/shard_map/ppermute | solution.py:1117
  199.8 6.0 %collective-permute-start.17 = (bf16[3,96,256]{2,1,0:T(8,128)(2,1)S(1)}, bf16[3,96,256]{2,1,0:T(8,128)(2,1)S(1)}, u32[]{:S(2)}, u32[]{:S(2)}) collective-permute-start(bf16[3,96,256]{2,1,0:T(8,128)(2,1)S(1)} %get-tuple-element.132), channel_id=1, source_target_pairs={{0,17},{1,16},{2,19},{3,18},{4,21},{5,20},{6,23},{7,22},{8,25},{9,... | collective-permute-start | bytes 442376 | tf_op jit(solution)/shard_map/ppermute | solution.py:1171
  200.0 5.7 %collective-permute-start.20 = (bf16[3,96,1024]{2,1,0:T(8,128)(2,1)}, bf16[3,96,1024]{2,1,0:T(8,128)(2,1)}, u32[]{:S(2)}, u32[]{:S(2)}) collective-permute-start(bf16[3,96,1024]{2,1,0:T(8,128)(2,1)} %collective-permute-done.19.refs_6_), channel_id=1, source_target_pairs={{0,1},{1,0},{2,3},{3,2},{4,5},{5,4},{6,7},{7,6},{8,9},{9,8},{10,11... | collective-permute-start | bytes 1769480 | tf_op jit(solution)/shard_map/ppermute | solution.py:1113
  203.2 2.6 copy-start.17
  203.2 22.5 %collective-permute-start.25 = (bf16[2,1,32,4096]{3,2,1,0:T(8,128)(2,1)}, bf16[2,1,32,4096]{3,2,1,0:T(8,128)(2,1)}, u32[]{:S(2)}, u32[]{:S(2)}) collective-permute-start(bf16[2,1,32,4096]{3,2,1,0:T(8,128)(2,1)} %fusion.5), channel_id=1, source_target_pairs={{0,4},{1,5},{2,6},{3,7},{4,0},{5,1},{6,2},{7,3},{8,12},{9,13},{10,... | collective-permute-start | bytes 1572872 | tf_op jit(solution)/shard_map/ppermute | solution.py:1113
  204.4 1.4 copy-start.18
  212.5 19.7 %collective-permute-start.21 = (bf16[4,3,32,1024]{3,2,1,0:T(8,128)(2,1)}, bf16[4,3,32,1024]{3,2,1,0:T(8,128)(2,1)S(1)}, u32[]{:S(2)}, u32[]{:S(2)}) collective-permute-start(bf16[4,3,32,1024]{3,2,1,0:T(8,128)(2,1)} %get-tuple-element.121), channel_id=1, source_target_pairs={{0,2},{1,3},{2,0},{3,1},{4,6},{5,7},{6,4},{7,5},{8,10},{9,11},{10,... | collective-permute-start | bytes 2359304 | tf_op jit(solution)/shard_map/ppermute | solution.py:1113
  214.0 0.9 copy-start.3
  221.3 10.8 %copy-start.13 = (bf16[4,3,32,1024]{3,2,1,0:T(8,128)(2,1)S(1)}, bf16[4,3,32,1024]{3,2,1,0:T(8,128)(2,1)}, u32[]{:S(2)}) copy-start(bf16[4,3,32,1024]{3,2,1,0:T(8,128)(2,1)} %get-tuple-element.120) | copy-start | bytes 2359300
  227.3 15.1 %collective-permute-start.26 = (bf16[1,1,32,4096]{3,2,1,0:T(8,128)(2,1)}, bf16[1,1,32,4096]{3,2,1,0:T(8,128)(2,1)}, u32[]{:S(2)}, u32[]{:S(2)}) collective-permute-start(bf16[1,1,32,4096]{3,2,1,0:T(8,128)(2,1)} %fusion.9), channel_id=1, source_target_pairs={{0,8},{1,9},{2,10},{3,11},{4,12},{5,13},{6,14},{7,15},{8,0},{9,1},... | collective-permute-start | bytes 786440 | tf_op jit(solution)/shard_map/ppermute | solution.py:1113
  233.2 15.8 %collective-permute-start.22 = (bf16[2,3,32,1024]{3,2,1,0:T(8,128)(2,1)}, bf16[2,3,32,1024]{3,2,1,0:T(8,128)(2,1)S(1)}, u32[]{:S(2)}, u32[]{:S(2)}) collective-permute-start(bf16[2,3,32,1024]{3,2,1,0:T(8,128)(2,1)} %get-tuple-element.127), channel_id=1, source_target_pairs={{0,4},{1,5},{2,6},{3,7},{4,0},{5,1},{6,2},{7,3},{8,12},{9,13},{10,... | collective-permute-start | bytes 1179656 | tf_op jit(solution)/shard_map/ppermute | solution.py:1113
  240.5 19.6 %copy-start.4 = (bf16[96,4096]{1,0:T(8,128)(2,1)S(1)}, bf16[96,4096]{1,0:T(8,128)(2,1)}, u32[]{:S(2)}) copy-start(bf16[96,4096]{1,0:T(8,128)(2,1)} %get-tuple-element.104) | copy-start | bytes 2359300
  240.5 19.6 %copy-start.7 = (f32[96,1024]{1,0:T(8,128)S(1)}, f32[96,1024]{1,0:T(8,128)}, u32[]{:S(2)}) copy-start(f32[96,1024]{1,0:T(8,128)} %get-tuple-element.103.later_ref) | copy-start | bytes 1179652
  241.6 9.8 %collective-permute-start.13 = (bf16[16,96,128]{2,1,0:T(8,128)(2,1)S(1)}, bf16[16,96,128]{2,1,0:T(8,128)(2,1)S(1)}, u32[]{:S(2)}, u32[]{:S(2)}) collective-permute-start(bf16[16,96,128]{2,1,0:T(8,128)(2,1)S(1)} %dynamic-slice_bitcast_fusion), channel_id=1, source_target_pairs={{0,16},{16,0},{1,17},{17,1},{2,18},{18,2},{3,19},{19,3},{4,20},{20... | collective-permute-start | bytes 1179656 | tf_op jit(solution)/shard_map/ppermute | solution.py:1117
  249.1 10.2 %collective-permute-start.23 = (bf16[1,3,32,1024]{3,2,1,0:T(8,128)(2,1)S(1)}, bf16[1,3,32,1024]{3,2,1,0:T(8,128)(2,1)S(1)}, u32[]{:S(2)}, u32[]{:S(2)}) collective-permute-start(bf16[1,3,32,1024]{3,2,1,0:T(8,128)(2,1)S(1)} %fusion.12), channel_id=1, source_target_pairs={{0,8},{1,9},{2,10},{3,11},{4,12},{5,13},{6,14},{7,15},{8,0},{9,1},... | collective-permute-start | bytes 589832 | tf_op jit(solution)/shard_map/ppermute | solution.py:1113
  254.1 18.5 %all-to-all-start.4 = ((bf16[16,128,128]{2,1,0:T(8,128)(2,1)}), bf16[16,128,128]{2,1,0:T(8,128)(2,1)S(1)}, u32[]{:S(2)}, u32[]{:S(2)}) async-start(bf16[16,128,128]{2,1,0:T(8,128)(2,1)} %pad_maximum_fusion.2), calls=%async_computation.4 | async-start | bytes 1048576 | tf_op jit(solution)/shard_map/all_to_all | solution.py:1168
  260.1 25.1 %copy-start.1 = (bf16[256,1024]{1,0:T(8,128)(2,1)S(1)}, bf16[256,1024]{1,0:T(8,128)(2,1)}, u32[]{:S(2)}) copy-start(bf16[256,1024]{1,0:T(8,128)(2,1)} %param.25) | copy-start | bytes 1572868
  265.8 17.9 %copy-start.24 = (f32[4,8]{1,0:T(4,128)S(1)}, f32[4,8]{1,0:T(4,128)}, u32[]{:S(2)}) copy-start(f32[4,8]{1,0:T(4,128)} %constant_dynamic-slice_fusion.1) | copy-start | bytes 388
  265.8 18.6 %copy-start.23 = (f32[4,32]{1,0:T(4,128)S(1)}, f32[4,32]{1,0:T(4,128)}, u32[]{:S(2)}) copy-start(f32[4,32]{1,0:T(4,128)} %fusion.21) | copy-start | bytes 1540
  275.5 4.0 %collective-permute-start.14 = (f32[32,128]{1,0:T(8,128)}, f32[32,128]{1,0:T(8,128)S(1)}, u32[]{:S(2)}, u32[]{:S(2)}) collective-permute-start(f32[32,128]{1,0:T(8,128)} %get-tuple-element.107), channel_id=1, source_target_pairs={{0,16},{16,0},{1,17},{17,1},{2,18},{18,2},{3,19},{19,3},{4,20},{20... | collective-permute-start | bytes 49160 | tf_op jit(solution)/shard_map/ppermute | solution.py:1117
  (7 other events, 4.9 us)
Sparse Core Ops, SparseCore 0:
  10.2 43.0 all-gather.2
  55.6 48.3 all-gather.4
where the time goes:
time: 294 us; the launch traced here: 292 us
  Pallas kernels  88.5 us (30%)
  waiting for transfers between devices  70.9 us (24%)
  starting transfers between devices  50.3 us (17%)
  matrix products  30.4 us (10%)
  other arithmetic  23.2 us (8%)
  between operations  14.5 us (5%)
  local copies, waits for them, and re-layouts  14.3 us (5%)
    ppermute x20, waiting for transfers between devices, xor_blk(): return lax.ppermute(values, 'blk', [(i, i ^ bit) for i in range(count)])  38.5 us
    all_to_all x5, starting transfers between devices, to_heads(): lax.all_to_all(values, 'blk', 0, 0, axis_index_groups=row_groups, tiled=T...  27 us
    pallas_call x3, Pallas kernels, product(): pl.pallas_call(product_kernel, grid=(entries, columns // part), in_specs=...  17.7 us
    all_to_all x5, waiting for transfers between devices, to_heads(): lax.all_to_all(values, 'blk', 0, 0, axis_index_groups=row_groups, tiled=T...  16.8 us
    dot_general x4, matrix products, mm(): return jnp.dot(a, b, preferred_element_type=F32)  15.6 us
    dot_general x3, matrix products, mm_nt(): lax.dot_general(a, b, (((1,), (1,)), ((), ())), preferred_element_type=F32)  14.9 us
    ppermute x20, starting transfers between devices, xor_blk(): return lax.ppermute(values, 'blk', [(i, i ^ bit) for i in range(count)])  13.7 us
    pallas_call x1, Pallas kernels, mlp(): pl.pallas_call(functools.partial(mlp_kernel, steps, devices), grid=(steps...  11.5 us
  transfers between devices with their start and end apart: 37, of which 15 were waited for; matrix products, arithmetic and copies ran while one was open for 20% of the time, Pallas kernels for 30%

commit v1 on v0

--- a/solution.py
+++ b/solution.py
@@ -1064,32 +1064,28 @@
 
 
 def product_kernel(half_ref, *refs):
-    x_refs, y_refs, (keep_ref, send_ref, left) = refs[:4], refs[4:8], refs[8:]
+    x_refs, y_refs, (keep_ref, send_ref, left, right) = refs[:4], refs[4:8], refs[8:]
+    rows = x_refs[0].shape[1]
 
     @pl.when(pl.program_id(1) == 0)
     def _():
-        left[...] = jnp.concatenate([ref[0] for ref in x_refs], axis=0).T
-
-    right = jnp.concatenate([ref[0] for ref in y_refs], axis=0)
-    quads, _, span, many = keep_ref.shape
-    both = mm(left[...], right).reshape(2, quads, 1, span, many)
-
-    @pl.when(half_ref[0] == 0)
-    def _():
-        keep_ref[...] = both[0].astype(BF)
-        send_ref[...] = both[1].astype(BF)
-
-    @pl.when(half_ref[0] == 1)
-    def _():
-        keep_ref[...] = both[1].astype(BF)
-        send_ref[...] = both[0].astype(BF)
+        for k, ref in enumerate(x_refs):
+            left[k * rows : (k + 1) * rows] = ref[0]
+
+    for k, ref in enumerate(y_refs):
+        right[k * rows : (k + 1) * rows] = ref[0]
+    wide = left.shape[1] // 2
+    half = half_ref[0]
+    for ref, which in ((keep_ref, half), (send_ref, 1 - half)):
+        at = pl.ds(pl.multiple_of(which * wide, LANES), wide)
+        ref[...] = mm_tn(left[:, at], right[...]).astype(BF).reshape(ref.shape)
 
 
 def product(half, quads, left, right):
     entries, rows, wide = left[0].shape
     columns = right[0].shape[2]
     span = wide // (2 * quads)
-    part = min(columns, 512)
+    part = min(columns, 1024)
     shape = jax.ShapeDtypeStruct((quads, entries, span, columns), BF)
     spec = pl.BlockSpec((quads, 1, span, part), lambda e, i: (0, e, 0, i))
     return pl.pallas_call(
@@ -1100,7 +1096,7 @@
         + [pl.BlockSpec((1, rows, part), lambda e, i: (e, 0, i))] * 4,
         out_specs=[spec, spec],
         out_shape=[shape, shape],
-        scratch_shapes=[pltpu.VMEM((wide, 4 * rows), BF)],
+        scratch_shapes=[pltpu.VMEM((4 * rows, wide), BF), pltpu.VMEM((4 * rows, part), BF)],
         compiler_params=pltpu.CompilerParams(vmem_limit_bytes=ROOM),
         cost_estimate=pl.CostEstimate(
             flops=8 * entries * rows * wide * columns, bytes_accessed=8 << 20, transcendentals=0
@@ -1308,15 +1304,13 @@
             (crossed.reshape(rows, width), normed_mid, attended_low),
             (d_later_low, d_cross_low, d_middle_low),
         ),
-        up_keep,
-        down_keep,
+        back_heads,
     )
     squares = exchange_x(pieces(devices, *lefts))
     rights = jnp.stack(rights)
     rights_far = swap_batch(rights)
     rights_near = xor_blk(rights, 1, count_blk)
 
-    back_heads = after(back_heads, up_keep, down_keep)
     d_q, d_kv = self_backward(
         triplane_count, qkv, kv, kv_first, back_heads, self_lse, spare == 1
     )

time: 294 us -> 284 us (0.966)
  waiting for transfers between devices: 70.9 us -> 62.3 us
  starting transfers between devices: 50.3 us -> 55.7 us
  Pallas kernels: 88.5 us -> 84 us
    ppermute x20, waiting for transfers between devices: 38.5 us -> 28 us  [xor_blk(): return lax.ppermute(values, 'blk', [(i, i ^ bit) for i in range(count)])]
    ppermute x20, starting transfers between devices: 13.7 us -> 18.8 us  [xor_blk(): return lax.ppermute(values, 'blk', [(i, i ^ bit) for i in range(count)])]
    pallas_call x3, Pallas kernels: 17.7 us -> 13.4 us  [product(): pl.pallas_call(product_kernel, grid=(entries, columns // part), in_specs=...]
    unnamed x68 -> x70, local copies, waits for them, and re-layouts: 4.58 us -> 6.06 us
  transfers between devices with their start and end apart: 37 -> 37, of which waited for: 15 -> 17; matrix products, arithmetic and copies ran while one was open for 20% -> 19% of each run, Pallas kernels for 30% -> 29%
where the time goes in v1:
time: 284 us; the launch traced here: 282 us
  Pallas kernels  84 us (30%)
  waiting for transfers between devices  62.3 us (22%)
  starting transfers between devices  55.7 us (20%)
  matrix products  30.5 us (11%)
  other arithmetic  21.7 us (8%)
  between operations  14.6 us (5%)
  local copies, waits for them, and re-layouts  13.5 us (5%)
    ppermute x20, waiting for transfers between devices, xor_blk(): return lax.ppermute(values, 'blk', [(i, i ^ bit) for i in range(count)])  28 us
    all_to_all x5, starting transfers between devices, to_heads(): lax.all_to_all(values, 'blk', 0, 0, axis_index_groups=row_groups, tiled=T...  25.5 us
    ppermute x20, starting transfers between devices, xor_blk(): return lax.ppermute(values, 'blk', [(i, i ^ bit) for i in range(count)])  18.8 us
    all_to_all x5, waiting for transfers between devices, to_heads(): lax.all_to_all(values, 'blk', 0, 0, axis_index_groups=row_groups, tiled=T...  17.8 us
    dot_general x4, matrix products, mm(): return jnp.dot(a, b, preferred_element_type=F32)  15.6 us
    dot_general x3, matrix products, mm_nt(): lax.dot_general(a, b, (((1,), (1,)), ((), ())), preferred_element_type=F32)  14.9 us
    pallas_call x3, Pallas kernels, product(): pl.pallas_call(product_kernel, grid=(entries, columns // part), in_specs=...  13.4 us
    ppermute x8, waiting for transfers between devices, swap_batch(): return lax.ppermute(values, 'batch', [(0, 1), (1, 0)])  12.4 us
  transfers between devices with their start and end apart: 37, of which 17 were waited for; matrix products, arithmetic and copies ran while one was open for 19% of the time, Pallas kernels for 29%

profile of v1, /device:TPU:0, one launch (start us, length us, event | category | flops | bytes accessed | tf_op | source)
XLA Modules:
  0.0 282.3 jit_solution(15474421607634347077)
XLA Ops:
  8.7 3.6 %fusion.3.mod_ref = f32[2,2048]{1,0:T(2,128)} fusion(bf16[1024,2048]{1,0:T(8,128)(2,1)} %param.26, bf16[256,1024]{1,0:T(8,128)(2,1)S(1)} %copy-done, bf16[2,256]{1,0:T(2,128)(2,1)S(1)} %convert_reduce_fusion.1), kind=kOutput, calls=%fused_computation.6 | convolution fusion | flops 9441280 | bytes 4736000 | tf_op jit(solution)/shard_map/dot_general | solution.py:30
  12.3 5.7 %project.1 = bf16[16,3,48,128]{3,2,1,0:T(8,128)(2,1)} custom-call(bf16[2,48,1024]{2,1,0:T(8,128)(2,1)} %tri_ref.3, f32[2,2048]{1,0:T(2,128)} %fusion.3.mod_ref, bf16[1024,3072]{1,0:T(8,128)(2,1)} %v_ref.5, bf16[1024,3072]{1,0:T(8,128)(2,1)} %v_ref.5, bf16[1024,3072]{1,0:T(8,128)(2,1)} %v_ref.5), custom_call_target="tpu_custom_call" | custom-call | flops 603979776 | bytes 8388608 | tf_op jit(solution)/shard_map/project/pallas_call | solution.py:434
  17.9 7.4 %all-to-all-start = ((bf16[16,3,48,128]{3,2,1,0:T(8,128)(2,1)}), bf16[16,3,48,128]{3,2,1,0:T(8,128)(2,1)S(1)}, u32[]{:S(2)}, u32[]{:S(2)}) async-start(bf16[16,3,48,128]{3,2,1,0:T(8,128)(2,1)} %project.1), calls=%async_computation | async-start | bytes 1179648 | tf_op jit(solution)/shard_map/all_to_all | solution.py:1164
  25.4 1.6 collective-permute-start.1
  26.9 7.3 %fusion.26.dh_ref = f32[96,4096]{1,0:T(8,128)} fusion(bf16[96,1024]{1,0:T(8,128)(2,1)S(1)} %bitcast.172, bf16[4096,1024]{1,0:T(8,128)(2,1)} %param.37), kind=kOutput, calls=%fused_computation.83 | convolution fusion | flops 805306368 | bytes 10158080 | tf_op jit(solution)/shard_map/dot_general | solution.py:34
  34.2 7.2 %all-to-all-done.q_ref.k_ref.v_ref = bf16[16,3,48,128]{3,2,1,0:T(8,128)(2,1)S(1)} async-done(((bf16[16,3,48,128]{3,2,1,0:T(8,128)(2,1)}), bf16[16,3,48,128]{3,2,1,0:T(8,128)(2,1)S(1)}, u32[]{:S(2)}, u32[]{:S(2)}) %all-to-all-start) | async-done | bytes 589856 | tf_op jit(solution)/shard_map/all_to_all | solution.py:1164
  42.3 4.3 %self_forward.1 = (bf16[16,48,128]{2,1,0:T(8,128)(2,1)}, f32[2,768]{1,0:T(2,128)}) custom-call(s32[2]{0:T(128)} %count_ref.8, bf16[16,3,48,128]{3,2,1,0:T(8,128)(2,1)} %copy-done.15, bf16[16,3,48,128]{3,2,1,0:T(8,128)(2,1)} %copy-done.15, bf16[16,3,48,128]{3,2,1,0:T(8,128)(2,1)} %copy-done.15), custom_call_target="tpu_custom_call" | custom-call | flops 603979776 | bytes 1048576 | tf_op jit(solution)/shard_map/self_forward/pallas_call | solution.py:146
  47.1 6.1 %all-to-all-start.1 = ((bf16[16,48,128]{2,1,0:T(8,128)(2,1)}), bf16[16,48,128]{2,1,0:T(8,128)(2,1)S(1)}, u32[]{:S(2)}, u32[]{:S(2)}) async-start(bf16[16,48,128]{2,1,0:T(8,128)(2,1)} %get-tuple-element.71), calls=%async_computation.1 | async-start | bytes 393216 | tf_op jit(solution)/shard_map/all_to_all | solution.py:1164
  53.3 6.2 %convolution_convert_fusion = bf16[512,2048]{1,0:T(8,128)(2,1)} fusion(bf16[512,1024]{1,0:T(8,128)(2,1)} %bitcast.155, bf16[1024,2048]{1,0:T(8,128)(2,1)} %param.32), kind=kOutput, calls=%fused_computation.2 | convolution fusion | flops 2148532224 | bytes 7340032 | tf_op jit(solution)/shard_map/dot_general | solution.py:30
  59.5 2.7 all-to-all-done.1.got_ref
  62.9 4.5 %middle_part.1 = (bf16[96,1024]{1,0:T(8,128)(2,1)}, f32[96,1024]{1,0:T(8,128)}, bf16[96,1024]{1,0:T(8,128)(2,1)}, bf16[96,1024]{1,0:T(8,128)(2,1)}) custom-call(bf16[16,48,128]{2,1,0:T(8,128)(2,1)} %copy-done.12, bf16[96,1024]{1,0:T(8,128)(2,1)} %bitcast.152, f32[1,1024]{1,0:T(1,128)} %bitcast.186, f32[1,1024]{1,0:T(1,128)} %bitcast.188, ...), custom_call_target="tpu_custom_call" | custom-call | flops 402653184 | bytes 5242880 | tf_op jit(solution)/shard_map/middle_part/pallas_call | solution.py:495
  67.4 5.2 %cross_forward.1 = (bf16[2,48,1024]{2,1,0:T(8,128)(2,1)}, f32[2,4,256]{2,1,0:T(4,128)}, f32[96,1024]{1,0:T(8,128)}, bf16[96,1024]{1,0:T(8,128)(2,1)}) custom-call(s32[2]{0:T(128)} %count_ref.9, bf16[2,48,1024]{2,1,0:T(8,128)(2,1)} %bitcast.162, bf16[2,256,2048]{2,1,0:T(8,128)(2,1)} %bitcast.148, f32[96,1024]{1,0:T(8,128)} %get-tuple-element.76.mid_ref, ...), custom_call_target="tpu_custom_call" | custom-call | flops 402653184 | bytes 3145728 | tf_op jit(solution)/shard_map/cross_forward/pallas_call | solution.py:288
  72.6 11.3 %mlp.1 = (bf16[96,4096]{1,0:T(8,128)(2,1)}, bf16[96,4096]{1,0:T(8,128)(2,1)}, bf16[4,96,256]{2,1,0:T(8,128)(2,1)}, bf16[4,96,1024]{2,1,0:T(8,128)(2,1)}, f32[96,...) custom-call(bf16[96,1024]{1,0:T(8,128)(2,1)} %get-tuple-element.78.normed_ref, ...), custom_call_target="tpu_custom_call" | custom-call | flops 1610612736 | bytes 12582912 | tf_op jit(solution)/shard_map/mlp/pallas_call | solution.py:999
  83.9 5.5 %cross_backward.1 = bf16[2,48,1024]{2,1,0:T(8,128)(2,1)} custom-call(s32[2]{0:T(128)} %count_ref.9, bf16[2,48,1024]{2,1,0:T(8,128)(2,1)} %bitcast.163, bf16[2,256,2048]{2,1,0:T(8,128)(2,1)} %bitcast.149, bf16[2,48,1024]{2,1,0:T(8,128)(2,1)} %bitcast.177, f32[2,4,256]{2,1,0:T(4,128)} %get-tuple-element.81.lse_ref), custom_call_target="tpu_custom_call" | custom-call | flops 1006632960 | bytes 6291456 | tf_op jit(solution)/shard_map/cross_backward/pallas_call | solution.py:320
  89.4 5.6 %middle_back.1 = (f32[96,1024]{1,0:T(8,128)}, bf16[96,1024]{1,0:T(8,128)(2,1)}, bf16[16,3,48,128]{3,2,1,0:T(8,128)(2,1)}, f32[2,1024]{1,0:T(2,128)}) custom-call(bf16[96,1024]{1,0:T(8,128)(2,1)} %bitcast.164, f32[96,1024]{1,0:T(8,128)} %get-tuple-element.76.mid_ref, f32[1,1024]{1,0:T(1,128)} %bitcast.187, f32[96,1024]{1,0:T(8,128)} %get-tuple-element.82.later_ref, ...), custom_call_target="tpu_custom_call" | custom-call | flops 402653184 | bytes 6291456 | tf_op jit(solution)/shard_map/middle_back/pallas_call | solution.py:561
  95.0 3.9 %all-to-all-start.2 = ((bf16[16,3,48,128]{3,2,1,0:T(8,128)(2,1)}), bf16[16,3,48,128]{3,2,1,0:T(8,128)(2,1)S(1)}, u32[]{:S(2)}, u32[]{:S(2)}) async-start(bf16[16,3,48,128]{3,2,1,0:T(8,128)(2,1)} %get-tuple-element.83), calls=%async_computation.2 | async-start | bytes 1179648 | tf_op jit(solution)/shard_map/all_to_all | solution.py:1164
  99.8 1.5 collective-permute-start.25
  101.6 1.6 collective-permute-start.19
  103.2 1.5 collective-permute-start.3
  104.7 6.6 %collective-permute-done.3 = s32[2,4]{1,0:T(2,128)S(1)} collective-permute-done((s32[2,4]{1,0:T(2,128)S(1)}, s32[2,4]{1,0:T(2,128)S(1)}, u32[]{:S(2)}, u32[]{:S(2)}) %collective-permute-start.3) | collective-permute-done | bytes 64 | tf_op jit(solution)/shard_map/ppermute | solution.py:1113
  112.1 3.8 %product.5 = (bf16[4,1,128,1024]{3,2,1,0:T(8,128)(2,1)}, bf16[4,1,128,1024]{3,2,1,0:T(8,128)(2,1)}) custom-call(s32[1]{0:T(128)} %bitcast.23.half_ref, bf16[1,96,1024]{2,1,0:T(8,128)(2,1)} %get-tuple-element.129.refs_0_, bf16[1,96,1024]{2,1,0:T(8,128)(2,1)} %bitcast.193, bf16[1,96,1024]{2,1,0:T(8,128)(2,1)} %bitcast.194, bf16[1,96,1024]{2,1,0:T(8,128)(2,1)} %bitcast.195, ...), custom_call_target="tpu_custom_call" | custom-call | flops 805306368 | bytes 8388608 | tf_op jit(solution)/shard_map/product/pallas_call | solution.py:1091
  115.9 1.6 collective-permute-start.27
  117.9 7.7 %collective-permute-done.19 = bf16[96,4096]{1,0:T(8,128)(2,1)} collective-permute-done((bf16[96,4096]{1,0:T(8,128)(2,1)}, bf16[96,4096]{1,0:T(8,128)(2,1)}, u32[]{:S(2)}, u32[]{:S(2)}) %collective-permute-start.19) | collective-permute-done | bytes 786464 | tf_op jit(solution)/shard_map/ppermute | solution.py:1109
  126.7 1.7 collective-permute-start.16
  129.3 4.1 %memory_back.1.dmem_ref = bf16[16,2,16,128]{3,2,1,0:T(8,128)(2,1)} custom-call(s32[1]{0:T(128)} %bitcast.9.head_ref, s32[2]{0:T(128)} %count_ref.9, bf16[16,3,48,128]{3,2,1,0:T(8,128)(2,1)} %copy-done.2, bf16[16,3,48,128]{3,2,1,0:T(8,128)(2,1)} %copy-done.2, bf16[2,256,2048]{2,1,0:T(8,128)(2,1)} %bitcast.150, bf16[2,256,2048]{2,1,0:T(8,128)(2,1)} %bitcast.151), custom_call_target="tpu_custom_call" | custom-call | flops 402653184 | bytes 2097152 | tf_op jit(solution)/shard_map/memory_back/pallas_call | solution.py:370
  133.4 6.6 %self_backward.1 = (bf16[16,1,48,128]{3,2,1,0:T(8,128)(2,1)}, bf16[16,2,48,128]{3,2,1,0:T(8,128)(2,1)}) custom-call(s32[2]{0:T(128)} %count_ref.8, bf16[16,3,48,128]{3,2,1,0:T(8,128)(2,1)} %copy-done.15, bf16[16,3,48,128]{3,2,1,0:T(8,128)(2,1)} %copy-done.15, bf16[16,3,48,128]{3,2,1,0:T(8,128)(2,1)} %copy-done.15, bf16[16,3,48,128]{3,2,1,0:T(8,128)(2,1)} %copy-done.2, ...), custom_call_target="tpu_custom_call" | custom-call | flops 1509949440 | bytes 2097152 | tf_op jit(solution)/shard_map/self_backward/pallas_call | solution.py:170
  140.0 2.0 pad_maximum_fusion
  142.0 4.1 %all-to-all-start.3 = ((bf16[16,176,128]{2,1,0:T(8,128)(2,1)}), bf16[16,176,128]{2,1,0:T(8,128)(2,1)S(1)}, u32[]{:S(2)}, u32[]{:S(2)}) async-start(bf16[16,176,128]{2,1,0:T(8,128)(2,1)} %pad_maximum_fusion), calls=%async_computation.3 | async-start | bytes 1441792 | tf_op jit(solution)/shard_map/all_to_all | solution.py:1164
  146.3 1.8 collective-permute-done.27
  148.1 1.5 collective-permute-start.10
  149.5 2.0 fusion.6
  152.2 1.9 collective-permute-start.28
  154.4 1.8 collective-permute-done.17
  156.7 4.9 %product.4 = (bf16[4,1,32,4096]{3,2,1,0:T(8,128)(2,1)}, bf16[4,1,32,4096]{3,2,1,0:T(8,128)(2,1)}) custom-call(s32[1]{0:T(128)} %bitcast.44.half_ref, bf16[1,96,256]{2,1,0:T(8,128)(2,1)} %get-tuple-element.140.refs_0_, bf16[1,96,256]{2,1,0:T(8,128)(2,1)} %bitcast.181, bf16[1,96,256]{2,1,0:T(8,128)(2,1)} %bitcast.182, bf16[1,96,256]{2,1,0:T(8,128)(2,1)} %bitcast.183, ...), custom_call_target="tpu_custom_call" | custom-call | flops 805306368 | bytes 8388608 | tf_op jit(solution)/shard_map/product/pallas_call | solution.py:1091
  162.7 2.5 pieces.1
  165.2 1.2 add_convert_fusion.1
  167.0 5.2 %collective-permute-done.28 = bf16[2,1,128,1024]{3,2,1,0:T(8,128)(2,1)} collective-permute-done((bf16[2,1,128,1024]{3,2,1,0:T(8,128)(2,1)}, bf16[2,1,128,1024]{3,2,1,0:T(8,128)(2,1)}, u32[]{:S(2)}, u32[]{:S(2)}) %collective-permute-start.28) | collective-permute-done | bytes 524320 | tf_op jit(solution)/shard_map/ppermute | solution.py:1109
  173.3 2.6 collective-permute-start.29
  175.8 1.8 dynamic-slice_bitcast_fusion.4
  179.0 1.4 collective-permute-start.7
  180.5 7.2 %collective-permute-done.29 = bf16[1,1,128,1024]{3,2,1,0:T(8,128)(2,1)S(1)} collective-permute-done((bf16[1,1,128,1024]{3,2,1,0:T(8,128)(2,1)S(1)}, bf16[1,1,128,1024]{3,2,1,0:T(8,128)(2,1)S(1)}, u32[]{:S(2)}, u32[]{:S(2)}) %collective-permute-start.29) | collective-permute-done | bytes 262176 | tf_op jit(solution)/shard_map/ppermute | solution.py:1109
  188.6 1.9 add_bitcast_fusion
  190.5 3.3 %collective-permute-done.8.refs_3_ = bf16[3,96,256]{2,1,0:T(8,128)(2,1)S(1)} collective-permute-done((bf16[3,96,256]{2,1,0:T(8,128)(2,1)S(1)}, bf16[3,96,256]{2,1,0:T(8,128)(2,1)S(1)}, u32[]{:S(2)}, u32[]{:S(2)}) %collective-permute-start.8) | collective-permute-done | bytes 147488 | tf_op jit(solution)/shard_map/ppermute | solution.py:1167
  195.3 4.7 %product.3 = (bf16[4,3,32,1024]{3,2,1,0:T(8,128)(2,1)}, bf16[4,3,32,1024]{3,2,1,0:T(8,128)(2,1)}) custom-call(s32[1]{0:T(128)} %bitcast.23.half_ref, bf16[3,96,256]{2,1,0:T(8,128)(2,1)} %get-tuple-element.133.refs_0_, bf16[3,96,256]{2,1,0:T(8,128)(2,1)} %copy-done.20, bf16[3,96,256]{2,1,0:T(8,128)(2,1)} %copy-done.21, bf16[3,96,256]{2,1,0:T(8,128)(2,1)} %copy-done.22, ...), custom_call_target="tpu_custom_call" | custom-call | flops 603979776 | bytes 8388608 | tf_op jit(solution)/shard_map/product/pallas_call | solution.py:1091
  200.0 1.4 collective-permute-start.12
  202.0 1.2 fusion.5
  204.0 4.2 %fusion = f32[2,16,1024]{2,1,0:T(8,128)} fusion(bf16[2,16,2048]{2,1,0:T(8,128)(2,1)S(1)} %dot_general.31, bf16[1024,2048]{1,0:T(8,128)(2,1)} %param.32), kind=kOutput, calls=%fused_computation | convolution fusion | flops 134217728 | bytes 4456448 | tf_op jit(solution)/shard_map/dot_general | solution.py:34
  208.2 6.5 %first_back.1 = f32[2,48,1024]{2,1,0:T(8,128)} custom-call(bf16[16,176,128]{2,1,0:T(8,128)(2,1)} %copy-done.3, bf16[1024,3072]{1,0:T(8,128)(2,1)} %v_ref.5, bf16[1024,3072]{1,0:T(8,128)(2,1)} %v_ref.5, bf16[1024,3072]{1,0:T(8,128)(2,1)} %v_ref.5, bf16[2,48,1024]{2,1,0:T(8,128)(2,1)} %tri_ref.3, f32[2,2048]{1,0:T(2,128)} %fusion.3.mod_ref, ...), custom_call_target="tpu_custom_call" | custom-call | flops 603979776 | bytes 8388608 | tf_op jit(solution)/shard_map/first_back/pallas_call | solution.py:636
  214.7 1.2 add_convert_fusion.3
  217.6 1.9 collective-permute-start.23
  219.9 1.7 add_convert_fusion.5
  221.6 1.6 collective-permute-start.13
  223.2 6.8 %head_back.1 = (bf16[32,96,128]{2,1,0:T(8,128)(2,1)}, bf16[32,128]{1,0:T(8,128)(2,1)}) custom-call(s32[1]{0:T(128)} %bitcast.9.head_ref, bf16[16,1,48,128]{3,2,1,0:T(8,128)(2,1)} %get-tuple-element.85.dq_ref, bf16[16,2,48,128]{3,2,1,0:T(8,128)(2,1)} %get-tuple-element.86.dkv_ref, bf16[16,2,16,128]{3,2,1,0:T(8,128)(2,1)} %memory_back.1.dmem_ref, ...), custom_call_target="tpu_custom_call" | custom-call | flops 603979776 | bytes 5242880 | tf_op jit(solution)/shard_map/head_back/pallas_call | solution.py:761
  230.1 1.1 dynamic-slice_bitcast_fusion
  232.2 1.8 add_bitcast_fusion.1
  234.0 2.2 collective-permute-done.13
  236.3 1.5 collective-permute-start.14
  237.8 4.1 %collective-permute-done.4 = bf16[16,96,128]{2,1,0:T(8,128)(2,1)S(1)} collective-permute-done((bf16[16,96,128]{2,1,0:T(8,128)(2,1)S(1)}, bf16[16,96,128]{2,1,0:T(8,128)(2,1)S(1)}, u32[]{:S(2)}, u32[]{:S(2)}) %collective-permute-start.4) | collective-permute-done | bytes 393248 | tf_op jit(solution)/shard_map/ppermute | solution.py:1113
  244.5 3.9 %all-to-all-start.4 = ((bf16[16,128,128]{2,1,0:T(8,128)(2,1)}), bf16[16,128,128]{2,1,0:T(8,128)(2,1)S(1)}, u32[]{:S(2)}, u32[]{:S(2)}) async-start(bf16[16,128,128]{2,1,0:T(8,128)(2,1)} %pad_maximum_fusion.2), calls=%async_computation.4 | async-start | bytes 1048576 | tf_op jit(solution)/shard_map/all_to_all | solution.py:1164
  249.3 5.6 %convolution_add_fusion = f32[96,1024]{1,0:T(8,128)} fusion(f32[96,1024]{1,0:T(8,128)S(1)} %copy-done.7, bf16[96,4096]{1,0:T(8,128)(2,1)S(1)} %copy-done.4, bf16[4096,1024]{1,0:T(8,128)(2,1)} %param.37), kind=kOutput, calls=%fused_computation.3 | convolution fusion | flops 805404672 | bytes 9961472 | tf_op jit(solution)/shard_map/dot_general | solution.py:30
  254.9 7.9 %all-to-all-done.4.got_ref = bf16[16,128,128]{2,1,0:T(8,128)(2,1)S(1)} async-done(((bf16[16,128,128]{2,1,0:T(8,128)(2,1)}), bf16[16,128,128]{2,1,0:T(8,128)(2,1)S(1)}, u32[]{:S(2)}, u32[]{:S(2)}) %all-to-all-start.4) | async-done | bytes 524320 | tf_op jit(solution)/shard_map/all_to_all | solution.py:1164
  263.6 2.1 unpack.1
  268.0 1.7 collective-permute-done.5
  270.5 3.4 %fusion.14 = f32[4,1024]{1,0:T(4,128)S(1)} fusion(bf16[1024,2048]{1,0:T(8,128)(2,1)} %param.26, f32[4,2048]{1,0:T(4,128)S(1)} %select_n.117), kind=kOutput, calls=%fused_computation.57 | convolution fusion | flops 16785408 | bytes 4243456 | tf_op jit(solution)/shard_map/dot_general | solution.py:34
  (150 shorter events, 29.6 us)
Async XLA Ops:
  7.2 1.5 copy-start
  7.2 46.1 %all-gather.3.cloned.1.call-start = ((), (), s32[]{:S(2)}) async-start(), calls=%async_computation.5 | async-start | bytes 1114112 | tf_op jit(solution)/shard_map/all_gather | solution.py:1235
  12.3 13.1 %copy-start.14 = (bf16[2,48,1024]{2,1,0:T(8,128)(2,1)S(1)}, bf16[2,48,1024]{2,1,0:T(8,128)(2,1)}, u32[]{:S(2)}) copy-start(bf16[2,48,1024]{2,1,0:T(8,128)(2,1)} %param.21) | copy-start | bytes 589828
  17.9 23.5 %all-to-all-start = ((bf16[16,3,48,128]{3,2,1,0:T(8,128)(2,1)}), bf16[16,3,48,128]{3,2,1,0:T(8,128)(2,1)S(1)}, u32[]{:S(2)}, u32[]{:S(2)}) async-start(bf16[16,3,48,128]{3,2,1,0:T(8,128)(2,1)} %project.1), calls=%async_computation | async-start | bytes 1179648 | tf_op jit(solution)/shard_map/all_to_all | solution.py:1164
  25.3 197.9 %all-gather.5.cloned.1.call-start = ((), (), s32[]{:S(2)}) async-start(), calls=%async_computation.6 | async-start | bytes 3342336 | tf_op jit(solution)/shard_map/all_gather | solution.py:1256
  25.4 21.3 %collective-permute-start.1 = (bf16[96,1024]{1,0:T(8,128)(2,1)S(1)}, bf16[96,1024]{1,0:T(8,128)(2,1)S(1)}, u32[]{:S(2)}, u32[]{:S(2)}) collective-permute-start(bf16[96,1024]{1,0:T(8,128)(2,1)S(1)} %bitcast.171), channel_id=1, source_target_pairs={{0,16},{16,0},{1,17},{17,1},{2,18},{18,2},{3,19},{19,3},{4,20},{20... | collective-permute-start | bytes 589832 | tf_op jit(solution)/shard_map/ppermute | solution.py:1113
  41.4 0.8 copy-start.15
  46.5 13.0 %collective-permute-start = (bf16[96,1024]{1,0:T(8,128)(2,1)S(1)}, bf16[96,1024]{1,0:T(8,128)(2,1)S(1)}, u32[]{:S(2)}, u32[]{:S(2)}) collective-permute-start(bf16[96,1024]{1,0:T(8,128)(2,1)S(1)} %bitcast.173), channel_id=1, source_target_pairs={{0,1},{1,0},{2,3},{3,2},{4,5},{5,4},{6,7},{7,6},{8,9},{9,8},{10,11... | collective-permute-start | bytes 589832 | tf_op jit(solution)/shard_map/ppermute | solution.py:1109
  46.6 12.9 %copy-start.29 = (bf16[96,1024]{1,0:T(8,128)(2,1)}, bf16[96,1024]{1,0:T(8,128)(2,1)S(1)}, u32[]{:S(2)}) copy-start(bf16[96,1024]{1,0:T(8,128)(2,1)S(1)} %collective-permute-done.1) | copy-start | bytes 589828
  46.6 12.9 %collective-permute-start.2 = (bf16[96,1024]{1,0:T(8,128)(2,1)S(1)}, bf16[96,1024]{1,0:T(8,128)(2,1)S(1)}, u32[]{:S(2)}, u32[]{:S(2)}) collective-permute-start(bf16[96,1024]{1,0:T(8,128)(2,1)S(1)} %collective-permute-done.1), channel_id=1, source_target_pairs={{0,1},{1,0},{2,3},{3,2},{4,5},{5,4},{6,7},{7,6},{8,9},{9,8},{10,11... | collective-permute-start | bytes 589832 | tf_op jit(solution)/shard_map/ppermute | solution.py:1109
  47.1 15.1 %all-to-all-start.1 = ((bf16[16,48,128]{2,1,0:T(8,128)(2,1)}), bf16[16,48,128]{2,1,0:T(8,128)(2,1)S(1)}, u32[]{:S(2)}, u32[]{:S(2)}) async-start(bf16[16,48,128]{2,1,0:T(8,128)(2,1)} %get-tuple-element.71), calls=%async_computation.1 | async-start | bytes 393216 | tf_op jit(solution)/shard_map/all_to_all | solution.py:1164
  59.5 29.9 %copy-start.30 = (bf16[96,1024]{1,0:T(8,128)(2,1)}, bf16[96,1024]{1,0:T(8,128)(2,1)S(1)}, u32[]{:S(2)}) copy-start(bf16[96,1024]{1,0:T(8,128)(2,1)S(1)} %collective-permute-done) | copy-start | bytes 589828
  59.5 29.9 %copy-start.31 = (bf16[96,1024]{1,0:T(8,128)(2,1)}, bf16[96,1024]{1,0:T(8,128)(2,1)S(1)}, u32[]{:S(2)}) copy-start(bf16[96,1024]{1,0:T(8,128)(2,1)S(1)} %collective-permute-done.2) | copy-start | bytes 589828
  89.4 9.6 %copy-start.13 = (bf16[4,96,1024]{2,1,0:T(8,128)(2,1)S(1)}, bf16[4,96,1024]{2,1,0:T(8,128)(2,1)}, u32[]{:S(2)}) copy-start(bf16[4,96,1024]{2,1,0:T(8,128)(2,1)} %get-tuple-element.117) | copy-start | bytes 2359300
  89.4 13.8 %copy-start.28 = (s32[2,4]{1,0:T(2,128)S(1)}, s32[2,4]{1,0:T(2,128)}, u32[]{:S(2)}) copy-start(s32[2,4]{1,0:T(2,128)} %param.22) | copy-start | bytes 100
  95.0 30.6 %copy-start.19 = (bf16[4,96,256]{2,1,0:T(8,128)(2,1)S(1)}, bf16[4,96,256]{2,1,0:T(8,128)(2,1)}, u32[]{:S(2)}) copy-start(bf16[4,96,256]{2,1,0:T(8,128)(2,1)} %get-tuple-element.113) | copy-start | bytes 589828
  95.0 33.4 %all-to-all-start.2 = ((bf16[16,3,48,128]{3,2,1,0:T(8,128)(2,1)}), bf16[16,3,48,128]{3,2,1,0:T(8,128)(2,1)S(1)}, u32[]{:S(2)}, u32[]{:S(2)}) async-start(bf16[16,3,48,128]{3,2,1,0:T(8,128)(2,1)} %get-tuple-element.83), calls=%async_computation.2 | async-start | bytes 1179648 | tf_op jit(solution)/shard_map/all_to_all | solution.py:1164
  99.8 11.6 %collective-permute-start.24 = (bf16[96,1024]{1,0:T(8,128)(2,1)S(1)}, bf16[96,1024]{1,0:T(8,128)(2,1)S(1)}, u32[]{:S(2)}, u32[]{:S(2)}) collective-permute-start(bf16[96,1024]{1,0:T(8,128)(2,1)S(1)} %get-tuple-element.128), channel_id=1, source_target_pairs={{0,1},{1,0},{2,3},{3,2},{4,5},{5,4},{6,7},{7,6},{8,9},{9,8},{10,11... | collective-permute-start | bytes 589832 | tf_op jit(solution)/shard_map/ppermute | solution.py:1109
  99.8 11.5 %collective-permute-start.25 = (bf16[96,1024]{1,0:T(8,128)(2,1)S(1)}, bf16[96,1024]{1,0:T(8,128)(2,1)S(1)}, u32[]{:S(2)}, u32[]{:S(2)}) collective-permute-start(bf16[96,1024]{1,0:T(8,128)(2,1)S(1)} %get-tuple-element.127), channel_id=1, source_target_pairs={{0,16},{16,0},{1,17},{17,1},{2,18},{18,2},{3,19},{19,3},{4,20},{20... | collective-permute-start | bytes 589832 | tf_op jit(solution)/shard_map/ppermute | solution.py:1113
  101.3 10.1 %collective-permute-start.26 = (bf16[96,1024]{1,0:T(8,128)(2,1)S(1)}, bf16[96,1024]{1,0:T(8,128)(2,1)S(1)}, u32[]{:S(2)}, u32[]{:S(2)}) collective-permute-start(bf16[96,1024]{1,0:T(8,128)(2,1)S(1)} %get-tuple-element.126), channel_id=1, source_target_pairs={{0,17},{1,16},{2,19},{3,18},{4,21},{5,20},{6,23},{7,22},{8,25},{9,... | collective-permute-start | bytes 589832 | tf_op jit(solution)/shard_map/ppermute | solution.py:1167
  101.6 24.0 %collective-permute-start.19 = (bf16[96,4096]{1,0:T(8,128)(2,1)}, bf16[96,4096]{1,0:T(8,128)(2,1)}, u32[]{:S(2)}, u32[]{:S(2)}) collective-permute-start(bf16[96,4096]{1,0:T(8,128)(2,1)} %get-tuple-element.114), channel_id=1, source_target_pairs={{0,2},{1,3},{2,0},{3,1},{4,6},{5,7},{6,4},{7,5},{8,10},{9,11},{10,... | collective-permute-start | bytes 2359304 | tf_op jit(solution)/shard_map/ppermute | solution.py:1109
  103.2 8.1 %collective-permute-start.3 = (s32[2,4]{1,0:T(2,128)S(1)}, s32[2,4]{1,0:T(2,128)S(1)}, u32[]{:S(2)}, u32[]{:S(2)}) collective-permute-start(s32[2,4]{1,0:T(2,128)S(1)} %copy-done.28), channel_id=1, source_target_pairs={{0,16},{16,0},{1,17},{17,1},{2,18},{18,2},{3,19},{19,3},{4,20},{20... | collective-permute-start | bytes 104 | tf_op jit(solution)/shard_map/ppermute | solution.py:1113
  115.9 32.2 %collective-permute-start.27 = (bf16[4,1,128,1024]{3,2,1,0:T(8,128)(2,1)}, bf16[4,1,128,1024]{3,2,1,0:T(8,128)(2,1)}, u32[]{:S(2)}, u32[]{:S(2)}) collective-permute-start(bf16[4,1,128,1024]{3,2,1,0:T(8,128)(2,1)} %get-tuple-element.123), channel_id=1, source_target_pairs={{0,2},{1,3},{2,0},{3,1},{4,6},{5,7},{6,4},{7,5},{8,10},{9,11},{10,... | collective-permute-start | bytes 3145736 | tf_op jit(solution)/shard_map/ppermute | solution.py:1109
  117.9 38.2 %collective-permute-start.18 = (bf16[96,4096]{1,0:T(8,128)(2,1)}, bf16[96,4096]{1,0:T(8,128)(2,1)}, u32[]{:S(2)}, u32[]{:S(2)}) collective-permute-start(bf16[96,4096]{1,0:T(8,128)(2,1)} %get-tuple-element.114), channel_id=1, source_target_pairs={{0,1},{1,0},{2,3},{3,2},{4,5},{5,4},{6,7},{7,6},{8,9},{9,8},{10,11... | collective-permute-start | bytes 2359304 | tf_op jit(solution)/shard_map/ppermute | solution.py:1109
  125.6 30.5 %collective-permute-start.20 = (bf16[96,4096]{1,0:T(8,128)(2,1)}, bf16[96,4096]{1,0:T(8,128)(2,1)}, u32[]{:S(2)}, u32[]{:S(2)}) collective-permute-start(bf16[96,4096]{1,0:T(8,128)(2,1)} %collective-permute-done.19), channel_id=1, source_target_pairs={{0,1},{1,0},{2,3},{3,2},{4,5},{5,4},{6,7},{7,6},{8,9},{9,8},{10,11... | collective-permute-start | bytes 2359304 | tf_op jit(solution)/shard_map/ppermute | solution.py:1109
  126.2 25.3 %collective-permute-start.15 = (bf16[96,256]{1,0:T(8,128)(2,1)S(1)}, bf16[96,256]{1,0:T(8,128)(2,1)S(1)}, u32[]{:S(2)}, u32[]{:S(2)}) collective-permute-start(bf16[96,256]{1,0:T(8,128)(2,1)S(1)} %get-tuple-element.139), channel_id=1, source_target_pairs={{0,1},{1,0},{2,3},{3,2},{4,5},{5,4},{6,7},{7,6},{8,9},{9,8},{10,11... | collective-permute-start | bytes 147464 | tf_op jit(solution)/shard_map/ppermute | solution.py:1109
  126.7 25.5 %collective-permute-start.16 = (bf16[96,256]{1,0:T(8,128)(2,1)S(1)}, bf16[96,256]{1,0:T(8,128)(2,1)S(1)}, u32[]{:S(2)}, u32[]{:S(2)}) collective-permute-start(bf16[96,256]{1,0:T(8,128)(2,1)S(1)} %get-tuple-element.138), channel_id=1, source_target_pairs={{0,2},{1,3},{2,0},{3,1},{4,6},{5,7},{6,4},{7,5},{8,10},{9,11},{10,... | collective-permute-start | bytes 147464 | tf_op jit(solution)/shard_map/ppermute | solution.py:1109
  128.4 0.8 copy-start.2
  133.4 6.7 %copy-start.8 = (bf16[16,2,16,128]{3,2,1,0:T(8,128)(2,1)S(1)}, bf16[16,2,16,128]{3,2,1,0:T(8,128)(2,1)}, u32[]{:S(2)}) copy-start(bf16[16,2,16,128]{3,2,1,0:T(8,128)(2,1)} %memory_back.1.dmem_ref) | copy-start | bytes 393220
  133.4 12.8 %copy-start.11 = (bf16[2,48,1024]{2,1,0:T(8,128)(2,1)S(1)}, bf16[2,48,1024]{2,1,0:T(8,128)(2,1)}, u32[]{:S(2)}) copy-start(bf16[2,48,1024]{2,1,0:T(8,128)(2,1)} %cross_backward.1) | copy-start | bytes 589828
  133.4 12.8 %copy-start.17 = (bf16[96,1024]{1,0:T(8,128)(2,1)S(1)}, bf16[96,1024]{1,0:T(8,128)(2,1)}, u32[]{:S(2)}) copy-start(bf16[96,1024]{1,0:T(8,128)(2,1)} %get-tuple-element.106) | copy-start | bytes 589828
  133.4 12.8 %copy-start.18 = (bf16[96,1024]{1,0:T(8,128)(2,1)S(1)}, bf16[96,1024]{1,0:T(8,128)(2,1)}, u32[]{:S(2)}) copy-start(bf16[96,1024]{1,0:T(8,128)(2,1)} %get-tuple-element.108) | copy-start | bytes 589828
  133.4 16.2 %copy-start.9 = (bf16[4,1,128,1024]{3,2,1,0:T(8,128)(2,1)S(1)}, bf16[4,1,128,1024]{3,2,1,0:T(8,128)(2,1)}, u32[]{:S(2)}) copy-start(bf16[4,1,128,1024]{3,2,1,0:T(8,128)(2,1)} %get-tuple-element.122) | copy-start | bytes 3145732
  140.0 14.1 %copy-start.26 = (f32[2,1024]{1,0:T(2,128)S(1)}, f32[2,1024]{1,0:T(2,128)}, u32[]{:S(2)}) copy-start(f32[2,1024]{1,0:T(2,128)} %get-tuple-element.89) | copy-start | bytes 24580
  140.0 14.1 %copy-start.27 = (f32[2,1024]{1,0:T(2,128)S(1)}, f32[2,1024]{1,0:T(2,128)}, u32[]{:S(2)}) copy-start(f32[2,1024]{1,0:T(2,128)} %get-tuple-element.88) | copy-start | bytes 24580
  142.0 59.3 %all-to-all-start.3 = ((bf16[16,176,128]{2,1,0:T(8,128)(2,1)}), bf16[16,176,128]{2,1,0:T(8,128)(2,1)S(1)}, u32[]{:S(2)}, u32[]{:S(2)}) async-start(bf16[16,176,128]{2,1,0:T(8,128)(2,1)} %pad_maximum_fusion), calls=%async_computation.3 | async-start | bytes 1441792 | tf_op jit(solution)/shard_map/all_to_all | solution.py:1164
  146.3 27.0 %copy-start.5 = (bf16[3,96,1024]{2,1,0:T(8,128)(2,1)}, bf16[3,96,1024]{2,1,0:T(8,128)(2,1)S(1)}, u32[]{:S(2)}) copy-start(bf16[3,96,1024]{2,1,0:T(8,128)(2,1)S(1)} %pad_maximum_fusion.1.refs_4_) | copy-start | bytes 1769476
  148.1 18.4 %collective-permute-start.10 = (bf16[3,96,1024]{2,1,0:T(8,128)(2,1)S(1)}, bf16[3,96,1024]{2,1,0:T(8,128)(2,1)}, u32[]{:S(2)}, u32[]{:S(2)}) collective-permute-start(bf16[3,96,1024]{2,1,0:T(8,128)(2,1)S(1)} %pad_maximum_fusion.1.refs_4_), channel_id=1, source_target_pairs={{0,16},{16,0},{1,17},{17,1},{2,18},{18,2},{3,19},{19,3},{4,20},{20... | collective-permute-start | bytes 1769480 | tf_op jit(solution)/shard_map/ppermute | solution.py:1113
  151.6 4.6 %copy-start.23 = (bf16[96,256]{1,0:T(8,128)(2,1)}, bf16[96,256]{1,0:T(8,128)(2,1)S(1)}, u32[]{:S(2)}) copy-start(bf16[96,256]{1,0:T(8,128)(2,1)S(1)} %collective-permute-done.15) | copy-start | bytes 147460
  151.6 4.6 %collective-permute-start.17 = (bf16[96,256]{1,0:T(8,128)(2,1)S(1)}, bf16[96,256]{1,0:T(8,128)(2,1)S(1)}, u32[]{:S(2)}, u32[]{:S(2)}) collective-permute-start(bf16[96,256]{1,0:T(8,128)(2,1)S(1)} %get-tuple-element.137), channel_id=1, source_target_pairs={{0,3},{1,2},{2,1},{3,0},{4,7},{5,6},{6,5},{7,4},{8,11},{9,10},{10,... | collective-permute-start | bytes 147464 | tf_op jit(solution)/shard_map/ppermute | solution.py:1109
  152.2 3.9 %copy-start.24 = (bf16[96,256]{1,0:T(8,128)(2,1)}, bf16[96,256]{1,0:T(8,128)(2,1)S(1)}, u32[]{:S(2)}) copy-start(bf16[96,256]{1,0:T(8,128)(2,1)S(1)} %collective-permute-done.16) | copy-start | bytes 147460
  152.2 20.0 %collective-permute-start.28 = (bf16[2,1,128,1024]{3,2,1,0:T(8,128)(2,1)}, bf16[2,1,128,1024]{3,2,1,0:T(8,128)(2,1)}, u32[]{:S(2)}, u32[]{:S(2)}) collective-permute-start(bf16[2,1,128,1024]{3,2,1,0:T(8,128)(2,1)} %fusion.6), channel_id=1, source_target_pairs={{0,4},{1,5},{2,6},{3,7},{4,0},{5,1},{6,2},{7,3},{8,12},{9,13},{10,... | collective-permute-start | bytes 1572872 | tf_op jit(solution)/shard_map/ppermute | solution.py:1109
  161.7 40.3 %collective-permute-start.21 = (bf16[4,1,32,4096]{3,2,1,0:T(8,128)(2,1)}, bf16[4,1,32,4096]{3,2,1,0:T(8,128)(2,1)}, u32[]{:S(2)}, u32[]{:S(2)}) collective-permute-start(bf16[4,1,32,4096]{3,2,1,0:T(8,128)(2,1)} %get-tuple-element.116), channel_id=1, source_target_pairs={{0,16},{16,0},{1,17},{17,1},{2,18},{18,2},{3,19},{19,3},{4,20},{20... | collective-permute-start | bytes 3145736 | tf_op jit(solution)/shard_map/ppermute | solution.py:1113
  162.6 31.2 %collective-permute-start.9 = (bf16[3,96,1024]{2,1,0:T(8,128)(2,1)S(1)}, bf16[3,96,1024]{2,1,0:T(8,128)(2,1)}, u32[]{:S(2)}, u32[]{:S(2)}) collective-permute-start(bf16[3,96,1024]{2,1,0:T(8,128)(2,1)S(1)} %pad_maximum_fusion.1.refs_4_), channel_id=1, source_target_pairs={{0,1},{1,0},{2,3},{3,2},{4,5},{5,4},{6,7},{7,6},{8,9},{9,8},{10,11... | collective-permute-start | bytes 1769480 | tf_op jit(solution)/shard_map/ppermute | solution.py:1109
  166.5 35.5 %copy-start.10 = (bf16[4,1,32,4096]{3,2,1,0:T(8,128)(2,1)S(1)}, bf16[4,1,32,4096]{3,2,1,0:T(8,128)(2,1)}, u32[]{:S(2)}) copy-start(bf16[4,1,32,4096]{3,2,1,0:T(8,128)(2,1)} %get-tuple-element.115) | copy-start | bytes 3145732
  166.5 27.4 %collective-permute-start.11 = (bf16[3,96,1024]{2,1,0:T(8,128)(2,1)}, bf16[3,96,1024]{2,1,0:T(8,128)(2,1)S(1)}, u32[]{:S(2)}, u32[]{:S(2)}) collective-permute-start(bf16[3,96,1024]{2,1,0:T(8,128)(2,1)} %collective-permute-done.10.refs_6_), channel_id=1, source_target_pairs={{0,1},{1,0},{2,3},{3,2},{4,5},{5,4},{6,7},{7,6},{8,9},{9,8},{10,11... | collective-permute-start | bytes 1769480 | tf_op jit(solution)/shard_map/ppermute | solution.py:1109
  173.3 14.4 %collective-permute-start.29 = (bf16[1,1,128,1024]{3,2,1,0:T(8,128)(2,1)S(1)}, bf16[1,1,128,1024]{3,2,1,0:T(8,128)(2,1)S(1)}, u32[]{:S(2)}, u32[]{:S(2)}) collective-permute-start(bf16[1,1,128,1024]{3,2,1,0:T(8,128)(2,1)S(1)} %fusion.7), channel_id=1, source_target_pairs={{0,8},{1,9},{2,10},{3,11},{4,12},{5,13},{6,14},{7,15},{8,0},{9,1},... | collective-permute-start | bytes 786440 | tf_op jit(solution)/shard_map/ppermute | solution.py:1109
  177.6 1.4 collective-permute-start.6
  179.0 15.5 %copy-start.20 = (bf16[3,96,256]{2,1,0:T(8,128)(2,1)}, bf16[3,96,256]{2,1,0:T(8,128)(2,1)S(1)}, u32[]{:S(2)}) copy-start(bf16[3,96,256]{2,1,0:T(8,128)(2,1)S(1)} %collective-permute-done.6.refs_1_) | copy-start | bytes 442372
  179.0 11.5 %collective-permute-start.7 = (bf16[3,96,256]{2,1,0:T(8,128)(2,1)S(1)}, bf16[3,96,256]{2,1,0:T(8,128)(2,1)S(1)}, u32[]{:S(2)}, u32[]{:S(2)}) collective-permute-start(bf16[3,96,256]{2,1,0:T(8,128)(2,1)S(1)} %get-tuple-element.131), channel_id=1, source_target_pairs={{0,16},{16,0},{1,17},{17,1},{2,18},{18,2},{3,19},{19,3},{4,20},{20... | collective-permute-start | bytes 442376 | tf_op jit(solution)/shard_map/ppermute | solution.py:1113
  187.7 6.1 %collective-permute-start.8 = (bf16[3,96,256]{2,1,0:T(8,128)(2,1)S(1)}, bf16[3,96,256]{2,1,0:T(8,128)(2,1)S(1)}, u32[]{:S(2)}, u32[]{:S(2)}) collective-permute-start(bf16[3,96,256]{2,1,0:T(8,128)(2,1)S(1)} %get-tuple-element.130), channel_id=1, source_target_pairs={{0,17},{1,16},{2,19},{3,18},{4,21},{5,20},{6,23},{7,22},{8,25},{9,... | collective-permute-start | bytes 442376 | tf_op jit(solution)/shard_map/ppermute | solution.py:1167
  190.5 3.3 %copy-start.21 = (bf16[3,96,256]{2,1,0:T(8,128)(2,1)}, bf16[3,96,256]{2,1,0:T(8,128)(2,1)S(1)}, u32[]{:S(2)}) copy-start(bf16[3,96,256]{2,1,0:T(8,128)(2,1)S(1)} %collective-permute-done.7.refs_2_) | copy-start | bytes 442372
  200.0 19.9 %collective-permute-start.12 = (bf16[4,3,32,1024]{3,2,1,0:T(8,128)(2,1)}, bf16[4,3,32,1024]{3,2,1,0:T(8,128)(2,1)}, u32[]{:S(2)}, u32[]{:S(2)}) collective-permute-start(bf16[4,3,32,1024]{3,2,1,0:T(8,128)(2,1)} %get-tuple-element.110), channel_id=1, source_target_pairs={{0,2},{1,3},{2,0},{3,1},{4,6},{5,7},{6,4},{7,5},{8,10},{9,11},{10,... | collective-permute-start | bytes 2359304 | tf_op jit(solution)/shard_map/ppermute | solution.py:1109
  201.4 6.8 %copy-start.3 = (bf16[16,176,128]{2,1,0:T(8,128)(2,1)}, bf16[16,176,128]{2,1,0:T(8,128)(2,1)S(1)}, u32[]{:S(2)}) copy-start(bf16[16,176,128]{2,1,0:T(8,128)(2,1)S(1)} %all-to-all-done.3.got_ref) | copy-start | bytes 2162692
  203.2 13.7 %collective-permute-start.22 = (bf16[2,1,32,4096]{3,2,1,0:T(8,128)(2,1)S(1)}, bf16[2,1,32,4096]{3,2,1,0:T(8,128)(2,1)S(1)}, u32[]{:S(2)}, u32[]{:S(2)}) collective-permute-start(bf16[2,1,32,4096]{3,2,1,0:T(8,128)(2,1)S(1)} %fusion.5), channel_id=1, source_target_pairs={{0,4},{1,5},{2,6},{3,7},{4,0},{5,1},{6,2},{7,3},{8,12},{9,13},{10,... | collective-permute-start | bytes 1572872 | tf_op jit(solution)/shard_map/ppermute | solution.py:1109
  217.6 14.6 %collective-permute-start.23 = (bf16[1,1,32,4096]{3,2,1,0:T(8,128)(2,1)}, bf16[1,1,32,4096]{3,2,1,0:T(8,128)(2,1)}, u32[]{:S(2)}, u32[]{:S(2)}) collective-permute-start(bf16[1,1,32,4096]{3,2,1,0:T(8,128)(2,1)} %fusion.9), channel_id=1, source_target_pairs={{0,8},{1,9},{2,10},{3,11},{4,12},{5,13},{6,14},{7,15},{8,0},{9,1},... | collective-permute-start | bytes 786440 | tf_op jit(solution)/shard_map/ppermute | solution.py:1109
  221.6 14.7 %collective-permute-start.13 = (bf16[2,3,32,1024]{3,2,1,0:T(8,128)(2,1)S(1)}, bf16[2,3,32,1024]{3,2,1,0:T(8,128)(2,1)S(1)}, u32[]{:S(2)}, u32[]{:S(2)}) collective-permute-start(bf16[2,3,32,1024]{3,2,1,0:T(8,128)(2,1)S(1)} %get-tuple-element.125), channel_id=1, source_target_pairs={{0,4},{1,5},{2,6},{3,7},{4,0},{5,1},{6,2},{7,3},{8,12},{9,13},{10,... | collective-permute-start | bytes 1179656 | tf_op jit(solution)/shard_map/ppermute | solution.py:1109
  230.1 19.2 %copy-start.4 = (bf16[96,4096]{1,0:T(8,128)(2,1)S(1)}, bf16[96,4096]{1,0:T(8,128)(2,1)}, u32[]{:S(2)}) copy-start(bf16[96,4096]{1,0:T(8,128)(2,1)} %get-tuple-element.93) | copy-start | bytes 2359300
  230.1 19.2 %copy-start.7 = (f32[96,1024]{1,0:T(8,128)S(1)}, f32[96,1024]{1,0:T(8,128)}, u32[]{:S(2)}) copy-start(f32[96,1024]{1,0:T(8,128)} %get-tuple-element.92.later_ref) | copy-start | bytes 1179652
  231.2 10.6 %collective-permute-start.4 = (bf16[16,96,128]{2,1,0:T(8,128)(2,1)S(1)}, bf16[16,96,128]{2,1,0:T(8,128)(2,1)S(1)}, u32[]{:S(2)}, u32[]{:S(2)}) collective-permute-start(bf16[16,96,128]{2,1,0:T(8,128)(2,1)S(1)} %dynamic-slice_bitcast_fusion), channel_id=1, source_target_pairs={{0,16},{16,0},{1,17},{17,1},{2,18},{18,2},{3,19},{19,3},{4,20},{20... | collective-permute-start | bytes 1179656 | tf_op jit(solution)/shard_map/ppermute | solution.py:1113
  236.3 12.1 %collective-permute-start.14 = (bf16[1,3,32,1024]{3,2,1,0:T(8,128)(2,1)S(1)}, bf16[1,3,32,1024]{3,2,1,0:T(8,128)(2,1)S(1)}, u32[]{:S(2)}, u32[]{:S(2)}) collective-permute-start(bf16[1,3,32,1024]{3,2,1,0:T(8,128)(2,1)S(1)} %fusion.12), channel_id=1, source_target_pairs={{0,8},{1,9},{2,10},{3,11},{4,12},{5,13},{6,14},{7,15},{8,0},{9,1},... | collective-permute-start | bytes 589832 | tf_op jit(solution)/shard_map/ppermute | solution.py:1109
  244.5 18.4 %all-to-all-start.4 = ((bf16[16,128,128]{2,1,0:T(8,128)(2,1)}), bf16[16,128,128]{2,1,0:T(8,128)(2,1)S(1)}, u32[]{:S(2)}, u32[]{:S(2)}) async-start(bf16[16,128,128]{2,1,0:T(8,128)(2,1)} %pad_maximum_fusion.2), calls=%async_computation.4 | async-start | bytes 1048576 | tf_op jit(solution)/shard_map/all_to_all | solution.py:1164
  249.3 26.1 %copy-start.1 = (bf16[256,1024]{1,0:T(8,128)(2,1)S(1)}, bf16[256,1024]{1,0:T(8,128)(2,1)}, u32[]{:S(2)}) copy-start(bf16[256,1024]{1,0:T(8,128)(2,1)} %param.25) | copy-start | bytes 1572868
  265.7 4.0 %collective-permute-start.5 = (f32[32,128]{1,0:T(8,128)}, f32[32,128]{1,0:T(8,128)S(1)}, u32[]{:S(2)}, u32[]{:S(2)}) collective-permute-start(f32[32,128]{1,0:T(8,128)} %get-tuple-element.96), channel_id=1, source_target_pairs={{0,16},{16,0},{1,17},{17,1},{2,18},{18,2},{3,19},{19,3},{4,20},{20... | collective-permute-start | bytes 49160 | tf_op jit(solution)/shard_map/ppermute | solution.py:1113
  (8 other events, 5.7 us)
Sparse Core Ops, SparseCore 0:
  10.2 42.9 all-gather.2
  55.5 44.9 all-gather.4

commit v2 on v1

--- a/solution.py
+++ b/solution.py
@@ -75,7 +75,8 @@
 def self_backward_kernel(
     steps, count_ref, q_ref, k_ref, v_ref, do_ref, lse_ref, *rest
 ):
-    dq_ref, dkv_ref, dk_acc, dv_acc = rest[-4:]
+    joined = len(rest) == 4 and len(rest[1].shape) == 3
+    dk_acc, dv_acc = rest[-2:]
     step = pl.program_id(0)
     queries = q_ref[...].reshape(-1, LANES) * BF(HEAD_DIM**-0.5)
     keys = k_ref[...].reshape(-1, LANES)
@@ -103,7 +104,13 @@
         span = slice(item * HEAD_DIM, (item + 1) * HEAD_DIM)
         parts.append(mm(keys_t[span], d_scores) * HEAD_DIM**-0.5)
     d_q = jnp.concatenate(parts, axis=0).T
-    dq_ref[...] = d_q.astype(BF).reshape(dq_ref.shape)
+    part, own = q_ref.shape[0], q_ref.shape[2]
+    if joined:
+        mem_ref, out_ref = rest[:2]
+        out_ref[pl.ds(step * part, part), :own] = d_q.astype(BF).reshape(part, own, LANES)
+    else:
+        dq_ref, dkv_ref = rest[:2]
+        dq_ref[...] = d_q.astype(BF).reshape(dq_ref.shape)
 
     @pl.when(step == 0)
     def _():
@@ -117,6 +124,13 @@
 
     @pl.when(step == steps - 1)
     def _():
+        if joined:
+            blocks = out_ref.shape[0]
+            shape = (blocks, own, LANES)
+            out_ref[:, own : 2 * own] = dk_acc[...].astype(BF).reshape(shape)
+            out_ref[:, 2 * own : 3 * own] = dv_acc[...].astype(BF).reshape(shape)
+            out_ref[:, 3 * own :] = mem_ref[...].reshape(blocks, -1, LANES)
+            return
         shape = (dkv_ref.shape[0], 1) + dkv_ref.shape[2:]
         dkv_ref[:, 0:1] = dk_acc[...].astype(dkv_ref.dtype).reshape(shape)
         dkv_ref[:, 1:2] = dv_acc[...].astype(dkv_ref.dtype).reshape(shape)
@@ -163,10 +177,25 @@
     )(counts, q_arr, kv_arr, kv_arr)
 
 
-def self_backward(counts, q_arr, kv_arr, first, d_out, lse, low):
+def self_backward(counts, q_arr, kv_arr, first, d_out, lse, d_mem):
     steps, part, rows, many, specs = self_specs(q_arr, kv_arr, first)
     blocks = q_arr.shape[0]
     pairs = blocks * rows * many * rows * 2
+    if d_mem is None:
+        more = []
+        out_specs = [
+            pl.BlockSpec((part, 1, rows, LANES), lambda i: (i, 0, 0, 0)),
+            whole((many, 2, rows, LANES)),
+        ]
+        shapes = [
+            jax.ShapeDtypeStruct((blocks, 1, rows, LANES), BF),
+            jax.ShapeDtypeStruct((many, 2, rows, LANES), F32),
+        ]
+    else:
+        more = [d_mem]
+        shape = (blocks, 3 * rows + 2 * d_mem.shape[2], LANES)
+        out_specs = whole(shape)
+        shapes = jax.ShapeDtypeStruct(shape, BF)
     return pl.pallas_call(
         functools.partial(self_backward_kernel, steps),
         grid=(steps,),
@@ -174,15 +203,10 @@
         + [
             pl.BlockSpec((part, 1, rows, LANES), lambda i: (i, 0, 0, 0)),
             pl.BlockSpec((2, part * rows), lambda i: (0, i)),
-        ],
-        out_specs=[
-            pl.BlockSpec((part, 1, rows, LANES), lambda i: (i, 0, 0, 0)),
-            pl.BlockSpec((many, 2, rows, LANES), lambda i: (0, 0, 0, 0)),
-        ],
-        out_shape=[
-            jax.ShapeDtypeStruct((blocks, 1, rows, LANES), BF),
-            jax.ShapeDtypeStruct((many, 2, rows, LANES), BF if low else F32),
-        ],
+        ]
+        + [whole(values.shape) for values in more],
+        out_specs=out_specs,
+        out_shape=shapes,
         scratch_shapes=[
             pltpu.VMEM((many * rows, LANES), F32),
             pltpu.VMEM((many * rows, LANES), F32),
@@ -192,7 +216,7 @@
             flops=pairs * 10 * LANES, bytes_accessed=2 << 20, transcendentals=pairs
         ),
         name="self_backward",
-    )(counts, q_arr, kv_arr, kv_arr, d_out, lse)
+    )(counts, q_arr, kv_arr, kv_arr, d_out, lse, *more)
 
 
 def stack_heads(block, lane):
@@ -658,10 +682,9 @@
 
 def head_back_kernel(
     packed,
+    own,
     head_ref,
-    dq_ref,
-    dkv_ref,
-    dmem_ref,
+    grads_ref,
     tri_ref,
     patch_ref,
     q_ref,
@@ -674,9 +697,8 @@
     items, many, width = tri_ref.shape
     odd = lax.rem(head_ref[0], 2) == 1
     grads = [
-        dq_ref[:, 0].reshape(many, LANES).astype(F32).T,
-        dkv_ref[:, 0].reshape(many, LANES).astype(F32).T,
-        dkv_ref[:, 1].reshape(many, LANES).astype(F32).T,
+        grads_ref[:, kind * own : (kind + 1) * own].reshape(many, LANES).astype(F32).T
+        for kind in range(3)
     ]
     weight = []
     for ref in (q_ref, k_ref, v_ref):
@@ -700,7 +722,14 @@
         product = term if product is None else product + term
     product = product.T
     patch_rows = patch_ref.shape[1]
-    grads = [dmem_ref[:, kind].reshape(patch_rows, LANES).astype(F32).T for kind in range(2)]
+    few = patch_rows // grads_ref.shape[0]
+    grads = [
+        grads_ref[:, 3 * own + kind * few : 3 * own + (kind + 1) * few]
+        .reshape(patch_rows, LANES)
+        .astype(F32)
+        .T
+        for kind in range(2)
+    ]
     memory = None
     for item in range(items):
         span = slice(item * HEAD_DIM, (item + 1) * HEAD_DIM)
@@ -734,9 +763,8 @@
     terms_ref[...] = jnp.concatenate(lines, axis=0).astype(BF)
 
 
-def head_back(head, d_q, d_kv, d_mem, rows_all, patch_part, qkv_weight, modulation, ends):
+def head_back(head, grads, own, rows_all, patch_part, qkv_weight, modulation, ends):
     items, many, width = rows_all.shape
-    blocks, _, own, _ = d_q.shape
     pairs = width // LANES
     product = jax.ShapeDtypeStruct((width, 3 * HEAD_DIM), BF)
     if ends is None:
@@ -759,14 +787,12 @@
         return pl.BlockSpec(shape, lambda i, h: (0,) * len(shape))
 
     return pl.pallas_call(
-        functools.partial(head_back_kernel, ends is not None),
+        functools.partial(head_back_kernel, ends is not None, own),
         grid_spec=pltpu.PrefetchScalarGridSpec(
             num_scalar_prefetch=1,
             grid=(1,),
             in_specs=[
-                pl.BlockSpec((blocks, 1, own, LANES), lambda i, h: (0, 0, 0, 0)),
-                pl.BlockSpec((blocks, 2, own, LANES), lambda i, h: (0, 0, 0, 0)),
-                whole_block(d_mem.shape),
+                whole_block(grads.shape),
                 pl.BlockSpec((items, many, width), lambda i, h: (0, 0, 0)),
                 whole_block(patch_part.shape),
                 pl.BlockSpec((width, LANES), lambda i, h: (0, lax.div(h[0], 2))),
@@ -786,9 +812,7 @@
         name="head_back",
     )(
         head,
-        d_q,
-        d_kv,
-        d_mem,
+        grads,
         rows_all,
         patch_part,
         qkv_weight,
@@ -926,7 +950,7 @@
     later_ref,
     c_ref,
     gain,
-    out_w,
+    out_hbm,
     hidden_ref,
     pre_ref,
     up_piece_ref,
@@ -936,11 +960,15 @@
     d_crossed_ref,
     sums_ref,
     total,
+    out_w,
+    sem,
 ):
     step = pl.program_id(0)
+    fetch = pltpu.make_async_copy(out_hbm, out_w, sem)
 
     @pl.when(step == 0)
     def _():
+        fetch.start()
         values = normed_ref[...].astype(F32)
         for quarter in range(4):
             starts = starts_y(values.shape[1], devices, quarter)
@@ -987,6 +1015,7 @@
         d_later_ref[...] = d_later
         low = d_later.astype(BF)
         low_ref[...] = low
+        fetch.wait()
         d_crossed_ref[...] = mm_nt(low, out_w[...]).astype(BF)
 
 
@@ -1006,7 +1035,7 @@
             whole((rows, width)),
             whole((rows, width)),
             whole((1, width)),
-            whole((width, width)),
+            ANYWHERE,
         ],
         out_specs=[
             pl.BlockSpec((rows, part), lambda i: (0, i)),
@@ -1028,7 +1057,11 @@
             low,
             jax.ShapeDtypeStruct((2, width), F32),
         ],
-        scratch_shapes=[pltpu.VMEM((rows, width), F32)],
+        scratch_shapes=[
+            pltpu.VMEM((rows, width), F32),
+            pltpu.VMEM((width, width), BF),
+            pltpu.SemaphoreType.DMA,
+        ],
         compiler_params=pltpu.CompilerParams(vmem_limit_bytes=ROOM),
         cost_estimate=pl.CostEstimate(
             flops=4 * rows * width * hidden_width,
@@ -1304,30 +1337,31 @@
             (crossed.reshape(rows, width), normed_mid, attended_low),
             (d_later_low, d_cross_low, d_middle_low),
         ),
-        back_heads,
+        d_middle_low,
     )
     squares = exchange_x(pieces(devices, *lefts))
     rights = jnp.stack(rights)
     rights_far = swap_batch(rights)
     rights_near = xor_blk(rights, 1, count_blk)
 
-    d_q, d_kv = self_backward(
-        triplane_count, qkv, kv, kv_first, back_heads, self_lse, spare == 1
-    )
     head = head_at.reshape(1).astype(jnp.int32)
     d_mem = memory_back(head, patch_count, back_heads, memory, own_patches, spare == 1)
-    if spare > 1:
+    if spare == 1:
+        d_heads = self_backward(triplane_count, qkv, kv, kv_first, back_heads, self_lse, d_mem)
+    else:
+        d_q, d_kv = self_backward(
+            triplane_count, qkv, kv, kv_first, back_heads, self_lse, None
+        )
         d_kv, d_mem = [
             lax.psum_scatter(
                 values, "blk", scatter_dimension=0, axis_index_groups=head_groups, tiled=True
             ).astype(BF)
             for values in (d_kv, d_mem)
         ]
-    d_got = to_heads(
-        jnp.concatenate(
+        d_heads = jnp.concatenate(
             [values.reshape(HEADS, -1, LANES) for values in (d_q, d_kv, d_mem)], axis=1
         )
-    )
+    d_got = to_heads(d_heads)
 
     mod_rows = width // devices
     ends = jnp.concatenate([sums_mid, sums_last], axis=0)
@@ -1341,9 +1375,8 @@
     first_patch = lax.div(blk_at, HEADS) * part_patches
     payload = head_back(
         head,
-        d_q,
-        d_kv,
-        d_mem,
+        d_heads,
+        own,
         rows_all,
         lax.dynamic_slice_in_dim(patches_all, first_patch, part_patches, 1)
         if spare > 1

time: 284 us -> 278 us (0.979)
  starting transfers between devices: 55.7 us -> 49.6 us
  waiting for transfers between devices: 62.3 us -> 65.5 us
    ppermute x8, waiting for transfers between devices: 12.4 us -> 21.7 us  [swap_batch(): return lax.ppermute(values, 'batch', [(0, 1), (1, 0)])]
    ppermute x20, starting transfers between devices: 18.8 us -> 12 us  [xor_blk(): return lax.ppermute(values, 'blk', [(i, i ^ bit) for i in range(count)])]
    ppermute x20, waiting for transfers between devices: 28 us -> 23.7 us  [xor_blk(): return lax.ppermute(values, 'blk', [(i, i ^ bit) for i in range(count)])]
    unnamed x70 -> x66, local copies, waits for them, and re-layouts: 6.06 us -> 4.56 us
  transfers between devices with their start and end apart: 37 -> 37, of which waited for: 17 -> 15; matrix products, arithmetic and copies ran while one was open for 19% -> 19% of each run, Pallas kernels for 29% -> 30%
where the time goes in v2:
time: 278 us; the launch traced here: 277 us
  Pallas kernels  83.8 us (30%)
  waiting for transfers between devices  65.5 us (24%)
  starting transfers between devices  49.6 us (18%)
  matrix products  30.4 us (11%)
  other arithmetic  20.6 us (7%)
  between operations  14.6 us (5%)
  local copies, waits for them, and re-layouts  12 us (4%)
    all_to_all x5, starting transfers between devices, to_heads(): lax.all_to_all(values, 'blk', 0, 0, axis_index_groups=row_groups, tiled=T...  24.9 us
    ppermute x20, waiting for transfers between devices, xor_blk(): return lax.ppermute(values, 'blk', [(i, i ^ bit) for i in range(count)])  23.7 us
    ppermute x8, waiting for transfers between devices, swap_batch(): return lax.ppermute(values, 'batch', [(0, 1), (1, 0)])  21.7 us
    all_to_all x5, waiting for transfers between devices, to_heads(): lax.all_to_all(values, 'blk', 0, 0, axis_index_groups=row_groups, tiled=T...  16.3 us
    dot_general x4, matrix products, mm(): return jnp.dot(a, b, preferred_element_type=F32)  15.6 us
    dot_general x3, matrix products, mm_nt(): lax.dot_general(a, b, (((1,), (1,)), ((), ())), preferred_element_type=F32)  14.8 us
    pallas_call x3, Pallas kernels, product(): pl.pallas_call(product_kernel, grid=(entries, columns // part), in_specs=...  13.4 us
    ppermute x20, starting transfers between devices, xor_blk(): return lax.ppermute(values, 'blk', [(i, i ^ bit) for i in range(count)])  12 us
  transfers between devices with their start and end apart: 37, of which 15 were waited for; matrix products, arithmetic and copies ran while one was open for 19% of the time, Pallas kernels for 30%

profile of v2, /device:TPU:0, one launch (start us, length us, event | category | flops | bytes accessed | tf_op | source)
XLA Modules:
  0.0 276.5 jit_solution(13818002492111116791)
XLA Ops:
  8.7 3.6 %fusion.3.mod_ref = f32[2,2048]{1,0:T(2,128)} fusion(bf16[1024,2048]{1,0:T(8,128)(2,1)} %param.26, bf16[256,1024]{1,0:T(8,128)(2,1)S(1)} %copy-done, bf16[2,256]{1,0:T(2,128)(2,1)S(1)} %convert_reduce_fusion.1), kind=kOutput, calls=%fused_computation.6 | convolution fusion | flops 9441280 | bytes 4736000 | tf_op jit(solution)/shard_map/dot_general | solution.py:30
  12.3 5.6 %project.1 = bf16[16,3,48,128]{3,2,1,0:T(8,128)(2,1)} custom-call(bf16[2,48,1024]{2,1,0:T(8,128)(2,1)} %tri_ref.3, f32[2,2048]{1,0:T(2,128)} %fusion.3.mod_ref, bf16[1024,3072]{1,0:T(8,128)(2,1)} %v_ref.5, bf16[1024,3072]{1,0:T(8,128)(2,1)} %v_ref.5, bf16[1024,3072]{1,0:T(8,128)(2,1)} %v_ref.5), custom_call_target="tpu_custom_call" | custom-call | flops 603979776 | bytes 8388608 | tf_op jit(solution)/shard_map/project/pallas_call | solution.py:458
  17.9 7.4 %all-to-all-start = ((bf16[16,3,48,128]{3,2,1,0:T(8,128)(2,1)}), bf16[16,3,48,128]{3,2,1,0:T(8,128)(2,1)S(1)}, u32[]{:S(2)}, u32[]{:S(2)}) async-start(bf16[16,3,48,128]{3,2,1,0:T(8,128)(2,1)} %project.1), calls=%async_computation | async-start | bytes 1179648 | tf_op jit(solution)/shard_map/all_to_all | solution.py:1197
  25.8 1.5 collective-permute-start.1
  27.3 7.2 %fusion.26.dh_ref = f32[96,4096]{1,0:T(8,128)} fusion(bf16[96,1024]{1,0:T(8,128)(2,1)S(1)} %bitcast.168, bf16[4096,1024]{1,0:T(8,128)(2,1)} %param.37), kind=kOutput, calls=%fused_computation.82 | convolution fusion | flops 805306368 | bytes 10158080 | tf_op jit(solution)/shard_map/dot_general | solution.py:34
  34.5 6.9 %all-to-all-done.q_ref.k_ref.v_ref = bf16[16,3,48,128]{3,2,1,0:T(8,128)(2,1)S(1)} async-done(((bf16[16,3,48,128]{3,2,1,0:T(8,128)(2,1)}), bf16[16,3,48,128]{3,2,1,0:T(8,128)(2,1)S(1)}, u32[]{:S(2)}, u32[]{:S(2)}) %all-to-all-start) | async-done | bytes 589856 | tf_op jit(solution)/shard_map/all_to_all | solution.py:1197
  42.3 4.3 %self_forward.1 = (bf16[16,48,128]{2,1,0:T(8,128)(2,1)}, f32[2,768]{1,0:T(2,128)}) custom-call(s32[2]{0:T(128)} %count_ref.9, bf16[16,3,48,128]{3,2,1,0:T(8,128)(2,1)} %copy-done.15, bf16[16,3,48,128]{3,2,1,0:T(8,128)(2,1)} %copy-done.15, bf16[16,3,48,128]{3,2,1,0:T(8,128)(2,1)} %copy-done.15), custom_call_target="tpu_custom_call" | custom-call | flops 603979776 | bytes 1048576 | tf_op jit(solution)/shard_map/self_forward/pallas_call | solution.py:160
  46.5 6.1 %all-to-all-start.1 = ((bf16[16,48,128]{2,1,0:T(8,128)(2,1)}), bf16[16,48,128]{2,1,0:T(8,128)(2,1)S(1)}, u32[]{:S(2)}, u32[]{:S(2)}) async-start(bf16[16,48,128]{2,1,0:T(8,128)(2,1)} %get-tuple-element.69), calls=%async_computation.1 | async-start | bytes 393216 | tf_op jit(solution)/shard_map/all_to_all | solution.py:1197
  53.4 6.2 %convolution_convert_fusion = bf16[512,2048]{1,0:T(8,128)(2,1)} fusion(bf16[512,1024]{1,0:T(8,128)(2,1)} %bitcast.150, bf16[1024,2048]{1,0:T(8,128)(2,1)} %param.32), kind=kOutput, calls=%fused_computation.2 | convolution fusion | flops 2148532224 | bytes 7340032 | tf_op jit(solution)/shard_map/dot_general | solution.py:30
  59.6 2.0 all-to-all-done.1.got_ref
  62.3 4.5 %middle_part.1 = (bf16[96,1024]{1,0:T(8,128)(2,1)}, f32[96,1024]{1,0:T(8,128)}, bf16[96,1024]{1,0:T(8,128)(2,1)}, bf16[96,1024]{1,0:T(8,128)(2,1)}) custom-call(bf16[16,48,128]{2,1,0:T(8,128)(2,1)} %copy-done.11, bf16[96,1024]{1,0:T(8,128)(2,1)} %bitcast.149, f32[1,1024]{1,0:T(1,128)} %bitcast.181, f32[1,1024]{1,0:T(1,128)} %bitcast.183, ...), custom_call_target="tpu_custom_call" | custom-call | flops 402653184 | bytes 5242880 | tf_op jit(solution)/shard_map/middle_part/pallas_call | solution.py:519
  66.8 5.2 %cross_forward.1 = (bf16[2,48,1024]{2,1,0:T(8,128)(2,1)}, f32[2,4,256]{2,1,0:T(4,128)}, f32[96,1024]{1,0:T(8,128)}, bf16[96,1024]{1,0:T(8,128)(2,1)}) custom-call(s32[2]{0:T(128)} %count_ref.8, bf16[2,48,1024]{2,1,0:T(8,128)(2,1)} %bitcast.156, bf16[2,256,2048]{2,1,0:T(8,128)(2,1)} %bitcast.145, f32[96,1024]{1,0:T(8,128)} %get-tuple-element.74.mid_ref, ...), custom_call_target="tpu_custom_call" | custom-call | flops 402653184 | bytes 3145728 | tf_op jit(solution)/shard_map/cross_forward/pallas_call | solution.py:312
  72.0 10.7 %mlp.1 = (bf16[96,4096]{1,0:T(8,128)(2,1)}, bf16[96,4096]{1,0:T(8,128)(2,1)}, bf16[4,96,256]{2,1,0:T(8,128)(2,1)}, bf16[4,96,1024]{2,1,0:T(8,128)(2,1)}, f32[96,...) custom-call(bf16[96,1024]{1,0:T(8,128)(2,1)} %get-tuple-element.76.normed_ref, ...), custom_call_target="tpu_custom_call" | custom-call | flops 1610612736 | bytes 12582912 | tf_op jit(solution)/shard_map/mlp/pallas_call | solution.py:1028
  82.7 5.5 %cross_backward.1 = bf16[2,48,1024]{2,1,0:T(8,128)(2,1)} custom-call(s32[2]{0:T(128)} %count_ref.8, bf16[2,48,1024]{2,1,0:T(8,128)(2,1)} %bitcast.157, bf16[2,256,2048]{2,1,0:T(8,128)(2,1)} %bitcast.146, bf16[2,48,1024]{2,1,0:T(8,128)(2,1)} %bitcast.172, f32[2,4,256]{2,1,0:T(4,128)} %get-tuple-element.79.lse_ref), custom_call_target="tpu_custom_call" | custom-call | flops 1006632960 | bytes 6291456 | tf_op jit(solution)/shard_map/cross_backward/pallas_call | solution.py:344
  88.3 5.6 %middle_back.1 = (f32[96,1024]{1,0:T(8,128)}, bf16[96,1024]{1,0:T(8,128)(2,1)}, bf16[16,3,48,128]{3,2,1,0:T(8,128)(2,1)}, f32[2,1024]{1,0:T(2,128)}) custom-call(bf16[96,1024]{1,0:T(8,128)(2,1)} %bitcast.158, f32[96,1024]{1,0:T(8,128)} %get-tuple-element.74.mid_ref, f32[1,1024]{1,0:T(1,128)} %bitcast.182, f32[96,1024]{1,0:T(8,128)} %get-tuple-element.80.later_ref, ...), custom_call_target="tpu_custom_call" | custom-call | flops 402653184 | bytes 6291456 | tf_op jit(solution)/shard_map/middle_back/pallas_call | solution.py:585
  94.7 1.6 collective-permute-start.25
  96.5 1.1 pad_maximum_fusion.refs_4_
  97.6 1.7 collective-permute-start.10
  99.3 4.0 %all-to-all-start.2 = ((bf16[16,3,48,128]{3,2,1,0:T(8,128)(2,1)}), bf16[16,3,48,128]{3,2,1,0:T(8,128)(2,1)S(1)}, u32[]{:S(2)}, u32[]{:S(2)}) async-start(bf16[16,3,48,128]{3,2,1,0:T(8,128)(2,1)} %get-tuple-element.81), calls=%async_computation.2 | async-start | bytes 1179648 | tf_op jit(solution)/shard_map/all_to_all | solution.py:1197
  103.3 2.6 collective-permute-done.26
  105.9 3.8 %product.5 = (bf16[4,1,128,1024]{3,2,1,0:T(8,128)(2,1)}, bf16[4,1,128,1024]{3,2,1,0:T(8,128)(2,1)}) custom-call(s32[1]{0:T(128)} %bitcast.20.half_ref, bf16[1,96,1024]{2,1,0:T(8,128)(2,1)} %get-tuple-element.125.refs_0_, bf16[1,96,1024]{2,1,0:T(8,128)(2,1)} %bitcast.188, bf16[1,96,1024]{2,1,0:T(8,128)(2,1)} %bitcast.63.refs_2_, ...), custom_call_target="tpu_custom_call" | custom-call | flops 805306368 | bytes 8388608 | tf_op jit(solution)/shard_map/product/pallas_call | solution.py:1124
  109.6 1.7 collective-permute-start.3
  111.4 7.5 %collective-permute-done.3 = s32[2,4]{1,0:T(2,128)S(1)} collective-permute-done((s32[2,4]{1,0:T(2,128)S(1)}, s32[2,4]{1,0:T(2,128)S(1)}, u32[]{:S(2)}, u32[]{:S(2)}) %collective-permute-start.3) | collective-permute-done | bytes 64 | tf_op jit(solution)/shard_map/ppermute | solution.py:1146
  119.1 2.5 pieces.1
  121.6 1.9 dynamic-slice_bitcast_fusion.4
  124.2 1.6 collective-permute-start.7
  126.1 4.4 %collective-permute-done.7.refs_2_ = bf16[3,96,256]{2,1,0:T(8,128)(2,1)S(1)} collective-permute-done((bf16[3,96,256]{2,1,0:T(8,128)(2,1)S(1)}, bf16[3,96,256]{2,1,0:T(8,128)(2,1)S(1)}, u32[]{:S(2)}, u32[]{:S(2)}) %collective-permute-start.7) | collective-permute-done | bytes 147488 | tf_op jit(solution)/shard_map/ppermute | solution.py:1146
  132.5 4.2 %memory_back.1.rest_0_ = bf16[16,2,16,128]{3,2,1,0:T(8,128)(2,1)} custom-call(s32[1]{0:T(128)} %bitcast.9.head_ref, s32[2]{0:T(128)} %count_ref.8, bf16[16,3,48,128]{3,2,1,0:T(8,128)(2,1)} %copy-done.2, bf16[16,3,48,128]{3,2,1,0:T(8,128)(2,1)} %copy-done.2, bf16[2,256,2048]{2,1,0:T(8,128)(2,1)} %bitcast.147, bf16[2,256,2048]{2,1,0:T(8,128)(2,1)} %bitcast.148), custom_call_target="tpu_custom_call" | custom-call | flops 402653184 | bytes 2097152 | tf_op jit(solution)/shard_map/memory_back/pallas_call | solution.py:394
  137.6 4.8 %product.3 = (bf16[4,3,32,1024]{3,2,1,0:T(8,128)(2,1)}, bf16[4,3,32,1024]{3,2,1,0:T(8,128)(2,1)}) custom-call(s32[1]{0:T(128)} %bitcast.20.half_ref, bf16[3,96,256]{2,1,0:T(8,128)(2,1)} %get-tuple-element.129.refs_0_, bf16[3,96,256]{2,1,0:T(8,128)(2,1)} %copy-done.20, bf16[3,96,256]{2,1,0:T(8,128)(2,1)} %copy-done.21, bf16[3,96,256]{2,1,0:T(8,128)(2,1)} %copy-done.22, ...), custom_call_target="tpu_custom_call" | custom-call | flops 603979776 | bytes 8388608 | tf_op jit(solution)/shard_map/product/pallas_call | solution.py:1124
  142.4 2.1 fusion.6
  144.5 1.4 collective-permute-start.28
  145.8 6.7 %self_backward.1.grads_ref = bf16[16,176,128]{2,1,0:T(8,128)(2,1)} custom-call(s32[2]{0:T(128)} %count_ref.9, bf16[16,3,48,128]{3,2,1,0:T(8,128)(2,1)} %copy-done.15, bf16[16,3,48,128]{3,2,1,0:T(8,128)(2,1)} %copy-done.15, bf16[16,3,48,128]{3,2,1,0:T(8,128)(2,1)} %copy-done.15, bf16[16,3,48,128]{3,2,1,0:T(8,128)(2,1)} %copy-done.2, ...), custom_call_target="tpu_custom_call" | custom-call | flops 1509949440 | bytes 2097152 | tf_op jit(solution)/shard_map/self_backward/pallas_call | solution.py:199
  152.5 3.9 %all-to-all-start.3 = ((bf16[16,176,128]{2,1,0:T(8,128)(2,1)}), bf16[16,176,128]{2,1,0:T(8,128)(2,1)S(1)}, u32[]{:S(2)}, u32[]{:S(2)}) async-start(bf16[16,176,128]{2,1,0:T(8,128)(2,1)} %self_backward.1.grads_ref), calls=%async_computation.3 | async-start | bytes 1441792 | tf_op jit(solution)/shard_map/all_to_all | solution.py:1197
  157.6 1.2 add_convert_fusion.1
  159.1 1.7 collective-permute-start.16
  160.9 1.0 fusion.7
  161.9 15.6 %collective-permute-done.12 = bf16[4,3,32,1024]{3,2,1,0:T(8,128)(2,1)} collective-permute-done((bf16[4,3,32,1024]{3,2,1,0:T(8,128)(2,1)}, bf16[4,3,32,1024]{3,2,1,0:T(8,128)(2,1)}, u32[]{:S(2)}, u32[]{:S(2)}) %collective-permute-start.12) | collective-permute-done | bytes 786464 | tf_op jit(solution)/shard_map/ppermute | solution.py:1142
  177.5 1.7 add_convert_fusion.5
  179.2 2.3 collective-permute-start.29
  181.4 1.1 collective-permute-start.13
  183.8 4.9 %product.4 = (bf16[4,1,32,4096]{3,2,1,0:T(8,128)(2,1)}, bf16[4,1,32,4096]{3,2,1,0:T(8,128)(2,1)}) custom-call(s32[1]{0:T(128)} %bitcast.41.half_ref, bf16[1,96,256]{2,1,0:T(8,128)(2,1)} %get-tuple-element.136.refs_0_, bf16[1,96,256]{2,1,0:T(8,128)(2,1)} %bitcast.176, bf16[1,96,256]{2,1,0:T(8,128)(2,1)} %bitcast.177, bf16[1,96,256]{2,1,0:T(8,128)(2,1)} %bitcast.178, ...), custom_call_target="tpu_custom_call" | custom-call | flops 805306368 | bytes 8388608 | tf_op jit(solution)/shard_map/product/pallas_call | solution.py:1124
  188.7 1.4 collective-permute-start.21
  190.1 4.3 %collective-permute-done.29 = bf16[1,1,128,1024]{3,2,1,0:T(8,128)(2,1)S(1)} collective-permute-done((bf16[1,1,128,1024]{3,2,1,0:T(8,128)(2,1)S(1)}, bf16[1,1,128,1024]{3,2,1,0:T(8,128)(2,1)S(1)}, u32[]{:S(2)}, u32[]{:S(2)}) %collective-permute-start.29) | collective-permute-done | bytes 262176 | tf_op jit(solution)/shard_map/ppermute | solution.py:1142
  194.4 1.9 add_bitcast_fusion
  196.3 1.2 collective-permute-done.13
  198.2 1.1 collective-permute-start.14
  199.9 4.2 %fusion = f32[2,16,1024]{2,1,0:T(8,128)} fusion(bf16[2,16,2048]{2,1,0:T(8,128)(2,1)S(1)} %dot_general.31, bf16[1024,2048]{1,0:T(8,128)(2,1)} %param.32), kind=kOutput, calls=%fused_computation | convolution fusion | flops 134217728 | bytes 4456448 | tf_op jit(solution)/shard_map/dot_general | solution.py:34
  204.1 6.6 %first_back.1 = f32[2,48,1024]{2,1,0:T(8,128)} custom-call(bf16[16,176,128]{2,1,0:T(8,128)(2,1)} %copy-done.3, bf16[1024,3072]{1,0:T(8,128)(2,1)} %v_ref.5, bf16[1024,3072]{1,0:T(8,128)(2,1)} %v_ref.5, bf16[1024,3072]{1,0:T(8,128)(2,1)} %v_ref.5, bf16[2,48,1024]{2,1,0:T(8,128)(2,1)} %tri_ref.3, f32[2,2048]{1,0:T(2,128)} %fusion.3.mod_ref, ...), custom_call_target="tpu_custom_call" | custom-call | flops 603979776 | bytes 8388608 | tf_op jit(solution)/shard_map/first_back/pallas_call | solution.py:660
  211.6 2.5 collective-permute-done.21
  214.1 2.0 fusion.5
  216.1 1.1 collective-permute-start.22
  217.1 1.2 add_convert_fusion.3
  218.3 6.8 %head_back.1 = (bf16[32,96,128]{2,1,0:T(8,128)(2,1)}, bf16[32,128]{1,0:T(8,128)(2,1)}) custom-call(s32[1]{0:T(128)} %bitcast.9.head_ref, bf16[16,176,128]{2,1,0:T(8,128)(2,1)} %self_backward.1.grads_ref, bf16[2,768,1024]{2,1,0:T(8,128)(2,1)} %all-gather.5.cloned.1.call-done.tri_ref, bf16[2,256,1024]{2,1,0:T(8,128)(2,1)} %all-gather.3.cloned.1.call-done.patch_ref, ...), custom_call_target="tpu_custom_call" | custom-call | flops 603979776 | bytes 5242880 | tf_op jit(solution)/shard_map/head_back/pallas_call | solution.py:789
  225.2 1.1 dynamic-slice_bitcast_fusion
  226.3 1.1 collective-permute-start.4
  227.5 1.8 collective-permute-done.22
  230.9 5.5 %collective-permute-done.4 = bf16[16,96,128]{2,1,0:T(8,128)(2,1)S(1)} collective-permute-done((bf16[16,96,128]{2,1,0:T(8,128)(2,1)S(1)}, bf16[16,96,128]{2,1,0:T(8,128)(2,1)S(1)}, u32[]{:S(2)}, u32[]{:S(2)}) %collective-permute-start.4) | collective-permute-done | bytes 393248 | tf_op jit(solution)/shard_map/ppermute | solution.py:1146
  236.4 1.1 fusion.4
  239.1 3.6 %all-to-all-start.4 = ((bf16[16,128,128]{2,1,0:T(8,128)(2,1)}), bf16[16,128,128]{2,1,0:T(8,128)(2,1)S(1)}, u32[]{:S(2)}, u32[]{:S(2)}) async-start(bf16[16,128,128]{2,1,0:T(8,128)(2,1)} %pad_maximum_fusion.1), calls=%async_computation.4 | async-start | bytes 1048576 | tf_op jit(solution)/shard_map/all_to_all | solution.py:1197
  244.0 5.6 %convolution_add_fusion = f32[96,1024]{1,0:T(8,128)} fusion(f32[96,1024]{1,0:T(8,128)S(1)} %copy-done.7, bf16[96,4096]{1,0:T(8,128)(2,1)S(1)} %copy-done.4, bf16[4096,1024]{1,0:T(8,128)(2,1)} %param.37), kind=kOutput, calls=%fused_computation.3 | convolution fusion | flops 805404672 | bytes 9961472 | tf_op jit(solution)/shard_map/dot_general | solution.py:30
  249.7 7.4 %all-to-all-done.4.got_ref = bf16[16,128,128]{2,1,0:T(8,128)(2,1)S(1)} async-done(((bf16[16,128,128]{2,1,0:T(8,128)(2,1)}), bf16[16,128,128]{2,1,0:T(8,128)(2,1)S(1)}, u32[]{:S(2)}, u32[]{:S(2)}) %all-to-all-start.4) | async-done | bytes 524320 | tf_op jit(solution)/shard_map/all_to_all | solution.py:1197
  257.9 2.1 unpack.1
  262.1 1.8 collective-permute-done.5
  264.7 3.4 %fusion.14 = f32[4,1024]{1,0:T(4,128)S(1)} fusion(bf16[1024,2048]{1,0:T(8,128)(2,1)} %param.26, f32[4,2048]{1,0:T(4,128)S(1)} %select_n.117), kind=kOutput, calls=%fused_computation.56 | convolution fusion | flops 16785408 | bytes 4243456 | tf_op jit(solution)/shard_map/dot_general | solution.py:34
  (145 shorter events, 24.4 us)
Async XLA Ops:
  7.2 1.5 copy-start
  7.2 46.2 %all-gather.3.cloned.1.call-start = ((), (), s32[]{:S(2)}) async-start(), calls=%async_computation.5 | async-start | bytes 1114112 | tf_op jit(solution)/shard_map/all_gather | solution.py:1268
  12.3 13.0 %copy-start.14 = (bf16[2,48,1024]{2,1,0:T(8,128)(2,1)S(1)}, bf16[2,48,1024]{2,1,0:T(8,128)(2,1)}, u32[]{:S(2)}) copy-start(bf16[2,48,1024]{2,1,0:T(8,128)(2,1)} %param.21) | copy-start | bytes 589828
  17.9 23.5 %all-to-all-start = ((bf16[16,3,48,128]{3,2,1,0:T(8,128)(2,1)}), bf16[16,3,48,128]{3,2,1,0:T(8,128)(2,1)S(1)}, u32[]{:S(2)}, u32[]{:S(2)}) async-start(bf16[16,3,48,128]{3,2,1,0:T(8,128)(2,1)} %project.1), calls=%async_computation | async-start | bytes 1179648 | tf_op jit(solution)/shard_map/all_to_all | solution.py:1197
  25.3 34.3 %collective-permute-start = (bf16[96,1024]{1,0:T(8,128)(2,1)S(1)}, bf16[96,1024]{1,0:T(8,128)(2,1)S(1)}, u32[]{:S(2)}, u32[]{:S(2)}) collective-permute-start(bf16[96,1024]{1,0:T(8,128)(2,1)S(1)} %bitcast.166), channel_id=1, source_target_pairs={{0,1},{1,0},{2,3},{3,2},{4,5},{5,4},{6,7},{7,6},{8,9},{9,8},{10,11... | collective-permute-start | bytes 589832 | tf_op jit(solution)/shard_map/ppermute | solution.py:1142
  25.8 8.7 %collective-permute-start.1 = (bf16[96,1024]{1,0:T(8,128)(2,1)S(1)}, bf16[96,1024]{1,0:T(8,128)(2,1)S(1)}, u32[]{:S(2)}, u32[]{:S(2)}) collective-permute-start(bf16[96,1024]{1,0:T(8,128)(2,1)S(1)} %bitcast.167), channel_id=1, source_target_pairs={{0,16},{16,0},{1,17},{17,1},{2,18},{18,2},{3,19},{19,3},{4,20},{20... | collective-permute-start | bytes 589832 | tf_op jit(solution)/shard_map/ppermute | solution.py:1146
  34.5 37.5 %copy-start.30 = (bf16[96,1024]{1,0:T(8,128)(2,1)}, bf16[96,1024]{1,0:T(8,128)(2,1)S(1)}, u32[]{:S(2)}) copy-start(bf16[96,1024]{1,0:T(8,128)(2,1)S(1)} %collective-permute-done.1) | copy-start | bytes 589828
  34.5 25.1 %collective-permute-start.2 = (bf16[96,1024]{1,0:T(8,128)(2,1)S(1)}, bf16[96,1024]{1,0:T(8,128)(2,1)S(1)}, u32[]{:S(2)}, u32[]{:S(2)}) collective-permute-start(bf16[96,1024]{1,0:T(8,128)(2,1)S(1)} %collective-permute-done.1), channel_id=1, source_target_pairs={{0,1},{1,0},{2,3},{3,2},{4,5},{5,4},{6,7},{7,6},{8,9},{9,8},{10,11... | collective-permute-start | bytes 589832 | tf_op jit(solution)/shard_map/ppermute | solution.py:1142
  46.5 15.1 %all-to-all-start.1 = ((bf16[16,48,128]{2,1,0:T(8,128)(2,1)}), bf16[16,48,128]{2,1,0:T(8,128)(2,1)S(1)}, u32[]{:S(2)}, u32[]{:S(2)}) async-start(bf16[16,48,128]{2,1,0:T(8,128)(2,1)} %get-tuple-element.69), calls=%async_computation.1 | async-start | bytes 393216 | tf_op jit(solution)/shard_map/all_to_all | solution.py:1197
  52.6 165.7 %all-gather.5.cloned.1.call-start = ((), (), s32[]{:S(2)}) async-start(), calls=%async_computation.6 | async-start | bytes 3342336 | tf_op jit(solution)/shard_map/all_gather | solution.py:1289
  59.6 28.7 %copy-start.29 = (bf16[96,1024]{1,0:T(8,128)(2,1)}, bf16[96,1024]{1,0:T(8,128)(2,1)S(1)}, u32[]{:S(2)}) copy-start(bf16[96,1024]{1,0:T(8,128)(2,1)S(1)} %collective-permute-done) | copy-start | bytes 589828
  59.6 28.6 %copy-start.31 = (bf16[96,1024]{1,0:T(8,128)(2,1)}, bf16[96,1024]{1,0:T(8,128)(2,1)S(1)}, u32[]{:S(2)}) copy-start(bf16[96,1024]{1,0:T(8,128)(2,1)S(1)} %collective-permute-done.2) | copy-start | bytes 589828
  82.7 11.2 %copy-start.12 = (bf16[4,96,1024]{2,1,0:T(8,128)(2,1)S(1)}, bf16[4,96,1024]{2,1,0:T(8,128)(2,1)}, u32[]{:S(2)}) copy-start(bf16[4,96,1024]{2,1,0:T(8,128)(2,1)} %get-tuple-element.113) | copy-start | bytes 2359300
  88.2 8.3 %copy-start.10 = (bf16[2,48,1024]{2,1,0:T(8,128)(2,1)S(1)}, bf16[2,48,1024]{2,1,0:T(8,128)(2,1)}, u32[]{:S(2)}) copy-start(bf16[2,48,1024]{2,1,0:T(8,128)(2,1)} %cross_backward.1) | copy-start | bytes 589828
  88.2 8.3 %copy-start.18 = (bf16[96,1024]{1,0:T(8,128)(2,1)S(1)}, bf16[96,1024]{1,0:T(8,128)(2,1)}, u32[]{:S(2)}) copy-start(bf16[96,1024]{1,0:T(8,128)(2,1)} %get-tuple-element.102) | copy-start | bytes 589828
  93.9 15.8 %copy-start.28 = (s32[2,4]{1,0:T(2,128)S(1)}, s32[2,4]{1,0:T(2,128)}, u32[]{:S(2)}) copy-start(s32[2,4]{1,0:T(2,128)} %param.22) | copy-start | bytes 100
  94.6 8.6 %collective-permute-start.24 = (bf16[96,1024]{1,0:T(8,128)(2,1)S(1)}, bf16[96,1024]{1,0:T(8,128)(2,1)S(1)}, u32[]{:S(2)}, u32[]{:S(2)}) collective-permute-start(bf16[96,1024]{1,0:T(8,128)(2,1)S(1)} %get-tuple-element.124), channel_id=1, source_target_pairs={{0,1},{1,0},{2,3},{3,2},{4,5},{5,4},{6,7},{7,6},{8,9},{9,8},{10,11... | collective-permute-start | bytes 589832 | tf_op jit(solution)/shard_map/ppermute | solution.py:1142
  94.7 8.6 %collective-permute-start.25 = (bf16[96,1024]{1,0:T(8,128)(2,1)S(1)}, bf16[96,1024]{1,0:T(8,128)(2,1)}, u32[]{:S(2)}, u32[]{:S(2)}) collective-permute-start(bf16[96,1024]{1,0:T(8,128)(2,1)S(1)} %get-tuple-element.123), channel_id=1, source_target_pairs={{0,16},{16,0},{1,17},{17,1},{2,18},{18,2},{3,19},{19,3},{4,20},{20... | collective-permute-start | bytes 589832 | tf_op jit(solution)/shard_map/ppermute | solution.py:1146
  96.2 9.6 %collective-permute-start.26 = (bf16[96,1024]{1,0:T(8,128)(2,1)S(1)}, bf16[96,1024]{1,0:T(8,128)(2,1)}, u32[]{:S(2)}, u32[]{:S(2)}) collective-permute-start(bf16[96,1024]{1,0:T(8,128)(2,1)S(1)} %get-tuple-element.122), channel_id=1, source_target_pairs={{0,17},{1,16},{2,19},{3,18},{4,21},{5,20},{6,23},{7,22},{8,25},{9,... | collective-permute-start | bytes 589832 | tf_op jit(solution)/shard_map/ppermute | solution.py:1200
  96.5 29.3 %copy-start.13 = (bf16[96,4096]{1,0:T(8,128)(2,1)S(1)}, bf16[96,4096]{1,0:T(8,128)(2,1)}, u32[]{:S(2)}) copy-start(bf16[96,4096]{1,0:T(8,128)(2,1)} %get-tuple-element.110) | copy-start | bytes 2359300
  96.5 34.9 %copy-start.26 = (f32[2,1024]{1,0:T(2,128)S(1)}, f32[2,1024]{1,0:T(2,128)}, u32[]{:S(2)}) copy-start(f32[2,1024]{1,0:T(2,128)} %get-tuple-element.85) | copy-start | bytes 24580
  96.5 34.9 %copy-start.27 = (f32[2,1024]{1,0:T(2,128)S(1)}, f32[2,1024]{1,0:T(2,128)}, u32[]{:S(2)}) copy-start(f32[2,1024]{1,0:T(2,128)} %get-tuple-element.84) | copy-start | bytes 24580
  97.6 39.1 %copy-start.5 = (bf16[3,96,1024]{2,1,0:T(8,128)(2,1)}, bf16[3,96,1024]{2,1,0:T(8,128)(2,1)S(1)}, u32[]{:S(2)}) copy-start(bf16[3,96,1024]{2,1,0:T(8,128)(2,1)S(1)} %pad_maximum_fusion.refs_4_) | copy-start | bytes 1769476
  97.6 26.4 %collective-permute-start.10 = (bf16[3,96,1024]{2,1,0:T(8,128)(2,1)S(1)}, bf16[3,96,1024]{2,1,0:T(8,128)(2,1)}, u32[]{:S(2)}, u32[]{:S(2)}) collective-permute-start(bf16[3,96,1024]{2,1,0:T(8,128)(2,1)S(1)} %pad_maximum_fusion.refs_4_), channel_id=1, source_target_pairs={{0,16},{16,0},{1,17},{17,1},{2,18},{18,2},{3,19},{19,3},{4,20},{20... | collective-permute-start | bytes 1769480 | tf_op jit(solution)/shard_map/ppermute | solution.py:1146
  99.3 32.4 %all-to-all-start.2 = ((bf16[16,3,48,128]{3,2,1,0:T(8,128)(2,1)}), bf16[16,3,48,128]{3,2,1,0:T(8,128)(2,1)S(1)}, u32[]{:S(2)}, u32[]{:S(2)}) async-start(bf16[16,3,48,128]{3,2,1,0:T(8,128)(2,1)} %get-tuple-element.81), calls=%async_computation.2 | async-start | bytes 1179648 | tf_op jit(solution)/shard_map/all_to_all | solution.py:1197
  103.2 2.6 copy-start.32
  109.6 32.7 %collective-permute-start.27 = (bf16[4,1,128,1024]{3,2,1,0:T(8,128)(2,1)}, bf16[4,1,128,1024]{3,2,1,0:T(8,128)(2,1)}, u32[]{:S(2)}, u32[]{:S(2)}) collective-permute-start(bf16[4,1,128,1024]{3,2,1,0:T(8,128)(2,1)} %get-tuple-element.119), channel_id=1, source_target_pairs={{0,2},{1,3},{2,0},{3,1},{4,6},{5,7},{6,4},{7,5},{8,10},{9,11},{10,... | collective-permute-start | bytes 3145736 | tf_op jit(solution)/shard_map/ppermute | solution.py:1142
  109.6 9.3 %collective-permute-start.3 = (s32[2,4]{1,0:T(2,128)S(1)}, s32[2,4]{1,0:T(2,128)S(1)}, u32[]{:S(2)}, u32[]{:S(2)}) collective-permute-start(s32[2,4]{1,0:T(2,128)S(1)} %copy-done.28), channel_id=1, source_target_pairs={{0,16},{16,0},{1,17},{17,1},{2,18},{18,2},{3,19},{19,3},{4,20},{20... | collective-permute-start | bytes 104 | tf_op jit(solution)/shard_map/ppermute | solution.py:1146
  119.0 18.5 %collective-permute-start.9 = (bf16[3,96,1024]{2,1,0:T(8,128)(2,1)S(1)}, bf16[3,96,1024]{2,1,0:T(8,128)(2,1)}, u32[]{:S(2)}, u32[]{:S(2)}) collective-permute-start(bf16[3,96,1024]{2,1,0:T(8,128)(2,1)S(1)} %pad_maximum_fusion.refs_4_), channel_id=1, source_target_pairs={{0,1},{1,0},{2,3},{3,2},{4,5},{5,4},{6,7},{7,6},{8,9},{9,8},{10,11... | collective-permute-start | bytes 1769480 | tf_op jit(solution)/shard_map/ppermute | solution.py:1142
  123.5 2.3 collective-permute-start.6
  124.0 13.6 %collective-permute-start.11 = (bf16[3,96,1024]{2,1,0:T(8,128)(2,1)}, bf16[3,96,1024]{2,1,0:T(8,128)(2,1)}, u32[]{:S(2)}, u32[]{:S(2)}) collective-permute-start(bf16[3,96,1024]{2,1,0:T(8,128)(2,1)} %collective-permute-done.10.refs_6_), channel_id=1, source_target_pairs={{0,1},{1,0},{2,3},{3,2},{4,5},{5,4},{6,7},{7,6},{8,9},{9,8},{10,11... | collective-permute-start | bytes 1769480 | tf_op jit(solution)/shard_map/ppermute | solution.py:1142
  124.2 6.2 %collective-permute-start.7 = (bf16[3,96,256]{2,1,0:T(8,128)(2,1)S(1)}, bf16[3,96,256]{2,1,0:T(8,128)(2,1)S(1)}, u32[]{:S(2)}, u32[]{:S(2)}) collective-permute-start(bf16[3,96,256]{2,1,0:T(8,128)(2,1)S(1)} %get-tuple-element.127), channel_id=1, source_target_pairs={{0,16},{16,0},{1,17},{17,1},{2,18},{18,2},{3,19},{19,3},{4,20},{20... | collective-permute-start | bytes 442376 | tf_op jit(solution)/shard_map/ppermute | solution.py:1146
  125.8 5.8 %copy-start.20 = (bf16[3,96,256]{2,1,0:T(8,128)(2,1)}, bf16[3,96,256]{2,1,0:T(8,128)(2,1)S(1)}, u32[]{:S(2)}) copy-start(bf16[3,96,256]{2,1,0:T(8,128)(2,1)S(1)} %collective-permute-done.6.refs_1_) | copy-start | bytes 442372
  125.8 31.4 %collective-permute-start.19 = (bf16[96,4096]{1,0:T(8,128)(2,1)S(1)}, bf16[96,4096]{1,0:T(8,128)(2,1)}, u32[]{:S(2)}, u32[]{:S(2)}) collective-permute-start(bf16[96,4096]{1,0:T(8,128)(2,1)S(1)} %copy-done.13), channel_id=1, source_target_pairs={{0,2},{1,3},{2,0},{3,1},{4,6},{5,7},{6,4},{7,5},{8,10},{9,11},{10,... | collective-permute-start | bytes 2359304 | tf_op jit(solution)/shard_map/ppermute | solution.py:1142
  130.4 7.2 %copy-start.21 = (bf16[3,96,256]{2,1,0:T(8,128)(2,1)}, bf16[3,96,256]{2,1,0:T(8,128)(2,1)S(1)}, u32[]{:S(2)}) copy-start(bf16[3,96,256]{2,1,0:T(8,128)(2,1)S(1)} %collective-permute-done.7.refs_2_) | copy-start | bytes 442372
  130.4 6.3 %collective-permute-start.8 = (bf16[3,96,256]{2,1,0:T(8,128)(2,1)}, bf16[3,96,256]{2,1,0:T(8,128)(2,1)S(1)}, u32[]{:S(2)}, u32[]{:S(2)}) collective-permute-start(bf16[3,96,256]{2,1,0:T(8,128)(2,1)} %get-tuple-element.126), channel_id=1, source_target_pairs={{0,17},{1,16},{2,19},{3,18},{4,21},{5,20},{6,23},{7,22},{8,25},{9,... | collective-permute-start | bytes 442376 | tf_op jit(solution)/shard_map/ppermute | solution.py:1200
  131.7 0.8 copy-start.2
  132.5 9.9 %copy-start.8 = (bf16[4,1,128,1024]{3,2,1,0:T(8,128)(2,1)S(1)}, bf16[4,1,128,1024]{3,2,1,0:T(8,128)(2,1)}, u32[]{:S(2)}) copy-start(bf16[4,1,128,1024]{3,2,1,0:T(8,128)(2,1)} %get-tuple-element.118) | copy-start | bytes 3145732
  136.7 46.5 %collective-permute-start.18 = (bf16[96,4096]{1,0:T(8,128)(2,1)S(1)}, bf16[96,4096]{1,0:T(8,128)(2,1)}, u32[]{:S(2)}, u32[]{:S(2)}) collective-permute-start(bf16[96,4096]{1,0:T(8,128)(2,1)S(1)} %copy-done.13), channel_id=1, source_target_pairs={{0,1},{1,0},{2,3},{3,2},{4,5},{5,4},{6,7},{7,6},{8,9},{9,8},{10,11... | collective-permute-start | bytes 2359304 | tf_op jit(solution)/shard_map/ppermute | solution.py:1142
  142.4 35.1 %collective-permute-start.12 = (bf16[4,3,32,1024]{3,2,1,0:T(8,128)(2,1)}, bf16[4,3,32,1024]{3,2,1,0:T(8,128)(2,1)}, u32[]{:S(2)}, u32[]{:S(2)}) collective-permute-start(bf16[4,3,32,1024]{3,2,1,0:T(8,128)(2,1)} %get-tuple-element.106), channel_id=1, source_target_pairs={{0,2},{1,3},{2,0},{3,1},{4,6},{5,7},{6,4},{7,5},{8,10},{9,11},{10,... | collective-permute-start | bytes 2359304 | tf_op jit(solution)/shard_map/ppermute | solution.py:1142
  142.4 14.0 %copy-start.19 = (bf16[4,96,256]{2,1,0:T(8,128)(2,1)S(1)}, bf16[4,96,256]{2,1,0:T(8,128)(2,1)}, u32[]{:S(2)}) copy-start(bf16[4,96,256]{2,1,0:T(8,128)(2,1)} %get-tuple-element.109) | copy-start | bytes 589828
  144.5 14.7 %collective-permute-start.28 = (bf16[2,1,128,1024]{3,2,1,0:T(8,128)(2,1)}, bf16[2,1,128,1024]{3,2,1,0:T(8,128)(2,1)}, u32[]{:S(2)}, u32[]{:S(2)}) collective-permute-start(bf16[2,1,128,1024]{3,2,1,0:T(8,128)(2,1)} %fusion.6), channel_id=1, source_target_pairs={{0,4},{1,5},{2,6},{3,7},{4,0},{5,1},{6,2},{7,3},{8,12},{9,13},{10,... | collective-permute-start | bytes 1572872 | tf_op jit(solution)/shard_map/ppermute | solution.py:1142
  152.5 46.8 %all-to-all-start.3 = ((bf16[16,176,128]{2,1,0:T(8,128)(2,1)}), bf16[16,176,128]{2,1,0:T(8,128)(2,1)S(1)}, u32[]{:S(2)}, u32[]{:S(2)}) async-start(bf16[16,176,128]{2,1,0:T(8,128)(2,1)} %self_backward.1.grads_ref), calls=%async_computation.3 | async-start | bytes 1441792 | tf_op jit(solution)/shard_map/all_to_all | solution.py:1197
  157.1 22.1 %collective-permute-start.15 = (bf16[96,256]{1,0:T(8,128)(2,1)S(1)}, bf16[96,256]{1,0:T(8,128)(2,1)S(1)}, u32[]{:S(2)}, u32[]{:S(2)}) collective-permute-start(bf16[96,256]{1,0:T(8,128)(2,1)S(1)} %get-tuple-element.135), channel_id=1, source_target_pairs={{0,1},{1,0},{2,3},{3,2},{4,5},{5,4},{6,7},{7,6},{8,9},{9,8},{10,11... | collective-permute-start | bytes 147464 | tf_op jit(solution)/shard_map/ppermute | solution.py:1142
  157.3 26.0 %collective-permute-start.20 = (bf16[96,4096]{1,0:T(8,128)(2,1)}, bf16[96,4096]{1,0:T(8,128)(2,1)}, u32[]{:S(2)}, u32[]{:S(2)}) collective-permute-start(bf16[96,4096]{1,0:T(8,128)(2,1)} %collective-permute-done.19), channel_id=1, source_target_pairs={{0,1},{1,0},{2,3},{3,2},{4,5},{5,4},{6,7},{7,6},{8,9},{9,8},{10,11... | collective-permute-start | bytes 2359304 | tf_op jit(solution)/shard_map/ppermute | solution.py:1142
  159.1 22.3 %collective-permute-start.16 = (bf16[96,256]{1,0:T(8,128)(2,1)S(1)}, bf16[96,256]{1,0:T(8,128)(2,1)S(1)}, u32[]{:S(2)}, u32[]{:S(2)}) collective-permute-start(bf16[96,256]{1,0:T(8,128)(2,1)S(1)} %get-tuple-element.134), channel_id=1, source_target_pairs={{0,2},{1,3},{2,0},{3,1},{4,6},{5,7},{6,4},{7,5},{8,10},{9,11},{10,... | collective-permute-start | bytes 147464 | tf_op jit(solution)/shard_map/ppermute | solution.py:1142
  177.5 5.8 %collective-permute-start.17 = (bf16[96,256]{1,0:T(8,128)(2,1)S(1)}, bf16[96,256]{1,0:T(8,128)(2,1)S(1)}, u32[]{:S(2)}, u32[]{:S(2)}) collective-permute-start(bf16[96,256]{1,0:T(8,128)(2,1)S(1)} %get-tuple-element.133), channel_id=1, source_target_pairs={{0,3},{1,2},{2,1},{3,0},{4,7},{5,6},{6,5},{7,4},{8,11},{9,10},{10,... | collective-permute-start | bytes 147464 | tf_op jit(solution)/shard_map/ppermute | solution.py:1142
  179.1 4.1 %copy-start.23 = (bf16[96,256]{1,0:T(8,128)(2,1)}, bf16[96,256]{1,0:T(8,128)(2,1)S(1)}, u32[]{:S(2)}) copy-start(bf16[96,256]{1,0:T(8,128)(2,1)S(1)} %collective-permute-done.15) | copy-start | bytes 147460
  179.2 15.2 %collective-permute-start.29 = (bf16[1,1,128,1024]{3,2,1,0:T(8,128)(2,1)S(1)}, bf16[1,1,128,1024]{3,2,1,0:T(8,128)(2,1)S(1)}, u32[]{:S(2)}, u32[]{:S(2)}) collective-permute-start(bf16[1,1,128,1024]{3,2,1,0:T(8,128)(2,1)S(1)} %fusion.7), channel_id=1, source_target_pairs={{0,8},{1,9},{2,10},{3,11},{4,12},{5,13},{6,14},{7,15},{8,0},{9,1},... | collective-permute-start | bytes 786440 | tf_op jit(solution)/shard_map/ppermute | solution.py:1142
  181.4 1.8 copy-start.24
  181.4 16.0 %collective-permute-start.13 = (bf16[2,3,32,1024]{3,2,1,0:T(8,128)(2,1)S(1)}, bf16[2,3,32,1024]{3,2,1,0:T(8,128)(2,1)S(1)}, u32[]{:S(2)}, u32[]{:S(2)}) collective-permute-start(bf16[2,3,32,1024]{3,2,1,0:T(8,128)(2,1)S(1)} %get-tuple-element.121), channel_id=1, source_target_pairs={{0,4},{1,5},{2,6},{3,7},{4,0},{5,1},{6,2},{7,3},{8,12},{9,13},{10,... | collective-permute-start | bytes 1179656 | tf_op jit(solution)/shard_map/ppermute | solution.py:1142
  188.7 25.4 %collective-permute-start.21 = (bf16[4,1,32,4096]{3,2,1,0:T(8,128)(2,1)}, bf16[4,1,32,4096]{3,2,1,0:T(8,128)(2,1)}, u32[]{:S(2)}, u32[]{:S(2)}) collective-permute-start(bf16[4,1,32,4096]{3,2,1,0:T(8,128)(2,1)} %get-tuple-element.112), channel_id=1, source_target_pairs={{0,16},{16,0},{1,17},{17,1},{2,18},{18,2},{3,19},{19,3},{4,20},{20... | collective-permute-start | bytes 3145736 | tf_op jit(solution)/shard_map/ppermute | solution.py:1146
  198.2 12.5 %collective-permute-start.14 = (bf16[1,3,32,1024]{3,2,1,0:T(8,128)(2,1)S(1)}, bf16[1,3,32,1024]{3,2,1,0:T(8,128)(2,1)S(1)}, u32[]{:S(2)}, u32[]{:S(2)}) collective-permute-start(bf16[1,3,32,1024]{3,2,1,0:T(8,128)(2,1)S(1)} %fusion.12), channel_id=1, source_target_pairs={{0,8},{1,9},{2,10},{3,11},{4,12},{5,13},{6,14},{7,15},{8,0},{9,1},... | collective-permute-start | bytes 589832 | tf_op jit(solution)/shard_map/ppermute | solution.py:1142
  199.3 4.8 %copy-start.3 = (bf16[16,176,128]{2,1,0:T(8,128)(2,1)}, bf16[16,176,128]{2,1,0:T(8,128)(2,1)S(1)}, u32[]{:S(2)}) copy-start(bf16[16,176,128]{2,1,0:T(8,128)(2,1)S(1)} %all-to-all-done.3.got_ref) | copy-start | bytes 2162692
  204.1 6.6 %copy-start.17 = (bf16[2,3,32,1024]{3,2,1,0:T(8,128)(2,1)S(1)}, bf16[2,3,32,1024]{3,2,1,0:T(8,128)(2,1)}, u32[]{:S(2)}) copy-start(bf16[2,3,32,1024]{3,2,1,0:T(8,128)(2,1)} %copy-done.16) | copy-start | bytes 1179652
  204.1 10.0 %copy-start.9 = (bf16[4,1,32,4096]{3,2,1,0:T(8,128)(2,1)S(1)}, bf16[4,1,32,4096]{3,2,1,0:T(8,128)(2,1)}, u32[]{:S(2)}) copy-start(bf16[4,1,32,4096]{3,2,1,0:T(8,128)(2,1)} %get-tuple-element.111) | copy-start | bytes 3145732
  216.1 13.2 %collective-permute-start.22 = (bf16[2,1,32,4096]{3,2,1,0:T(8,128)(2,1)}, bf16[2,1,32,4096]{3,2,1,0:T(8,128)(2,1)S(1)}, u32[]{:S(2)}, u32[]{:S(2)}) collective-permute-start(bf16[2,1,32,4096]{3,2,1,0:T(8,128)(2,1)} %fusion.5), channel_id=1, source_target_pairs={{0,4},{1,5},{2,6},{3,7},{4,0},{5,1},{6,2},{7,3},{8,12},{9,13},{10,... | collective-permute-start | bytes 1572872 | tf_op jit(solution)/shard_map/ppermute | solution.py:1142
  225.2 18.9 %copy-start.4 = (bf16[96,4096]{1,0:T(8,128)(2,1)S(1)}, bf16[96,4096]{1,0:T(8,128)(2,1)}, u32[]{:S(2)}) copy-start(bf16[96,4096]{1,0:T(8,128)(2,1)} %get-tuple-element.89) | copy-start | bytes 2359300
  225.2 18.9 %copy-start.7 = (f32[96,1024]{1,0:T(8,128)S(1)}, f32[96,1024]{1,0:T(8,128)}, u32[]{:S(2)}) copy-start(f32[96,1024]{1,0:T(8,128)} %get-tuple-element.88.later_ref) | copy-start | bytes 1179652
  226.3 10.1 %collective-permute-start.4 = (bf16[16,96,128]{2,1,0:T(8,128)(2,1)S(1)}, bf16[16,96,128]{2,1,0:T(8,128)(2,1)S(1)}, u32[]{:S(2)}, u32[]{:S(2)}) collective-permute-start(bf16[16,96,128]{2,1,0:T(8,128)(2,1)S(1)} %dynamic-slice_bitcast_fusion), channel_id=1, source_target_pairs={{0,16},{16,0},{1,17},{17,1},{2,18},{18,2},{3,19},{19,3},{4,20},{20... | collective-permute-start | bytes 1179656 | tf_op jit(solution)/shard_map/ppermute | solution.py:1146
  230.0 13.2 %collective-permute-start.23 = (bf16[1,1,32,4096]{3,2,1,0:T(8,128)(2,1)}, bf16[1,1,32,4096]{3,2,1,0:T(8,128)(2,1)S(1)}, u32[]{:S(2)}, u32[]{:S(2)}) collective-permute-start(bf16[1,1,32,4096]{3,2,1,0:T(8,128)(2,1)} %fusion.9), channel_id=1, source_target_pairs={{0,8},{1,9},{2,10},{3,11},{4,12},{5,13},{6,14},{7,15},{8,0},{9,1},... | collective-permute-start | bytes 786440 | tf_op jit(solution)/shard_map/ppermute | solution.py:1142
  239.1 18.0 %all-to-all-start.4 = ((bf16[16,128,128]{2,1,0:T(8,128)(2,1)}), bf16[16,128,128]{2,1,0:T(8,128)(2,1)S(1)}, u32[]{:S(2)}, u32[]{:S(2)}) async-start(bf16[16,128,128]{2,1,0:T(8,128)(2,1)} %pad_maximum_fusion.1), calls=%async_computation.4 | async-start | bytes 1048576 | tf_op jit(solution)/shard_map/all_to_all | solution.py:1197
  244.0 25.6 %copy-start.1 = (bf16[256,1024]{1,0:T(8,128)(2,1)S(1)}, bf16[256,1024]{1,0:T(8,128)(2,1)}, u32[]{:S(2)}) copy-start(bf16[256,1024]{1,0:T(8,128)(2,1)} %param.25) | copy-start | bytes 1572868
  260.0 4.0 %collective-permute-start.5 = (f32[32,128]{1,0:T(8,128)}, f32[32,128]{1,0:T(8,128)S(1)}, u32[]{:S(2)}, u32[]{:S(2)}) collective-permute-start(f32[32,128]{1,0:T(8,128)} %get-tuple-element.92), channel_id=1, source_target_pairs={{0,16},{16,0},{1,17},{17,1},{2,18},{18,2},{3,19},{19,3},{4,20},{20... | collective-permute-start | bytes 49160 | tf_op jit(solution)/shard_map/ppermute | solution.py:1146
  (6 other events, 4.5 us)
Sparse Core Ops, SparseCore 0:
  10.2 43.0 all-gather.2
  55.7 46.4 all-gather.4

commit v3 on v2

--- a/solution.py
+++ b/solution.py
@@ -1288,9 +1288,7 @@
     kept = lax.optimization_barrier((triplane, attended_heads))[0]
     rows_all = lax.all_gather(kept, "blk", axis=1, axis_index_groups=row_groups, tiled=True)
 
-    attended_got, memory, grad_quad = lax.optimization_barrier(
-        (attended_got, memory, grad_quad)
-    )
+    attended_got, memory = lax.optimization_barrier((attended_got, memory))
     attended_low, middle, normed_mid, cross_q = middle_part(
         attended_got, triplane.reshape(rows, width), self_out, gain_mid, bias_mid, cross_query
     )

time: 278 us -> 278 us (level)
  no operation moved by 1% of the time
where the time goes in v3:
time: 278 us; the launch traced here: 276 us
  Pallas kernels  83.8 us (30%)
  waiting for transfers between devices  64.2 us (23%)
  starting transfers between devices  50.7 us (18%)
  matrix products  30.4 us (11%)
  other arithmetic  20.6 us (7%)
  between operations  14.5 us (5%)
  local copies, waits for them, and re-layouts  12 us (4%)
    all_to_all x5, starting transfers between devices, to_heads(): lax.all_to_all(values, 'blk', 0, 0, axis_index_groups=row_groups, tiled=T...  24.9 us
    ppermute x20, waiting for transfers between devices, xor_blk(): return lax.ppermute(values, 'blk', [(i, i ^ bit) for i in range(count)])  23.4 us
    ppermute x8, waiting for transfers between devices, swap_batch(): return lax.ppermute(values, 'batch', [(0, 1), (1, 0)])  20.5 us
    all_to_all x5, waiting for transfers between devices, to_heads(): lax.all_to_all(values, 'blk', 0, 0, axis_index_groups=row_groups, tiled=T...  16.5 us
    dot_general x4, matrix products, mm(): return jnp.dot(a, b, preferred_element_type=F32)  15.6 us
    dot_general x3, matrix products, mm_nt(): lax.dot_general(a, b, (((1,), (1,)), ((), ())), preferred_element_type=F32)  14.8 us
    pallas_call x3, Pallas kernels, product(): pl.pallas_call(product_kernel, grid=(entries, columns // part), in_specs=...  13.5 us
    ppermute x20, starting transfers between devices, xor_blk(): return lax.ppermute(values, 'blk', [(i, i ^ bit) for i in range(count)])  12.4 us
  transfers between devices with their start and end apart: 37, of which 15 were waited for; matrix products, arithmetic and copies ran while one was open for 19% of the time, Pallas kernels for 30%

profile of v3, /device:TPU:0, one launch (start us, length us, event | category | flops | bytes accessed | tf_op | source)
XLA Modules:
  0.0 276.2 jit_solution(6123239871419984970)
XLA Ops:
  8.7 3.6 %fusion.3.mod_ref = f32[2,2048]{1,0:T(2,128)} fusion(bf16[1024,2048]{1,0:T(8,128)(2,1)} %param.26, bf16[256,1024]{1,0:T(8,128)(2,1)S(1)} %copy-done, bf16[2,256]{1,0:T(2,128)(2,1)S(1)} %convert_reduce_fusion.1), kind=kOutput, calls=%fused_computation.6 | convolution fusion | flops 9441280 | bytes 4736000 | tf_op jit(solution)/shard_map/dot_general | solution.py:30
  12.3 5.6 %project.1 = bf16[16,3,48,128]{3,2,1,0:T(8,128)(2,1)} custom-call(bf16[2,48,1024]{2,1,0:T(8,128)(2,1)} %tri_ref.3, f32[2,2048]{1,0:T(2,128)} %fusion.3.mod_ref, bf16[1024,3072]{1,0:T(8,128)(2,1)} %v_ref.5, bf16[1024,3072]{1,0:T(8,128)(2,1)} %v_ref.5, bf16[1024,3072]{1,0:T(8,128)(2,1)} %v_ref.5), custom_call_target="tpu_custom_call" | custom-call | flops 603979776 | bytes 8388608 | tf_op jit(solution)/shard_map/project/pallas_call | solution.py:458
  17.9 7.4 %all-to-all-start = ((bf16[16,3,48,128]{3,2,1,0:T(8,128)(2,1)}), bf16[16,3,48,128]{3,2,1,0:T(8,128)(2,1)S(1)}, u32[]{:S(2)}, u32[]{:S(2)}) async-start(bf16[16,3,48,128]{3,2,1,0:T(8,128)(2,1)} %project.1), calls=%async_computation | async-start | bytes 1179648 | tf_op jit(solution)/shard_map/all_to_all | solution.py:1197
  25.8 1.5 collective-permute-start.25
  27.3 7.2 %fusion.26.dh_ref = f32[96,4096]{1,0:T(8,128)} fusion(bf16[96,1024]{1,0:T(8,128)(2,1)S(1)} %bitcast.168, bf16[4096,1024]{1,0:T(8,128)(2,1)} %param.37), kind=kOutput, calls=%fused_computation.82 | convolution fusion | flops 805306368 | bytes 10158080 | tf_op jit(solution)/shard_map/dot_general | solution.py:34
  34.5 6.9 %all-to-all-done.q_ref.k_ref.v_ref = bf16[16,3,48,128]{3,2,1,0:T(8,128)(2,1)S(1)} async-done(((bf16[16,3,48,128]{3,2,1,0:T(8,128)(2,1)}), bf16[16,3,48,128]{3,2,1,0:T(8,128)(2,1)S(1)}, u32[]{:S(2)}, u32[]{:S(2)}) %all-to-all-start) | async-done | bytes 589856 | tf_op jit(solution)/shard_map/all_to_all | solution.py:1197
  42.2 4.3 %self_forward.1 = (bf16[16,48,128]{2,1,0:T(8,128)(2,1)}, f32[2,768]{1,0:T(2,128)}) custom-call(s32[2]{0:T(128)} %count_ref.9, bf16[16,3,48,128]{3,2,1,0:T(8,128)(2,1)} %copy-done.15, bf16[16,3,48,128]{3,2,1,0:T(8,128)(2,1)} %copy-done.15, bf16[16,3,48,128]{3,2,1,0:T(8,128)(2,1)} %copy-done.15), custom_call_target="tpu_custom_call" | custom-call | flops 603979776 | bytes 1048576 | tf_op jit(solution)/shard_map/self_forward/pallas_call | solution.py:160
  46.5 6.1 %all-to-all-start.1 = ((bf16[16,48,128]{2,1,0:T(8,128)(2,1)}), bf16[16,48,128]{2,1,0:T(8,128)(2,1)S(1)}, u32[]{:S(2)}, u32[]{:S(2)}) async-start(bf16[16,48,128]{2,1,0:T(8,128)(2,1)} %get-tuple-element.65), calls=%async_computation.1 | async-start | bytes 393216 | tf_op jit(solution)/shard_map/all_to_all | solution.py:1197
  53.4 6.2 %convolution_convert_fusion = bf16[512,2048]{1,0:T(8,128)(2,1)} fusion(bf16[512,1024]{1,0:T(8,128)(2,1)} %bitcast.150, bf16[1024,2048]{1,0:T(8,128)(2,1)} %param.32), kind=kOutput, calls=%fused_computation.2 | convolution fusion | flops 2148532224 | bytes 7340032 | tf_op jit(solution)/shard_map/dot_general | solution.py:30
  59.6 2.0 all-to-all-done.1.got_ref
  62.3 4.5 %middle_part.1 = (bf16[96,1024]{1,0:T(8,128)(2,1)}, f32[96,1024]{1,0:T(8,128)}, bf16[96,1024]{1,0:T(8,128)(2,1)}, bf16[96,1024]{1,0:T(8,128)(2,1)}) custom-call(bf16[16,48,128]{2,1,0:T(8,128)(2,1)} %copy-done.11, bf16[96,1024]{1,0:T(8,128)(2,1)} %bitcast.149, f32[1,1024]{1,0:T(1,128)} %bitcast.181, f32[1,1024]{1,0:T(1,128)} %bitcast.183, ...), custom_call_target="tpu_custom_call" | custom-call | flops 402653184 | bytes 5242880 | tf_op jit(solution)/shard_map/middle_part/pallas_call | solution.py:519
  66.8 5.2 %cross_forward.1 = (bf16[2,48,1024]{2,1,0:T(8,128)(2,1)}, f32[2,4,256]{2,1,0:T(4,128)}, f32[96,1024]{1,0:T(8,128)}, bf16[96,1024]{1,0:T(8,128)(2,1)}) custom-call(s32[2]{0:T(128)} %count_ref.8, bf16[2,48,1024]{2,1,0:T(8,128)(2,1)} %bitcast.156, bf16[2,256,2048]{2,1,0:T(8,128)(2,1)} %bitcast.145, f32[96,1024]{1,0:T(8,128)} %get-tuple-element.69.mid_ref, ...), custom_call_target="tpu_custom_call" | custom-call | flops 402653184 | bytes 3145728 | tf_op jit(solution)/shard_map/cross_forward/pallas_call | solution.py:312
  72.0 10.7 %mlp.1 = (bf16[96,4096]{1,0:T(8,128)(2,1)}, bf16[96,4096]{1,0:T(8,128)(2,1)}, bf16[4,96,256]{2,1,0:T(8,128)(2,1)}, bf16[4,96,1024]{2,1,0:T(8,128)(2,1)}, f32[96,...) custom-call(bf16[96,1024]{1,0:T(8,128)(2,1)} %get-tuple-element.71.normed_ref, ...), custom_call_target="tpu_custom_call" | custom-call | flops 1610612736 | bytes 12582912 | tf_op jit(solution)/shard_map/mlp/pallas_call | solution.py:1028
  82.7 5.5 %cross_backward.1 = bf16[2,48,1024]{2,1,0:T(8,128)(2,1)} custom-call(s32[2]{0:T(128)} %count_ref.8, bf16[2,48,1024]{2,1,0:T(8,128)(2,1)} %bitcast.157, bf16[2,256,2048]{2,1,0:T(8,128)(2,1)} %bitcast.146, bf16[2,48,1024]{2,1,0:T(8,128)(2,1)} %bitcast.172, f32[2,4,256]{2,1,0:T(4,128)} %get-tuple-element.74.lse_ref), custom_call_target="tpu_custom_call" | custom-call | flops 1006632960 | bytes 6291456 | tf_op jit(solution)/shard_map/cross_backward/pallas_call | solution.py:344
  88.2 5.6 %middle_back.1 = (f32[96,1024]{1,0:T(8,128)}, bf16[96,1024]{1,0:T(8,128)(2,1)}, bf16[16,3,48,128]{3,2,1,0:T(8,128)(2,1)}, f32[2,1024]{1,0:T(2,128)}) custom-call(bf16[96,1024]{1,0:T(8,128)(2,1)} %bitcast.158, f32[96,1024]{1,0:T(8,128)} %get-tuple-element.69.mid_ref, f32[1,1024]{1,0:T(1,128)} %bitcast.182, f32[96,1024]{1,0:T(8,128)} %get-tuple-element.75.later_ref, ...), custom_call_target="tpu_custom_call" | custom-call | flops 402653184 | bytes 6291456 | tf_op jit(solution)/shard_map/middle_back/pallas_call | solution.py:585
  94.6 1.6 collective-permute-start.22
  96.5 1.1 pad_maximum_fusion.refs_4_
  97.6 1.7 collective-permute-start.7
  99.3 3.9 %all-to-all-start.2 = ((bf16[16,3,48,128]{3,2,1,0:T(8,128)(2,1)}), bf16[16,3,48,128]{3,2,1,0:T(8,128)(2,1)S(1)}, u32[]{:S(2)}, u32[]{:S(2)}) async-start(bf16[16,3,48,128]{3,2,1,0:T(8,128)(2,1)} %get-tuple-element.76), calls=%async_computation.2 | async-start | bytes 1179648 | tf_op jit(solution)/shard_map/all_to_all | solution.py:1197
  103.2 2.6 collective-permute-done.23
  105.8 3.8 %product.5 = (bf16[4,1,128,1024]{3,2,1,0:T(8,128)(2,1)}, bf16[4,1,128,1024]{3,2,1,0:T(8,128)(2,1)}) custom-call(s32[1]{0:T(128)} %bitcast.20.half_ref, bf16[1,96,1024]{2,1,0:T(8,128)(2,1)} %get-tuple-element.117.refs_0_, bf16[1,96,1024]{2,1,0:T(8,128)(2,1)} %bitcast.61.refs_1_, bf16[1,96,1024]{2,1,0:T(8,128)(2,1)} %bitcast.63.refs_2_, ...), custom_call_target="tpu_custom_call" | custom-call | flops 805306368 | bytes 8388608 | tf_op jit(solution)/shard_map/product/pallas_call | solution.py:1124
  109.6 1.7 collective-permute-start
  111.5 7.4 %collective-permute-done = s32[2,4]{1,0:T(2,128)S(1)} collective-permute-done((s32[2,4]{1,0:T(2,128)S(1)}, s32[2,4]{1,0:T(2,128)S(1)}, u32[]{:S(2)}, u32[]{:S(2)}) %collective-permute-start) | collective-permute-done | bytes 64 | tf_op jit(solution)/shard_map/ppermute | solution.py:1146
  119.1 2.5 pieces.1
  121.5 1.9 dynamic-slice_bitcast_fusion.4
  124.1 1.6 collective-permute-start.4
  126.0 4.3 %collective-permute-done.4.refs_2_ = bf16[3,96,256]{2,1,0:T(8,128)(2,1)S(1)} collective-permute-done((bf16[3,96,256]{2,1,0:T(8,128)(2,1)S(1)}, bf16[3,96,256]{2,1,0:T(8,128)(2,1)S(1)}, u32[]{:S(2)}, u32[]{:S(2)}) %collective-permute-start.4) | collective-permute-done | bytes 147488 | tf_op jit(solution)/shard_map/ppermute | solution.py:1146
  132.4 4.2 %memory_back.1.rest_0_ = bf16[16,2,16,128]{3,2,1,0:T(8,128)(2,1)} custom-call(s32[1]{0:T(128)} %bitcast.9.head_ref, s32[2]{0:T(128)} %count_ref.8, bf16[16,3,48,128]{3,2,1,0:T(8,128)(2,1)} %copy-done.2, bf16[16,3,48,128]{3,2,1,0:T(8,128)(2,1)} %copy-done.2, bf16[2,256,2048]{2,1,0:T(8,128)(2,1)} %bitcast.147, bf16[2,256,2048]{2,1,0:T(8,128)(2,1)} %bitcast.148), custom_call_target="tpu_custom_call" | custom-call | flops 402653184 | bytes 2097152 | tf_op jit(solution)/shard_map/memory_back/pallas_call | solution.py:394
  137.5 4.7 %product.3 = (bf16[4,3,32,1024]{3,2,1,0:T(8,128)(2,1)}, bf16[4,3,32,1024]{3,2,1,0:T(8,128)(2,1)}) custom-call(s32[1]{0:T(128)} %bitcast.20.half_ref, bf16[3,96,256]{2,1,0:T(8,128)(2,1)} %get-tuple-element.121.refs_0_, bf16[3,96,256]{2,1,0:T(8,128)(2,1)} %copy-done.20, bf16[3,96,256]{2,1,0:T(8,128)(2,1)} %copy-done.21, bf16[3,96,256]{2,1,0:T(8,128)(2,1)} %copy-done.22, ...), custom_call_target="tpu_custom_call" | custom-call | flops 603979776 | bytes 8388608 | tf_op jit(solution)/shard_map/product/pallas_call | solution.py:1124
  142.3 2.1 fusion.6
  144.4 1.2 collective-permute-start.28
  145.6 6.7 %self_backward.1.grads_ref = bf16[16,176,128]{2,1,0:T(8,128)(2,1)} custom-call(s32[2]{0:T(128)} %count_ref.9, bf16[16,3,48,128]{3,2,1,0:T(8,128)(2,1)} %copy-done.15, bf16[16,3,48,128]{3,2,1,0:T(8,128)(2,1)} %copy-done.15, bf16[16,3,48,128]{3,2,1,0:T(8,128)(2,1)} %copy-done.15, bf16[16,3,48,128]{3,2,1,0:T(8,128)(2,1)} %copy-done.2, ...), custom_call_target="tpu_custom_call" | custom-call | flops 1509949440 | bytes 2097152 | tf_op jit(solution)/shard_map/self_backward/pallas_call | solution.py:199
  152.3 3.9 %all-to-all-start.3 = ((bf16[16,176,128]{2,1,0:T(8,128)(2,1)}), bf16[16,176,128]{2,1,0:T(8,128)(2,1)S(1)}, u32[]{:S(2)}, u32[]{:S(2)}) async-start(bf16[16,176,128]{2,1,0:T(8,128)(2,1)} %self_backward.1.grads_ref), calls=%async_computation.3 | async-start | bytes 1441792 | tf_op jit(solution)/shard_map/all_to_all | solution.py:1197
  157.4 1.2 add_convert_fusion.1
  159.1 1.7 collective-permute-start.13
  161.8 15.6 %collective-permute-done.9 = bf16[4,3,32,1024]{3,2,1,0:T(8,128)(2,1)} collective-permute-done((bf16[4,3,32,1024]{3,2,1,0:T(8,128)(2,1)}, bf16[4,3,32,1024]{3,2,1,0:T(8,128)(2,1)}, u32[]{:S(2)}, u32[]{:S(2)}) %collective-permute-start.9) | collective-permute-done | bytes 786464 | tf_op jit(solution)/shard_map/ppermute | solution.py:1142
  177.5 1.7 add_convert_fusion.5
  179.2 2.3 collective-permute-start.29
  183.9 4.9 %product.4 = (bf16[4,1,32,4096]{3,2,1,0:T(8,128)(2,1)}, bf16[4,1,32,4096]{3,2,1,0:T(8,128)(2,1)}) custom-call(s32[1]{0:T(128)} %bitcast.41.half_ref, bf16[1,96,256]{2,1,0:T(8,128)(2,1)} %get-tuple-element.128.refs_0_, bf16[1,96,256]{2,1,0:T(8,128)(2,1)} %bitcast.176, bf16[1,96,256]{2,1,0:T(8,128)(2,1)} %bitcast.177, bf16[1,96,256]{2,1,0:T(8,128)(2,1)} %bitcast.178, ...), custom_call_target="tpu_custom_call" | custom-call | flops 805306368 | bytes 8388608 | tf_op jit(solution)/shard_map/product/pallas_call | solution.py:1124
  188.7 1.3 collective-permute-start.18
  190.0 4.3 %collective-permute-done.29 = bf16[1,1,128,1024]{3,2,1,0:T(8,128)(2,1)S(1)} collective-permute-done((bf16[1,1,128,1024]{3,2,1,0:T(8,128)(2,1)S(1)}, bf16[1,1,128,1024]{3,2,1,0:T(8,128)(2,1)S(1)}, u32[]{:S(2)}, u32[]{:S(2)}) %collective-permute-start.29) | collective-permute-done | bytes 262176 | tf_op jit(solution)/shard_map/ppermute | solution.py:1142
  194.4 1.9 add_bitcast_fusion
  196.2 1.1 collective-permute-done.10
  198.1 1.2 collective-permute-start.11
  199.9 4.2 %fusion = f32[2,16,1024]{2,1,0:T(8,128)} fusion(bf16[2,16,2048]{2,1,0:T(8,128)(2,1)S(1)} %dot_general.31, bf16[1024,2048]{1,0:T(8,128)(2,1)} %param.32), kind=kOutput, calls=%fused_computation | convolution fusion | flops 134217728 | bytes 4456448 | tf_op jit(solution)/shard_map/dot_general | solution.py:34
  204.1 6.6 %first_back.1 = f32[2,48,1024]{2,1,0:T(8,128)} custom-call(bf16[16,176,128]{2,1,0:T(8,128)(2,1)} %copy-done.3, bf16[1024,3072]{1,0:T(8,128)(2,1)} %v_ref.5, bf16[1024,3072]{1,0:T(8,128)(2,1)} %v_ref.5, bf16[1024,3072]{1,0:T(8,128)(2,1)} %v_ref.5, bf16[2,48,1024]{2,1,0:T(8,128)(2,1)} %tri_ref.3, f32[2,2048]{1,0:T(2,128)} %fusion.3.mod_ref, ...), custom_call_target="tpu_custom_call" | custom-call | flops 603979776 | bytes 8388608 | tf_op jit(solution)/shard_map/first_back/pallas_call | solution.py:660
  211.5 2.4 collective-permute-done.18
  214.0 2.0 fusion.5
  215.9 1.0 collective-permute-start.19
  217.0 1.2 add_convert_fusion.3
  218.2 6.9 %head_back.1 = (bf16[32,96,128]{2,1,0:T(8,128)(2,1)}, bf16[32,128]{1,0:T(8,128)(2,1)}) custom-call(s32[1]{0:T(128)} %bitcast.9.head_ref, bf16[16,176,128]{2,1,0:T(8,128)(2,1)} %self_backward.1.grads_ref, bf16[2,768,1024]{2,1,0:T(8,128)(2,1)} %all-gather.5.cloned.1.call-done.tri_ref, bf16[2,256,1024]{2,1,0:T(8,128)(2,1)} %all-gather.3.cloned.1.call-done.patch_ref, ...), custom_call_target="tpu_custom_call" | custom-call | flops 603979776 | bytes 5242880 | tf_op jit(solution)/shard_map/head_back/pallas_call | solution.py:789
  225.0 1.1 dynamic-slice_bitcast_fusion
  226.2 1.3 collective-permute-start.1
  227.4 1.5 collective-permute-done.19
  229.7 1.3 collective-permute-start.20
  231.0 4.9 %collective-permute-done.1 = bf16[16,96,128]{2,1,0:T(8,128)(2,1)S(1)} collective-permute-done((bf16[16,96,128]{2,1,0:T(8,128)(2,1)S(1)}, bf16[16,96,128]{2,1,0:T(8,128)(2,1)S(1)}, u32[]{:S(2)}, u32[]{:S(2)}) %collective-permute-start.1) | collective-permute-done | bytes 393248 | tf_op jit(solution)/shard_map/ppermute | solution.py:1146
  235.9 1.1 fusion.4
  238.6 3.7 %all-to-all-start.4 = ((bf16[16,128,128]{2,1,0:T(8,128)(2,1)}), bf16[16,128,128]{2,1,0:T(8,128)(2,1)S(1)}, u32[]{:S(2)}, u32[]{:S(2)}) async-start(bf16[16,128,128]{2,1,0:T(8,128)(2,1)} %pad_maximum_fusion.1), calls=%async_computation.4 | async-start | bytes 1048576 | tf_op jit(solution)/shard_map/all_to_all | solution.py:1197
  243.6 5.6 %convolution_add_fusion = f32[96,1024]{1,0:T(8,128)} fusion(f32[96,1024]{1,0:T(8,128)S(1)} %copy-done.7, bf16[96,4096]{1,0:T(8,128)(2,1)S(1)} %copy-done.4, bf16[4096,1024]{1,0:T(8,128)(2,1)} %param.37), kind=kOutput, calls=%fused_computation.3 | convolution fusion | flops 805404672 | bytes 9961472 | tf_op jit(solution)/shard_map/dot_general | solution.py:30
  249.2 7.6 %all-to-all-done.4.got_ref = bf16[16,128,128]{2,1,0:T(8,128)(2,1)S(1)} async-done(((bf16[16,128,128]{2,1,0:T(8,128)(2,1)}), bf16[16,128,128]{2,1,0:T(8,128)(2,1)S(1)}, u32[]{:S(2)}, u32[]{:S(2)}) %all-to-all-start.4) | async-done | bytes 524320 | tf_op jit(solution)/shard_map/all_to_all | solution.py:1197
  257.6 2.1 unpack.1
  259.7 1.2 collective-permute-start.2
  262.3 1.4 collective-permute-done.2
  264.5 3.4 %fusion.14 = f32[4,1024]{1,0:T(4,128)S(1)} fusion(bf16[1024,2048]{1,0:T(8,128)(2,1)} %param.26, f32[4,2048]{1,0:T(4,128)S(1)} %select_n.117), kind=kOutput, calls=%fused_computation.56 | convolution fusion | flops 16785408 | bytes 4243456 | tf_op jit(solution)/shard_map/dot_general | solution.py:34
  (137 shorter events, 24.8 us)
Async XLA Ops:
  7.2 1.5 copy-start
  7.2 46.2 %all-gather.3.cloned.1.call-start = ((), (), s32[]{:S(2)}) async-start(), calls=%async_computation.5 | async-start | bytes 1114112 | tf_op jit(solution)/shard_map/all_gather | solution.py:1268
  12.3 13.0 %copy-start.14 = (bf16[2,48,1024]{2,1,0:T(8,128)(2,1)S(1)}, bf16[2,48,1024]{2,1,0:T(8,128)(2,1)}, u32[]{:S(2)}) copy-start(bf16[2,48,1024]{2,1,0:T(8,128)(2,1)} %param.21) | copy-start | bytes 589828
  17.9 23.5 %all-to-all-start = ((bf16[16,3,48,128]{3,2,1,0:T(8,128)(2,1)}), bf16[16,3,48,128]{3,2,1,0:T(8,128)(2,1)S(1)}, u32[]{:S(2)}, u32[]{:S(2)}) async-start(bf16[16,3,48,128]{3,2,1,0:T(8,128)(2,1)} %project.1), calls=%async_computation | async-start | bytes 1179648 | tf_op jit(solution)/shard_map/all_to_all | solution.py:1197
  25.3 72.3 %collective-permute-start.24 = (bf16[96,1024]{1,0:T(8,128)(2,1)S(1)}, bf16[96,1024]{1,0:T(8,128)(2,1)}, u32[]{:S(2)}, u32[]{:S(2)}) collective-permute-start(bf16[96,1024]{1,0:T(8,128)(2,1)S(1)} %bitcast.166), channel_id=1, source_target_pairs={{0,1},{1,0},{2,3},{3,2},{4,5},{5,4},{6,7},{7,6},{8,9},{9,8},{10,11... | collective-permute-start | bytes 589832 | tf_op jit(solution)/shard_map/ppermute | solution.py:1142
  25.8 8.7 %collective-permute-start.25 = (bf16[96,1024]{1,0:T(8,128)(2,1)S(1)}, bf16[96,1024]{1,0:T(8,128)(2,1)}, u32[]{:S(2)}, u32[]{:S(2)}) collective-permute-start(bf16[96,1024]{1,0:T(8,128)(2,1)S(1)} %bitcast.167), channel_id=1, source_target_pairs={{0,16},{16,0},{1,17},{17,1},{2,18},{18,2},{3,19},{19,3},{4,20},{20... | collective-permute-start | bytes 589832 | tf_op jit(solution)/shard_map/ppermute | solution.py:1146
  34.5 68.7 %collective-permute-start.26 = (bf16[96,1024]{1,0:T(8,128)(2,1)}, bf16[96,1024]{1,0:T(8,128)(2,1)}, u32[]{:S(2)}, u32[]{:S(2)}) collective-permute-start(bf16[96,1024]{1,0:T(8,128)(2,1)} %collective-permute-done.25), channel_id=1, source_target_pairs={{0,1},{1,0},{2,3},{3,2},{4,5},{5,4},{6,7},{7,6},{8,9},{9,8},{10,11... | collective-permute-start | bytes 589832 | tf_op jit(solution)/shard_map/ppermute | solution.py:1142
  41.4 0.8 copy-start.15
  46.5 15.1 %all-to-all-start.1 = ((bf16[16,48,128]{2,1,0:T(8,128)(2,1)}), bf16[16,48,128]{2,1,0:T(8,128)(2,1)S(1)}, u32[]{:S(2)}, u32[]{:S(2)}) async-start(bf16[16,48,128]{2,1,0:T(8,128)(2,1)} %get-tuple-element.65), calls=%async_computation.1 | async-start | bytes 393216 | tf_op jit(solution)/shard_map/all_to_all | solution.py:1197
  52.6 165.6 %all-gather.5.cloned.1.call-start = ((), (), s32[]{:S(2)}) async-start(), calls=%async_computation.6 | async-start | bytes 3342336 | tf_op jit(solution)/shard_map/all_gather | solution.py:1289
  82.7 11.1 %copy-start.12 = (bf16[4,96,1024]{2,1,0:T(8,128)(2,1)S(1)}, bf16[4,96,1024]{2,1,0:T(8,128)(2,1)}, u32[]{:S(2)}) copy-start(bf16[4,96,1024]{2,1,0:T(8,128)(2,1)} %get-tuple-element.108) | copy-start | bytes 2359300
  88.2 8.2 %copy-start.10 = (bf16[2,48,1024]{2,1,0:T(8,128)(2,1)S(1)}, bf16[2,48,1024]{2,1,0:T(8,128)(2,1)}, u32[]{:S(2)}) copy-start(bf16[2,48,1024]{2,1,0:T(8,128)(2,1)} %cross_backward.1) | copy-start | bytes 589828
  88.2 8.2 %copy-start.18 = (bf16[96,1024]{1,0:T(8,128)(2,1)S(1)}, bf16[96,1024]{1,0:T(8,128)(2,1)}, u32[]{:S(2)}) copy-start(bf16[96,1024]{1,0:T(8,128)(2,1)} %get-tuple-element.97) | copy-start | bytes 589828
  93.8 15.8 %copy-start.28 = (s32[2,4]{1,0:T(2,128)S(1)}, s32[2,4]{1,0:T(2,128)}, u32[]{:S(2)}) copy-start(s32[2,4]{1,0:T(2,128)} %param.22) | copy-start | bytes 100
  94.6 8.6 %collective-permute-start.21 = (bf16[96,1024]{1,0:T(8,128)(2,1)S(1)}, bf16[96,1024]{1,0:T(8,128)(2,1)}, u32[]{:S(2)}, u32[]{:S(2)}) collective-permute-start(bf16[96,1024]{1,0:T(8,128)(2,1)S(1)} %get-tuple-element.116), channel_id=1, source_target_pairs={{0,1},{1,0},{2,3},{3,2},{4,5},{5,4},{6,7},{7,6},{8,9},{9,8},{10,11... | collective-permute-start | bytes 589832 | tf_op jit(solution)/shard_map/ppermute | solution.py:1142
  94.6 8.5 %collective-permute-start.22 = (bf16[96,1024]{1,0:T(8,128)(2,1)S(1)}, bf16[96,1024]{1,0:T(8,128)(2,1)}, u32[]{:S(2)}, u32[]{:S(2)}) collective-permute-start(bf16[96,1024]{1,0:T(8,128)(2,1)S(1)} %get-tuple-element.115), channel_id=1, source_target_pairs={{0,16},{16,0},{1,17},{17,1},{2,18},{18,2},{3,19},{19,3},{4,20},{20... | collective-permute-start | bytes 589832 | tf_op jit(solution)/shard_map/ppermute | solution.py:1146
  96.2 9.6 %collective-permute-start.23 = (bf16[96,1024]{1,0:T(8,128)(2,1)S(1)}, bf16[96,1024]{1,0:T(8,128)(2,1)}, u32[]{:S(2)}, u32[]{:S(2)}) collective-permute-start(bf16[96,1024]{1,0:T(8,128)(2,1)S(1)} %get-tuple-element.114), channel_id=1, source_target_pairs={{0,17},{1,16},{2,19},{3,18},{4,21},{5,20},{6,23},{7,22},{8,25},{9,... | collective-permute-start | bytes 589832 | tf_op jit(solution)/shard_map/ppermute | solution.py:1200
  96.5 29.3 %copy-start.13 = (bf16[96,4096]{1,0:T(8,128)(2,1)S(1)}, bf16[96,4096]{1,0:T(8,128)(2,1)}, u32[]{:S(2)}) copy-start(bf16[96,4096]{1,0:T(8,128)(2,1)} %get-tuple-element.105) | copy-start | bytes 2359300
  96.5 34.9 %copy-start.26 = (f32[2,1024]{1,0:T(2,128)S(1)}, f32[2,1024]{1,0:T(2,128)}, u32[]{:S(2)}) copy-start(f32[2,1024]{1,0:T(2,128)} %get-tuple-element.80) | copy-start | bytes 24580
  96.5 34.9 %copy-start.27 = (f32[2,1024]{1,0:T(2,128)S(1)}, f32[2,1024]{1,0:T(2,128)}, u32[]{:S(2)}) copy-start(f32[2,1024]{1,0:T(2,128)} %get-tuple-element.79) | copy-start | bytes 24580
  97.5 39.1 %copy-start.5 = (bf16[3,96,1024]{2,1,0:T(8,128)(2,1)}, bf16[3,96,1024]{2,1,0:T(8,128)(2,1)S(1)}, u32[]{:S(2)}) copy-start(bf16[3,96,1024]{2,1,0:T(8,128)(2,1)S(1)} %pad_maximum_fusion.refs_4_) | copy-start | bytes 1769476
  97.6 26.3 %collective-permute-start.7 = (bf16[3,96,1024]{2,1,0:T(8,128)(2,1)S(1)}, bf16[3,96,1024]{2,1,0:T(8,128)(2,1)}, u32[]{:S(2)}, u32[]{:S(2)}) collective-permute-start(bf16[3,96,1024]{2,1,0:T(8,128)(2,1)S(1)} %pad_maximum_fusion.refs_4_), channel_id=1, source_target_pairs={{0,16},{16,0},{1,17},{17,1},{2,18},{18,2},{3,19},{19,3},{4,20},{20... | collective-permute-start | bytes 1769480 | tf_op jit(solution)/shard_map/ppermute | solution.py:1146
  99.3 32.3 %all-to-all-start.2 = ((bf16[16,3,48,128]{3,2,1,0:T(8,128)(2,1)}), bf16[16,3,48,128]{3,2,1,0:T(8,128)(2,1)S(1)}, u32[]{:S(2)}, u32[]{:S(2)}) async-start(bf16[16,3,48,128]{3,2,1,0:T(8,128)(2,1)} %get-tuple-element.76), calls=%async_computation.2 | async-start | bytes 1179648 | tf_op jit(solution)/shard_map/all_to_all | solution.py:1197
  109.6 32.7 %collective-permute-start.27 = (bf16[4,1,128,1024]{3,2,1,0:T(8,128)(2,1)}, bf16[4,1,128,1024]{3,2,1,0:T(8,128)(2,1)}, u32[]{:S(2)}, u32[]{:S(2)}) collective-permute-start(bf16[4,1,128,1024]{3,2,1,0:T(8,128)(2,1)} %get-tuple-element.111), channel_id=1, source_target_pairs={{0,2},{1,3},{2,0},{3,1},{4,6},{5,7},{6,4},{7,5},{8,10},{9,11},{10,... | collective-permute-start | bytes 3145736 | tf_op jit(solution)/shard_map/ppermute | solution.py:1142
  109.6 9.2 %collective-permute-start = (s32[2,4]{1,0:T(2,128)S(1)}, s32[2,4]{1,0:T(2,128)S(1)}, u32[]{:S(2)}, u32[]{:S(2)}) collective-permute-start(s32[2,4]{1,0:T(2,128)S(1)} %copy-done.28), channel_id=1, source_target_pairs={{0,16},{16,0},{1,17},{17,1},{2,18},{18,2},{3,19},{19,3},{4,20},{20... | collective-permute-start | bytes 104 | tf_op jit(solution)/shard_map/ppermute | solution.py:1146
  119.0 18.5 %collective-permute-start.6 = (bf16[3,96,1024]{2,1,0:T(8,128)(2,1)S(1)}, bf16[3,96,1024]{2,1,0:T(8,128)(2,1)}, u32[]{:S(2)}, u32[]{:S(2)}) collective-permute-start(bf16[3,96,1024]{2,1,0:T(8,128)(2,1)S(1)} %pad_maximum_fusion.refs_4_), channel_id=1, source_target_pairs={{0,1},{1,0},{2,3},{3,2},{4,5},{5,4},{6,7},{7,6},{8,9},{9,8},{10,11... | collective-permute-start | bytes 1769480 | tf_op jit(solution)/shard_map/ppermute | solution.py:1142
  123.4 2.4 collective-permute-start.3
  123.9 13.6 %collective-permute-start.8 = (bf16[3,96,1024]{2,1,0:T(8,128)(2,1)}, bf16[3,96,1024]{2,1,0:T(8,128)(2,1)}, u32[]{:S(2)}, u32[]{:S(2)}) collective-permute-start(bf16[3,96,1024]{2,1,0:T(8,128)(2,1)} %collective-permute-done.7.refs_6_), channel_id=1, source_target_pairs={{0,1},{1,0},{2,3},{3,2},{4,5},{5,4},{6,7},{7,6},{8,9},{9,8},{10,11... | collective-permute-start | bytes 1769480 | tf_op jit(solution)/shard_map/ppermute | solution.py:1142
  124.1 6.2 %collective-permute-start.4 = (bf16[3,96,256]{2,1,0:T(8,128)(2,1)S(1)}, bf16[3,96,256]{2,1,0:T(8,128)(2,1)S(1)}, u32[]{:S(2)}, u32[]{:S(2)}) collective-permute-start(bf16[3,96,256]{2,1,0:T(8,128)(2,1)S(1)} %get-tuple-element.119), channel_id=1, source_target_pairs={{0,16},{16,0},{1,17},{17,1},{2,18},{18,2},{3,19},{19,3},{4,20},{20... | collective-permute-start | bytes 442376 | tf_op jit(solution)/shard_map/ppermute | solution.py:1146
  125.8 5.8 %copy-start.20 = (bf16[3,96,256]{2,1,0:T(8,128)(2,1)}, bf16[3,96,256]{2,1,0:T(8,128)(2,1)S(1)}, u32[]{:S(2)}) copy-start(bf16[3,96,256]{2,1,0:T(8,128)(2,1)S(1)} %collective-permute-done.3.refs_1_) | copy-start | bytes 442372
  125.8 31.3 %collective-permute-start.16 = (bf16[96,4096]{1,0:T(8,128)(2,1)S(1)}, bf16[96,4096]{1,0:T(8,128)(2,1)}, u32[]{:S(2)}, u32[]{:S(2)}) collective-permute-start(bf16[96,4096]{1,0:T(8,128)(2,1)S(1)} %copy-done.13), channel_id=1, source_target_pairs={{0,2},{1,3},{2,0},{3,1},{4,6},{5,7},{6,4},{7,5},{8,10},{9,11},{10,... | collective-permute-start | bytes 2359304 | tf_op jit(solution)/shard_map/ppermute | solution.py:1142
  130.3 7.2 %copy-start.21 = (bf16[3,96,256]{2,1,0:T(8,128)(2,1)}, bf16[3,96,256]{2,1,0:T(8,128)(2,1)S(1)}, u32[]{:S(2)}) copy-start(bf16[3,96,256]{2,1,0:T(8,128)(2,1)S(1)} %collective-permute-done.4.refs_2_) | copy-start | bytes 442372
  130.3 6.3 %collective-permute-start.5 = (bf16[3,96,256]{2,1,0:T(8,128)(2,1)}, bf16[3,96,256]{2,1,0:T(8,128)(2,1)S(1)}, u32[]{:S(2)}, u32[]{:S(2)}) collective-permute-start(bf16[3,96,256]{2,1,0:T(8,128)(2,1)} %get-tuple-element.118), channel_id=1, source_target_pairs={{0,17},{1,16},{2,19},{3,18},{4,21},{5,20},{6,23},{7,22},{8,25},{9,... | collective-permute-start | bytes 442376 | tf_op jit(solution)/shard_map/ppermute | solution.py:1200
  131.6 0.8 copy-start.2
  132.4 9.9 %copy-start.8 = (bf16[4,1,128,1024]{3,2,1,0:T(8,128)(2,1)S(1)}, bf16[4,1,128,1024]{3,2,1,0:T(8,128)(2,1)}, u32[]{:S(2)}) copy-start(bf16[4,1,128,1024]{3,2,1,0:T(8,128)(2,1)} %get-tuple-element.110) | copy-start | bytes 3145732
  136.7 0.8 copy-start.22
  136.7 46.6 %collective-permute-start.15 = (bf16[96,4096]{1,0:T(8,128)(2,1)S(1)}, bf16[96,4096]{1,0:T(8,128)(2,1)}, u32[]{:S(2)}, u32[]{:S(2)}) collective-permute-start(bf16[96,4096]{1,0:T(8,128)(2,1)S(1)} %copy-done.13), channel_id=1, source_target_pairs={{0,1},{1,0},{2,3},{3,2},{4,5},{5,4},{6,7},{7,6},{8,9},{9,8},{10,11... | collective-permute-start | bytes 2359304 | tf_op jit(solution)/shard_map/ppermute | solution.py:1142
  142.2 35.2 %collective-permute-start.9 = (bf16[4,3,32,1024]{3,2,1,0:T(8,128)(2,1)}, bf16[4,3,32,1024]{3,2,1,0:T(8,128)(2,1)}, u32[]{:S(2)}, u32[]{:S(2)}) collective-permute-start(bf16[4,3,32,1024]{3,2,1,0:T(8,128)(2,1)} %get-tuple-element.101), channel_id=1, source_target_pairs={{0,2},{1,3},{2,0},{3,1},{4,6},{5,7},{6,4},{7,5},{8,10},{9,11},{10,... | collective-permute-start | bytes 2359304 | tf_op jit(solution)/shard_map/ppermute | solution.py:1142
  142.3 13.9 %copy-start.19 = (bf16[4,96,256]{2,1,0:T(8,128)(2,1)S(1)}, bf16[4,96,256]{2,1,0:T(8,128)(2,1)}, u32[]{:S(2)}) copy-start(bf16[4,96,256]{2,1,0:T(8,128)(2,1)} %get-tuple-element.104) | copy-start | bytes 589828
  144.4 14.7 %collective-permute-start.28 = (bf16[2,1,128,1024]{3,2,1,0:T(8,128)(2,1)}, bf16[2,1,128,1024]{3,2,1,0:T(8,128)(2,1)}, u32[]{:S(2)}, u32[]{:S(2)}) collective-permute-start(bf16[2,1,128,1024]{3,2,1,0:T(8,128)(2,1)} %fusion.6), channel_id=1, source_target_pairs={{0,4},{1,5},{2,6},{3,7},{4,0},{5,1},{6,2},{7,3},{8,12},{9,13},{10,... | collective-permute-start | bytes 1572872 | tf_op jit(solution)/shard_map/ppermute | solution.py:1142
  152.3 47.0 %all-to-all-start.3 = ((bf16[16,176,128]{2,1,0:T(8,128)(2,1)}), bf16[16,176,128]{2,1,0:T(8,128)(2,1)S(1)}, u32[]{:S(2)}, u32[]{:S(2)}) async-start(bf16[16,176,128]{2,1,0:T(8,128)(2,1)} %self_backward.1.grads_ref), calls=%async_computation.3 | async-start | bytes 1441792 | tf_op jit(solution)/shard_map/all_to_all | solution.py:1197
  156.9 22.3 %collective-permute-start.12 = (bf16[96,256]{1,0:T(8,128)(2,1)S(1)}, bf16[96,256]{1,0:T(8,128)(2,1)S(1)}, u32[]{:S(2)}, u32[]{:S(2)}) collective-permute-start(bf16[96,256]{1,0:T(8,128)(2,1)S(1)} %get-tuple-element.127), channel_id=1, source_target_pairs={{0,1},{1,0},{2,3},{3,2},{4,5},{5,4},{6,7},{7,6},{8,9},{9,8},{10,11... | collective-permute-start | bytes 147464 | tf_op jit(solution)/shard_map/ppermute | solution.py:1142
  157.1 26.2 %collective-permute-start.17 = (bf16[96,4096]{1,0:T(8,128)(2,1)}, bf16[96,4096]{1,0:T(8,128)(2,1)}, u32[]{:S(2)}, u32[]{:S(2)}) collective-permute-start(bf16[96,4096]{1,0:T(8,128)(2,1)} %collective-permute-done.16), channel_id=1, source_target_pairs={{0,1},{1,0},{2,3},{3,2},{4,5},{5,4},{6,7},{7,6},{8,9},{9,8},{10,11... | collective-permute-start | bytes 2359304 | tf_op jit(solution)/shard_map/ppermute | solution.py:1142
  159.1 22.4 %collective-permute-start.13 = (bf16[96,256]{1,0:T(8,128)(2,1)S(1)}, bf16[96,256]{1,0:T(8,128)(2,1)S(1)}, u32[]{:S(2)}, u32[]{:S(2)}) collective-permute-start(bf16[96,256]{1,0:T(8,128)(2,1)S(1)} %get-tuple-element.126), channel_id=1, source_target_pairs={{0,2},{1,3},{2,0},{3,1},{4,6},{5,7},{6,4},{7,5},{8,10},{9,11},{10,... | collective-permute-start | bytes 147464 | tf_op jit(solution)/shard_map/ppermute | solution.py:1142
  177.5 5.8 %collective-permute-start.14 = (bf16[96,256]{1,0:T(8,128)(2,1)S(1)}, bf16[96,256]{1,0:T(8,128)(2,1)S(1)}, u32[]{:S(2)}, u32[]{:S(2)}) collective-permute-start(bf16[96,256]{1,0:T(8,128)(2,1)S(1)} %get-tuple-element.125), channel_id=1, source_target_pairs={{0,3},{1,2},{2,1},{3,0},{4,7},{5,6},{6,5},{7,4},{8,11},{9,10},{10,... | collective-permute-start | bytes 147464 | tf_op jit(solution)/shard_map/ppermute | solution.py:1142
  179.1 4.1 %copy-start.23 = (bf16[96,256]{1,0:T(8,128)(2,1)}, bf16[96,256]{1,0:T(8,128)(2,1)S(1)}, u32[]{:S(2)}) copy-start(bf16[96,256]{1,0:T(8,128)(2,1)S(1)} %collective-permute-done.12) | copy-start | bytes 147460
  179.2 15.2 %collective-permute-start.29 = (bf16[1,1,128,1024]{3,2,1,0:T(8,128)(2,1)S(1)}, bf16[1,1,128,1024]{3,2,1,0:T(8,128)(2,1)S(1)}, u32[]{:S(2)}, u32[]{:S(2)}) collective-permute-start(bf16[1,1,128,1024]{3,2,1,0:T(8,128)(2,1)S(1)} %fusion.7), channel_id=1, source_target_pairs={{0,8},{1,9},{2,10},{3,11},{4,12},{5,13},{6,14},{7,15},{8,0},{9,1},... | collective-permute-start | bytes 786440 | tf_op jit(solution)/shard_map/ppermute | solution.py:1142
  181.5 1.8 copy-start.24
  181.5 15.8 %collective-permute-start.10 = (bf16[2,3,32,1024]{3,2,1,0:T(8,128)(2,1)S(1)}, bf16[2,3,32,1024]{3,2,1,0:T(8,128)(2,1)S(1)}, u32[]{:S(2)}, u32[]{:S(2)}) collective-permute-start(bf16[2,3,32,1024]{3,2,1,0:T(8,128)(2,1)S(1)} %get-tuple-element.113), channel_id=1, source_target_pairs={{0,4},{1,5},{2,6},{3,7},{4,0},{5,1},{6,2},{7,3},{8,12},{9,13},{10,... | collective-permute-start | bytes 1179656 | tf_op jit(solution)/shard_map/ppermute | solution.py:1142
  188.7 25.2 %collective-permute-start.18 = (bf16[4,1,32,4096]{3,2,1,0:T(8,128)(2,1)}, bf16[4,1,32,4096]{3,2,1,0:T(8,128)(2,1)}, u32[]{:S(2)}, u32[]{:S(2)}) collective-permute-start(bf16[4,1,32,4096]{3,2,1,0:T(8,128)(2,1)} %get-tuple-element.107), channel_id=1, source_target_pairs={{0,16},{16,0},{1,17},{17,1},{2,18},{18,2},{3,19},{19,3},{4,20},{20... | collective-permute-start | bytes 3145736 | tf_op jit(solution)/shard_map/ppermute | solution.py:1146
  197.3 0.7 copy-start.16
  198.1 12.6 %collective-permute-start.11 = (bf16[1,3,32,1024]{3,2,1,0:T(8,128)(2,1)S(1)}, bf16[1,3,32,1024]{3,2,1,0:T(8,128)(2,1)S(1)}, u32[]{:S(2)}, u32[]{:S(2)}) collective-permute-start(bf16[1,3,32,1024]{3,2,1,0:T(8,128)(2,1)S(1)} %fusion.12), channel_id=1, source_target_pairs={{0,8},{1,9},{2,10},{3,11},{4,12},{5,13},{6,14},{7,15},{8,0},{9,1},... | collective-permute-start | bytes 589832 | tf_op jit(solution)/shard_map/ppermute | solution.py:1142
  199.3 4.8 %copy-start.3 = (bf16[16,176,128]{2,1,0:T(8,128)(2,1)}, bf16[16,176,128]{2,1,0:T(8,128)(2,1)S(1)}, u32[]{:S(2)}) copy-start(bf16[16,176,128]{2,1,0:T(8,128)(2,1)S(1)} %all-to-all-done.3.got_ref) | copy-start | bytes 2162692
  204.1 6.6 %copy-start.17 = (bf16[2,3,32,1024]{3,2,1,0:T(8,128)(2,1)S(1)}, bf16[2,3,32,1024]{3,2,1,0:T(8,128)(2,1)}, u32[]{:S(2)}) copy-start(bf16[2,3,32,1024]{3,2,1,0:T(8,128)(2,1)} %copy-done.16) | copy-start | bytes 1179652
  204.1 9.9 %copy-start.9 = (bf16[4,1,32,4096]{3,2,1,0:T(8,128)(2,1)S(1)}, bf16[4,1,32,4096]{3,2,1,0:T(8,128)(2,1)}, u32[]{:S(2)}) copy-start(bf16[4,1,32,4096]{3,2,1,0:T(8,128)(2,1)} %get-tuple-element.106) | copy-start | bytes 3145732
  215.9 13.0 %collective-permute-start.19 = (bf16[2,1,32,4096]{3,2,1,0:T(8,128)(2,1)}, bf16[2,1,32,4096]{3,2,1,0:T(8,128)(2,1)S(1)}, u32[]{:S(2)}, u32[]{:S(2)}) collective-permute-start(bf16[2,1,32,4096]{3,2,1,0:T(8,128)(2,1)} %fusion.5), channel_id=1, source_target_pairs={{0,4},{1,5},{2,6},{3,7},{4,0},{5,1},{6,2},{7,3},{8,12},{9,13},{10,... | collective-permute-start | bytes 1572872 | tf_op jit(solution)/shard_map/ppermute | solution.py:1142
  225.0 18.5 %copy-start.4 = (bf16[96,4096]{1,0:T(8,128)(2,1)S(1)}, bf16[96,4096]{1,0:T(8,128)(2,1)}, u32[]{:S(2)}) copy-start(bf16[96,4096]{1,0:T(8,128)(2,1)} %get-tuple-element.84) | copy-start | bytes 2359300
  225.0 18.6 %copy-start.7 = (f32[96,1024]{1,0:T(8,128)S(1)}, f32[96,1024]{1,0:T(8,128)}, u32[]{:S(2)}) copy-start(f32[96,1024]{1,0:T(8,128)} %get-tuple-element.83.later_ref) | copy-start | bytes 1179652
  226.2 9.8 %collective-permute-start.1 = (bf16[16,96,128]{2,1,0:T(8,128)(2,1)S(1)}, bf16[16,96,128]{2,1,0:T(8,128)(2,1)S(1)}, u32[]{:S(2)}, u32[]{:S(2)}) collective-permute-start(bf16[16,96,128]{2,1,0:T(8,128)(2,1)S(1)} %dynamic-slice_bitcast_fusion), channel_id=1, source_target_pairs={{0,16},{16,0},{1,17},{17,1},{2,18},{18,2},{3,19},{19,3},{4,20},{20... | collective-permute-start | bytes 1179656 | tf_op jit(solution)/shard_map/ppermute | solution.py:1146
  229.7 13.0 %collective-permute-start.20 = (bf16[1,1,32,4096]{3,2,1,0:T(8,128)(2,1)}, bf16[1,1,32,4096]{3,2,1,0:T(8,128)(2,1)S(1)}, u32[]{:S(2)}, u32[]{:S(2)}) collective-permute-start(bf16[1,1,32,4096]{3,2,1,0:T(8,128)(2,1)} %fusion.9), channel_id=1, source_target_pairs={{0,8},{1,9},{2,10},{3,11},{4,12},{5,13},{6,14},{7,15},{8,0},{9,1},... | collective-permute-start | bytes 786440 | tf_op jit(solution)/shard_map/ppermute | solution.py:1142
  238.6 18.2 %all-to-all-start.4 = ((bf16[16,128,128]{2,1,0:T(8,128)(2,1)}), bf16[16,128,128]{2,1,0:T(8,128)(2,1)S(1)}, u32[]{:S(2)}, u32[]{:S(2)}) async-start(bf16[16,128,128]{2,1,0:T(8,128)(2,1)} %pad_maximum_fusion.1), calls=%async_computation.4 | async-start | bytes 1048576 | tf_op jit(solution)/shard_map/all_to_all | solution.py:1197
  243.6 25.8 %copy-start.1 = (bf16[256,1024]{1,0:T(8,128)(2,1)S(1)}, bf16[256,1024]{1,0:T(8,128)(2,1)}, u32[]{:S(2)}) copy-start(bf16[256,1024]{1,0:T(8,128)(2,1)} %param.25) | copy-start | bytes 1572868
  256.8 0.8 copy-start.6
  259.7 4.0 %collective-permute-start.2 = (f32[32,128]{1,0:T(8,128)}, f32[32,128]{1,0:T(8,128)S(1)}, u32[]{:S(2)}, u32[]{:S(2)}) collective-permute-start(f32[32,128]{1,0:T(8,128)} %get-tuple-element.87), channel_id=1, source_target_pairs={{0,16},{16,0},{1,17},{17,1},{2,18},{18,2},{3,19},{19,3},{4,20},{20... | collective-permute-start | bytes 49160 | tf_op jit(solution)/shard_map/ppermute | solution.py:1146
  (2 other events, 1.3 us)
Sparse Core Ops, SparseCore 0:
  10.2 42.9 all-gather.2
  55.7 46.5 all-gather.4
